TPU v7x, 256 devices: a whole 4x4x8 slice. The times are simulated.
256 devices in a mesh: batch: 16 (over x, z_lo, core), row: 4 (over z_hi), col: 4 (over y).
Axes of the slice: x: 4, y: 4, z: 8 (z_hi: 4, z_lo: 2; z = z_hi * 2 + z_lo), core: 2. Of those that a mesh axis runs over, the one named last changes fastest.
Arguments:
- view_one: bfloat16 [2048, 8192], P('batch', ('row', 'col')), may hold values from -20 to 20, as said below
- view_two: bfloat16 [2048, 8192], P('batch', ('row', 'col')), may hold values from -20 to 20, as said below
Outputs:
- grad_one: bfloat16 [2048, 8192], P('batch', ('row', 'col'))
- grad_two: bfloat16 [2048, 8192], P('batch', ('row', 'col'))
Inputs may be any that keep to these rules, and one draw needn't show every extreme that they name: `view_one`: projector outputs; features differ in scale. `view_two`: projector outputs; features differ in scale.
All inputs are finite; a program needn't handle non-finite values.
Results may differ from a plain program's by a relative error of at most 0.0051.
Values may be sent and summed in bfloat16 or wider, within the bound.
No kernel may reach another device: no remote copies, remote signals or barrier semaphores. Data moves between devices by JAX's collectives and lax.ppermute only.
A program may use at most 128 MiB of HBM per device.

v0:
```python
import jax
import jax.numpy as jnp
from jax import lax
from jax.sharding import PartitionSpec as P


def hinge_of(variance):
    std_val = jnp.sqrt(variance + 0.0001)
    return jnp.where(std_val < 1.0, 1.0 / std_val, jnp.zeros_like(std_val))


def on_device(view_one, view_two):
    local_rows, shard_width = view_one.shape
    groups = lax.axis_size("batch")
    col_count = lax.axis_size("col")
    sample_count = local_rows * groups
    first_view = view_one.astype(jnp.float32)
    second_view = view_two.astype(jnp.float32)
    totals = lax.psum((jnp.sum(first_view, axis=0), jnp.sum(second_view, axis=0)), "batch")
    cent_one = first_view - totals[0] / sample_count
    cent_two = second_view - totals[1] / sample_count
    squares = lax.psum(
        (jnp.sum(cent_one * cent_one, axis=0), jnp.sum(cent_two * cent_two, axis=0)), "batch"
    )
    var_one = squares[0] / (sample_count - 1)
    var_two = squares[1] / (sample_count - 1)
    hinge_one = hinge_of(var_one)
    hinge_two = hinge_of(var_two)
    stacked = jnp.stack([cent_one, cent_two]).astype(jnp.bfloat16)
    row_block = lax.all_gather(stacked, "col", axis=2, tiled=True)
    row_slice = lax.all_to_all(row_block, "batch", split_axis=2, concat_axis=1, tiled=True)
    col_set = lax.all_gather(stacked, "row", axis=2, tiled=True)
    col_all = lax.all_gather(col_set, "batch", axis=1, tiled=True)
    cov_tile = jnp.einsum(
        "vnk,vnp->vkp", row_slice, col_all, preferred_element_type=jnp.float32
    ) / (sample_count - 1)
    slice_rows = row_slice.shape[2]
    block_width = row_block.shape[2]
    set_width = col_set.shape[2]
    global_rows = (
        lax.axis_index("row") * block_width
        + lax.axis_index("batch") * slice_rows
        + jnp.arange(slice_rows, dtype=jnp.int32)
    )
    positions = jnp.arange(set_width, dtype=jnp.int32)
    global_cols = (
        positions // shard_width * col_count + lax.axis_index("col")
    ) * shard_width + positions % shard_width
    off_diag = global_rows[:, None] != global_cols[None, :]
    cov_off = jnp.where(off_diag[None], cov_tile, jnp.zeros_like(cov_tile)).astype(jnp.bfloat16)
    partial_value = jnp.einsum(
        "vnk,vkp->vnp", row_slice, cov_off, preferred_element_type=jnp.float32
    )
    own_samples = lax.psum_scatter(partial_value, "batch", scatter_dimension=1, tiled=True)
    product = lax.psum_scatter(own_samples, "row", scatter_dimension=2, tiled=True)
    coef_var = sample_count / (2.0 * (sample_count - 1))
    coef_cov = 2.0 * sample_count / (25.0 * (sample_count - 1))
    grad_one = first_view - second_view - coef_var * hinge_one * cent_one + coef_cov * product[0]
    grad_two = second_view - first_view - coef_var * hinge_two * cent_two + coef_cov * product[1]
    return (grad_one.astype(jnp.bfloat16), grad_two.astype(jnp.bfloat16))


def solution(mesh):
    in_specs = (P("batch", ("row", "col")), P("batch", ("row", "col")))
    out_specs = (P("batch", ("row", "col")), P("batch", ("row", "col")))
    return jax.shard_map(
        on_device, mesh=mesh, in_specs=in_specs, out_specs=out_specs, check_vma=False
    )
```

profile of v0, /device:TPU:38, one launch (start us, length us, event | category | flops | bytes accessed | tf_op | source)
XLA Modules:
  0.0 639.0 jit_solution(9168926206493943016)
XLA Ops:
  7.2 0.0 all-gather.6.cloned.1.call-start
  7.2 0.9 convert_reduce_fusion.1
  8.2 0.9 convert_reduce_fusion
  9.1 24.2 %all-reduce.1 = (f32[512]{0:T(512)S(1)}, f32[512]{0:T(512)S(1)}) all-reduce(f32[512]{0:T(512)S(1)} %convert_reduce_fusion, f32[512]{0:T(512)S(1)} %convert_reduce_fusion.1), channel_id=1, replica_groups=mesh['batch'=16,'row'=4,'col'=4] {'batch'}, use_global_device_ids=true, to_apply=%region_5.0 | all-reduce | flops 1024 | bytes 8192 | tf_op jit(solution)/shard_map/psum | solution.py:19
  33.3 1.0 fusion.8
  34.3 1.0 fusion.12
  35.3 0.7 pad_maximum_fusion
  36.0 0.0 all-gather.6.cloned.1.call-update
  36.0 0.0 all-gather.4.cloned.1.call-start
  36.1 0.7 all-gather.4.cloned.1.call-update
  36.8 0.0 all-gather.8.cloned.1.call-start
  36.8 39.2 %all-gather.6.cloned.1.call-done = bf16[2,128,2048]{2,1,0:T(8,128)(2,1)} async-done(((bf16[2,128,512]{2,1,0:T(8,128)(2,1)}), bf16[2,128,2048]{2,1,0:T(8,128)(2,1)}) %all-gather.6.cloned.1.call-update) | async-done | bytes 1048592 | tf_op jit(solution)/shard_map/all_gather | solution.py:32
  76.0 0.0 all-gather.8.cloned.1.call-update
  76.0 27.1 %all-gather.4.cloned.1.call-done = bf16[2,128,2048]{2,1,0:T(8,128)(2,1)} async-done(((bf16[2,128,512]{2,1,0:T(8,128)(2,1)}), bf16[2,128,2048]{2,1,0:T(8,128)(2,1)}) %all-gather.4.cloned.1.call-update) | async-done | bytes 1048592 | tf_op jit(solution)/shard_map/all_gather | solution.py:30
  103.1 3.7 copy.5
  106.8 5.7 all-to-all-start
  112.6 0.0 reduce-scatter.3.cloned.1.call-start
  112.6 0.2 broadcast_compare_fusion
  112.9 20.7 %all-to-all-done = bf16[2,128,2048]{1,0,2:T(2,128)(2,1)S(1)} async-done(((bf16[2,128,2048]{1,0,2:T(2,128)(2,1)}), bf16[2,128,2048]{1,0,2:T(2,128)(2,1)S(1)}, u32[]{:S(2)}, u32[]{:S(2)}) %all-to-all-start) | async-done | bytes 1048608 | tf_op jit(solution)/shard_map/all_to_all | solution.py:31
  133.6 0.9 copy.6
  134.5 71.7 %all-gather.8.cloned.1.call-done = bf16[2,2048,2048]{2,1,0:T(8,128)(2,1)} async-done(((bf16[2,128,2048]{2,1,0:T(8,128)(2,1)}), bf16[2,2048,2048]{2,1,0:T(8,128)(2,1)}) %all-gather.8.cloned.1.call-update) | async-done | bytes 16777232 | tf_op jit(solution)/shard_map/all_gather | solution.py:33
  206.2 8.4 %fusion.1 = bf16[2,128,2048]{2,1,0:T(8,128)(2,1)S(1)} fusion(bf16[2,2048,128]{2,1,0:T(8,128)(2,1)S(1)} %bitcast.20, bf16[2,2048,2048]{2,1,0:T(8,128)(2,1)} %all-gather.8.cloned.1.call-done, pred[128,2048]{1,0:T(8,128)(4,1)S(1)} %broadcast_compare_fusion), kind=kOutput, calls=%fused_computation.2 | convolution fusion | flops 2149056512 | bytes 19136512 | tf_op jit(solution)/shard_map/vnk,vnp->vkp/dot_general | solution.py:34
  214.6 13.1 %fusion.33 = f32[2,2048,2048]{2,1,0:T(8,128)} fusion(bf16[2,2048,128]{2,1,0:T(8,128)(2,1)S(1)} %bitcast.21, bf16[2,128,2048]{2,1,0:T(8,128)(2,1)S(1)} %fusion.1), kind=kOutput, calls=%fused_computation.55 | convolution fusion | flops 2147483648 | bytes 35651584 | tf_op jit(solution)/shard_map/vnk,vkp->vnp/dot_general | solution.py:51
  227.7 0.0 copy-start
  227.7 0.0 copy-start.1
  227.7 0.0 reduce-scatter.3.cloned.1.call-update
  227.7 0.0 reduce-scatter.5.cloned.1.call-start
  227.8 350.4 %reduce-scatter.3.cloned.1.call-done = f32[2,128,2048]{2,1,0:T(8,128)} async-done(((f32[2,2048,2048]{2,1,0:T(8,128)}), f32[2,128,2048]{2,1,0:T(8,128)}) %reduce-scatter.3.cloned.1.call-update) | async-done | bytes 2097168 | tf_op jit(solution)/shard_map/reduce_scatter | solution.py:54
  578.2 0.0 reduce-scatter.5.cloned.1.call-update
  578.2 27.3 %all-reduce = (f32[512]{0:T(512)S(1)}, f32[512]{0:T(512)S(1)}) all-reduce(f32[512]{0:T(512)S(1)} %get-tuple-element.10, f32[512]{0:T(512)S(1)} %get-tuple-element.8), channel_id=1, replica_groups=mesh['batch'=16,'row'=4,'col'=4] {'batch'}, use_global_device_ids=true, to_apply=%region_3.0 | all-reduce | flops 1024 | bytes 8192 | tf_op jit(solution)/shard_map/psum | solution.py:22
  605.5 25.1 %reduce-scatter.5.cloned.1.call-done = f32[2,128,512]{2,1,0:T(8,128)} async-done(((f32[2,128,2048]{2,1,0:T(8,128)}), f32[2,128,512]{2,1,0:T(8,128)}) %reduce-scatter.5.cloned.1.call-update) | async-done | bytes 524304 | tf_op jit(solution)/shard_map/reduce_scatter | solution.py:55
  630.6 0.0 copy-done
  630.6 0.0 copy-done.1
  630.6 1.9 fusion.11
  (5 shorter events, 0.0 us)
Async XLA Ops:
  7.2 68.8 %all-gather.6.cloned.1.call-start = ((), (), s32[]{:S(2)}) async-start(), calls=%async_computation.4 | async-start | bytes 1310720 | tf_op jit(solution)/shard_map/all_gather | solution.py:32
  36.0 67.1 %all-gather.4.cloned.1.call-start = ((), (), s32[]{:S(2)}) async-start(), calls=%async_computation.3 | async-start | bytes 1310720 | tf_op jit(solution)/shard_map/all_gather | solution.py:30
  36.8 169.4 %all-gather.8.cloned.1.call-start = ((), (), s32[]{:S(2)}) async-start(), calls=%async_computation.5 | async-start | bytes 17825792 | tf_op jit(solution)/shard_map/all_gather | solution.py:33
  106.8 26.7 %all-to-all-start = ((bf16[2,128,2048]{1,0,2:T(2,128)(2,1)}), bf16[2,128,2048]{1,0,2:T(2,128)(2,1)S(1)}, u32[]{:S(2)}, u32[]{:S(2)}) async-start(bf16[2,128,2048]{1,0,2:T(2,128)(2,1)} %copy.5), calls=%async_computation | async-start | bytes 2097152 | tf_op jit(solution)/shard_map/all_to_all | solution.py:31
  112.6 465.6 %reduce-scatter.3.cloned.1.call-start = ((), (), s32[]{:S(2)}) async-start(), calls=%async_computation.6 | async-start | bytes 35651584 | tf_op jit(solution)/shard_map/reduce_scatter | solution.py:54
  227.7 402.9 %copy-start = (bf16[128,512]{1,0:T(8,128)(2,1)S(1)}, bf16[128,512]{1,0:T(8,128)(2,1)}, u32[]{:S(2)}) copy-start(bf16[128,512]{1,0:T(8,128)(2,1)} %param.3) | copy-start | bytes 393220
  227.7 402.9 %copy-start.1 = (bf16[128,512]{1,0:T(8,128)(2,1)S(1)}, bf16[128,512]{1,0:T(8,128)(2,1)}, u32[]{:S(2)}) copy-start(bf16[128,512]{1,0:T(8,128)(2,1)} %param.2) | copy-start | bytes 393220
  227.7 402.8 %reduce-scatter.5.cloned.1.call-start = ((), (), s32[]{:S(2)}) async-start(), calls=%async_computation.7 | async-start | bytes 2621440 | tf_op jit(solution)/shard_map/reduce_scatter | solution.py:55
Sparse Core Ops, SparseCore 0:
  36.1 39.8 all-gather.5
  77.8 25.2 all-gather.3
  105.0 101.2 all-gather.7
  227.9 350.2 reduce-scatter.2
  580.6 49.9 reduce-scatter.4
where the time goes:
time: 643 us; the launch traced here: 639 us
  waiting for transfers between devices  535 us (83%)
  blocking collectives  51.5 us (8%)
  matrix products  21.5 us (3%)
  between operations  13.8 us (2%)
  other arithmetic  6.67 us (1%)
    reduce_scatter x1, waiting for transfers between devices, on_device(): lax.psum_scatter(partial_value, 'batch', scatter_dimension=1, tiled=True)  350 us
    all_gather x1, waiting for transfers between devices, on_device(): col_all = lax.all_gather(col_set, 'batch', axis=1, tiled=True)  71.7 us
    all_gather x1, waiting for transfers between devices, on_device(): col_set = lax.all_gather(stacked, 'row', axis=2, tiled=True)  39.2 us
    psum x1, blocking collectives, on_device(): lax.psum((jnp.sum(cent_one * cent_one, axis=0), jnp.sum(cent_two * cent_t...  27.3 us
    all_gather x1, waiting for transfers between devices, on_device(): row_block = lax.all_gather(stacked, 'col', axis=2, tiled=True)  27.1 us
    reduce_scatter x1, waiting for transfers between devices, on_device(): lax.psum_scatter(own_samples, 'row', scatter_dimension=2, tiled=True)  25.1 us
    psum x1, blocking collectives, on_device(): lax.psum((jnp.sum(first_view, axis=0), jnp.sum(second_view, axis=0)), 'ba...  24.2 us
    all_to_all x1, waiting for transfers between devices, on_device(): lax.all_to_all(row_block, 'batch', split_axis=2, concat_axis=1, tiled=True)  20.7 us
  transfers between devices with their start and end apart: 6, of which 6 were waited for; matrix products, arithmetic and copies ran while one was open for 1% of the time, Pallas kernels for 0%

commit v1 on v0

v1 whole, which is shorter than its diff:
```python
import jax
import jax.numpy as jnp
from jax import lax
from jax.sharding import PartitionSpec as P

BF = jnp.bfloat16
F32 = jnp.float32


def hinge_of(variance):
    std_val = jnp.sqrt(variance + 0.0001)
    return jnp.where(std_val < 1.0, 1.0 / std_val, jnp.zeros_like(std_val))


def swap(x, bit):
    return lax.ppermute(x, "batch", [(i, i ^ bit) for i in range(lax.axis_size("batch"))])


def partner(place, core, turn):
    return place ^ 1 if turn == core else 3 - place


def exchange(x, axis, turn, same=False):
    groups, size = lax.axis_size("batch"), lax.axis_size(axis)
    pairs = [
        (b * size + i, b * size + partner(i, 0 if same else b % 2, turn))
        for b in range(groups)
        for i in range(size)
    ]
    return lax.ppermute(x, ("batch", axis), pairs)


def move(x, places, flip=0):
    pairs = [
        (b, ((b // 4 + places) % 4 * 4 + b % 4) ^ (2 * flip))
        for b in range(lax.axis_size("batch"))
    ]
    return lax.ppermute(x, "batch", pairs)


def scatter_sum(parts, axis, send):
    keep = parts[:2] + exchange(send, axis, 0).astype(F32)
    return keep[0] + exchange(keep[1].astype(BF), axis, 1).astype(F32)


def gather_pair(x, axis):
    return jnp.concatenate([x, exchange(x, axis, 1, same=True)], axis=0)


def full_sum(x, axis):
    for turn in (0, 1):
        x = x + exchange(x.astype(BF), axis, turn).astype(F32)
    return x


def ordered(x, axis, turned, back=False):
    place = lax.axis_index(axis)
    high = place // 2
    low = high ^ (place % 2)
    x = x.reshape((2, 2) + x.shape[1:])
    if back:
        x = jnp.where(turned, x.swapaxes(0, 1), x)
    x = jnp.where(high == 1, x[::-1], x)
    x = jnp.where(low == 1, x[:, ::-1], x)
    if not back:
        x = jnp.where(turned, x.swapaxes(0, 1), x)
    return x.reshape((4,) + x.shape[2:])


def on_device(view_one, view_two):
    local_rows, width = view_one.shape
    groups = lax.axis_size("batch")
    sample_count = local_rows * groups
    place = lax.axis_index("batch")
    first = place // 2 % 2 == 0
    core = place % 2
    other = jnp.where(first, view_two, view_one)
    mine = jnp.where(first, view_one, view_two)
    away, away_far = move(other, 0, flip=1), move(other, 2, flip=1)
    low, high = move(mine, 1), move(mine, -1)
    near = jnp.concatenate([mine, low, away, move(away, 1)], axis=0)
    rest = jnp.concatenate([high, move(away, -1), move(high, -1), away_far], axis=0)
    full = jnp.concatenate([near, rest, swap(near, 1), swap(rest, 1)], axis=0)
    mean_val = jnp.sum(full.astype(F32), axis=0, keepdims=True) / sample_count
    rounded = (full.astype(F32) - mean_val).astype(BF)
    coef_var = sample_count / (2.0 * (sample_count - 1))
    coef_cov = 2.0 * sample_count / (25.0 * (sample_count - 1) * (sample_count - 1))
    quarter = local_rows // 4

    def gram_of(raw, earlier=None):
        own_cent = raw.astype(F32) - mean_val
        own = own_cent.astype(BF)
        blocks = ordered(own.reshape(4, quarter, width), "col", core == 0).reshape(local_rows, width)
        if earlier is not None:
            blocks, earlier = lax.optimization_barrier((blocks, earlier))
        gram = jnp.dot(blocks, rounded.T, preferred_element_type=F32)
        parts = gram.reshape(4, quarter, sample_count)
        return parts, parts[2:].astype(BF)

    def term_of(raw):
        own_cent = raw.astype(F32) - mean_late
        own = own_cent.astype(BF)
        return own.astype(F32) * feature_squares * coef_cov + coef_var * hinge * own_cent

    def pair_of(parts, send):
        total = full_sum(scatter_sum(parts, "col", send), "row").astype(BF)
        return gather_pair(total, "col")

    def away_part(rows, term):
        return (coef_cov * jnp.dot(rows, rounded, preferred_element_type=F32) - term).astype(BF)

    parts_away, send_away = gram_of(away)
    parts_mine, send_mine = gram_of(mine, send_away)
    full_late, mean_late, away_late, mine_late, _ = lax.optimization_barrier(
        (full, mean_val, away, mine, send_mine)
    )
    cent = full_late.astype(F32) - mean_late
    variance = jnp.sum(cent * cent, axis=0, keepdims=True) / (sample_count - 1)
    hinge = hinge_of(variance)
    wide = cent.astype(BF).astype(F32)
    feature_squares = jnp.sum(wide * wide, axis=0, keepdims=True)
    term_away, term_mine = term_of(away_late), term_of(mine_late)
    term_away = ordered(term_away.reshape(4, quarter, width), "col", True)
    term_away = term_away.reshape(2, 2 * quarter, width)
    pair_away = pair_of(parts_away, send_away)
    wide_away = exchange(pair_away, "col", 0, same=True)
    early = away_part(pair_away, term_away[0])
    late = away_part(wide_away, term_away[1])
    extra_other = jnp.concatenate([swap(early, 2), swap(late, 2)], axis=0)
    extra_other = extra_other.astype(F32).reshape(4, quarter, width)
    extra_other = ordered(extra_other, "col", True, back=True).reshape(local_rows, width)
    pair_mine = pair_of(parts_mine, send_mine)
    wide_mine = exchange(pair_mine, "col", 0, same=True)
    whole, _ = lax.optimization_barrier((jnp.concatenate([pair_mine, wide_mine], axis=0), late))
    product = jnp.dot(whole, rounded, preferred_element_type=F32)
    product = ordered(product.reshape(4, quarter, width), "col", True, back=True)
    extra_mine = coef_cov * product.reshape(local_rows, width) - term_mine
    diff = view_one.astype(F32) - view_two.astype(F32)
    grad_one = diff + jnp.where(first, extra_mine, extra_other)
    grad_two = jnp.where(first, extra_other, extra_mine) - diff
    return (grad_one.astype(BF), grad_two.astype(BF))


def solution(mesh):
    in_specs = (P("batch", ("row", "col")), P("batch", ("row", "col")))
    out_specs = (P("batch", ("row", "col")), P("batch", ("row", "col")))
    return jax.shard_map(
        on_device, mesh=mesh, in_specs=in_specs, out_specs=out_specs, check_vma=False
    )
```

time: 643 us -> 74.3 us (0.12)
  waiting for transfers between devices: 535 us -> 22.3 us
  blocking collectives: 51.5 us -> 0 us
  starting transfers between devices: 5.91 us -> 43.4 us
  matrix products: 21.5 us -> 3.3 us
  between operations: 13.8 us -> 1.14 us
    reduce_scatter x2 -> x0, waiting for transfers between devices: 375 us -> none  [the longest x1 350 us: on_device(): lax.psum_scatter(partial_value, 'batch', scatter_dimension=1, tiled=True)]
    all_gather x3 -> x0, waiting for transfers between devices: 138 us -> none  [the longest x1 71.7 us: on_device(): col_all = lax.all_gather(col_set, 'batch', axis=1, tiled=True)]
    psum x2 -> x0, blocking collectives: 51.5 us -> none  [the longest x1 27.3 us: on_device(): lax.psum((jnp.sum(cent_one * cent_one, axis=0), jnp.sum(cent_two * cent_t...]
    ppermute x0 -> x23, starting transfers between devices: none -> 43.4 us  [the longest x12 34.8 us: exchange(): return lax.ppermute(x, ('batch', axis), pairs)]
    ppermute x0 -> x23, waiting for transfers between devices: none -> 22.3 us  [the longest x12 11.6 us: exchange(): return lax.ppermute(x, ('batch', axis), pairs)]
    all_to_all x1 -> x0, waiting for transfers between devices: 20.7 us -> none  [on_device(): lax.all_to_all(row_block, 'batch', split_axis=2, concat_axis=1, tiled=True)]
    dot_general x2 -> x5, matrix products: 21.5 us -> 3.3 us  [the longest x2 1.69 us: gram_of(): gram = jnp.dot(blocks, rounded.T, preferred_element_type=F32)]
  transfers between devices with their start and end apart: 6 -> 23, of which waited for: 6 -> 14; matrix products, arithmetic and copies ran while one was open for 1% -> 5% of each run, Pallas kernels for 0% -> 0%
where the time goes in v1:
time: 74.3 us; the launch traced here: 74.2 us
  starting transfers between devices  43.4 us (58%)
  waiting for transfers between devices  22.3 us (30%)
  other arithmetic  3.77 us (5%)
  matrix products  3.3 us (4%)
  between operations  1.14 us (2%)
    ppermute x12, starting transfers between devices, exchange(): return lax.ppermute(x, ('batch', axis), pairs)  34.8 us
    ppermute x12, waiting for transfers between devices, exchange(): return lax.ppermute(x, ('batch', axis), pairs)  11.6 us
    ppermute x7, starting transfers between devices, move(): return lax.ppermute(x, 'batch', pairs)  8.22 us
    ppermute x7, waiting for transfers between devices, move(): return lax.ppermute(x, 'batch', pairs)  7.73 us
    ppermute x4, waiting for transfers between devices, swap(): lax.ppermute(x, 'batch', [(i, i ^ bit) for i in range(lax.axis_size('batc...  3.06 us
    dot_general x2, matrix products, gram_of(): gram = jnp.dot(blocks, rounded.T, preferred_element_type=F32)  1.69 us
  transfers between devices with their start and end apart: 23, of which 14 were waited for; matrix products, arithmetic and copies ran while one was open for 5% of the time, Pallas kernels for 0%

profile of v1, /device:TPU:38, one launch (start us, length us, event | category | flops | bytes accessed | tf_op | source)
XLA Modules:
  0.0 74.2 jit_solution(9832274874767510562)
XLA Ops:
  0.7 1.0 %constant_dynamic-update-slice_fusion.9 = (bf16[2048,512]{1,0:T(8,128)(2,1)S(1)}, bf16[128,512]{1,0:T(8,128)(2,1)S(1)}, bf16[128,512]{1,0:T(8,128)(2,1)S(1)}) fusion(bf16[128,512]{1,0:T(8,128)(2,1)} %param.2, bf16[128,512]{1,0:T(8,128)(2,1)} %param.3, pred[]{:T(512)S(6)} %eq.29), kind=kLoop, calls=%fused_computation.85 | loop fusion | flops 131071 | bytes 655361
  1.7 0.2 collective-permute-start.1
  1.9 0.8 %collective-permute-start.3 = (bf16[128,512]{1,0:T(8,128)(2,1)S(1)}, bf16[128,512]{1,0:T(8,128)(2,1)S(1)}, u32[]{:S(2)}, u32[]{:S(2)}) collective-permute-start(bf16[128,512]{1,0:T(8,128)(2,1)S(1)} %get-tuple-element.13), channel_id=1, source_target_pairs={{0,192},{16,208},{32,224},{48,240},{64,0},{80,16},{96,32},{112,48}... | collective-permute-start | bytes 393224 | tf_op jit(solution)/shard_map/ppermute | solution.py:38
  2.7 2.4 %collective-permute-start = (bf16[128,512]{1,0:T(8,128)(2,1)S(1)}, bf16[128,512]{1,0:T(8,128)(2,1)S(1)}, u32[]{:S(2)}, u32[]{:S(2)}) collective-permute-start(bf16[128,512]{1,0:T(8,128)(2,1)S(1)} %get-tuple-element.13), channel_id=1, source_target_pairs={{0,64},{16,80},{32,96},{48,112},{64,128},{80,144},{96,160},{112,17... | collective-permute-start | bytes 393224 | tf_op jit(solution)/shard_map/ppermute | solution.py:38
  5.1 1.5 %collective-permute-start.6 = (bf16[128,512]{1,0:T(8,128)(2,1)S(1)}, bf16[128,512]{1,0:T(8,128)(2,1)S(1)}, u32[]{:S(2)}, u32[]{:S(2)}) collective-permute-start(bf16[128,512]{1,0:T(8,128)(2,1)S(1)} %get-tuple-element.22), channel_id=1, source_target_pairs={{0,160},{16,176},{32,128},{48,144},{64,224},{80,240},{96,192},{112... | collective-permute-start | bytes 393224 | tf_op jit(solution)/shard_map/ppermute | solution.py:38
  6.7 0.4 collective-permute-done.1
  7.1 1.0 %collective-permute-start.4 = (bf16[128,512]{1,0:T(8,128)(2,1)S(1)}, bf16[128,512]{1,0:T(8,128)(2,1)S(1)}, u32[]{:S(2)}, u32[]{:S(2)}) collective-permute-start(bf16[128,512]{1,0:T(8,128)(2,1)S(1)} %collective-permute-done.1), channel_id=1, source_target_pairs={{0,192},{16,208},{32,224},{48,240},{64,0},{80,16},{96,32},{112,48}... | collective-permute-start | bytes 393224 | tf_op jit(solution)/shard_map/ppermute | solution.py:38
  8.1 2.2 %collective-permute-start.2 = (bf16[128,512]{1,0:T(8,128)(2,1)S(1)}, bf16[128,512]{1,0:T(8,128)(2,1)S(1)}, u32[]{:S(2)}, u32[]{:S(2)}) collective-permute-start(bf16[128,512]{1,0:T(8,128)(2,1)S(1)} %collective-permute-done.1), channel_id=1, source_target_pairs={{0,64},{16,80},{32,96},{48,112},{64,128},{80,144},{96,160},{112,17... | collective-permute-start | bytes 393224 | tf_op jit(solution)/shard_map/ppermute | solution.py:38
  10.3 0.3 collective-permute-done
  10.6 2.8 %collective-permute-done.2 = bf16[128,512]{1,0:T(8,128)(2,1)S(1)} collective-permute-done((bf16[128,512]{1,0:T(8,128)(2,1)S(1)}, bf16[128,512]{1,0:T(8,128)(2,1)S(1)}, u32[]{:S(2)}, u32[]{:S(2)}) %collective-permute-start.2) | collective-permute-done | bytes 131104 | tf_op jit(solution)/shard_map/ppermute | solution.py:38
  13.5 0.1 collective-permute-start.7
  13.6 1.8 %collective-permute-done.4 = bf16[128,512]{1,0:T(8,128)(2,1)S(1)} collective-permute-done((bf16[128,512]{1,0:T(8,128)(2,1)S(1)}, bf16[128,512]{1,0:T(8,128)(2,1)S(1)}, u32[]{:S(2)}, u32[]{:S(2)}) %collective-permute-start.4) | collective-permute-done | bytes 131104 | tf_op jit(solution)/shard_map/ppermute | solution.py:38
  15.4 2.4 %collective-permute-done.5 = bf16[128,512]{1,0:T(8,128)(2,1)S(1)} collective-permute-done((bf16[128,512]{1,0:T(8,128)(2,1)S(1)}, bf16[128,512]{1,0:T(8,128)(2,1)S(1)}, u32[]{:S(2)}, u32[]{:S(2)}) %collective-permute-start.5) | collective-permute-done | bytes 131104 | tf_op jit(solution)/shard_map/ppermute | solution.py:38
  17.9 0.1 collective-permute-start.8
  18.1 1.7 %collective-permute-done.8 = bf16[512,512]{1,0:T(8,128)(2,1)S(1)} collective-permute-done((bf16[512,512]{1,0:T(8,128)(2,1)S(1)}, bf16[512,512]{1,0:T(8,128)(2,1)S(1)}, u32[]{:S(2)}, u32[]{:S(2)}) %collective-permute-start.8) | collective-permute-done | bytes 524320 | tf_op jit(solution)/shard_map/ppermute | solution.py:16
  19.9 0.3 convert_reduce_fusion
  20.4 0.8 %fusion.12 = f32[128,2048]{1,0:T(8,128)S(1)} fusion(bf16[128,512]{1,0:T(8,128)(2,1)S(1)} %bitcast.84, bf16[2048,512]{1,0:T(8,128)(2,1)S(1)} %constant_dynamic-update-slice_fusion, f32[512]{0:T(512)S(1)} %broadcast_multiply_fusion), kind=kOutput, calls=%fused_computation.15 | convolution fusion | flops 271581184 | bytes 3278848 | tf_op jit(solution)/shard_map/dot_general | solution.py:96
  21.4 1.7 %collective-permute-start.15 = (bf16[2,32,2048]{2,1,0:T(8,128)(2,1)S(1)}, bf16[2,32,2048]{2,1,0:T(8,128)(2,1)S(1)}, u32[]{:S(2)}, u32[]{:S(2)}) collective-permute-start(bf16[2,32,2048]{2,1,0:T(8,128)(2,1)S(1)} %bitcast.80), channel_id=1, source_target_pairs={{0,1},{1,0},{2,3},{3,2},{16,19},{17,18},{18,17},{19,16},{32,33},{3... | collective-permute-start | bytes 786440 | tf_op jit(solution)/shard_map/ppermute | solution.py:30
  23.0 0.8 %fusion.10 = f32[128,2048]{1,0:T(8,128)S(1)} fusion(bf16[128,512]{1,0:T(8,128)(2,1)S(1)} %bitcast.83, bf16[2048,512]{1,0:T(8,128)(2,1)S(1)} %constant_dynamic-update-slice_fusion, f32[512]{0:T(512)S(1)} %broadcast_multiply_fusion), kind=kOutput, calls=%fused_computation.14 | convolution fusion | flops 271581184 | bytes 3278848 | tf_op jit(solution)/shard_map/dot_general | solution.py:96
  23.9 0.5 collective-permute-start.9
  24.5 0.6 multiply_reduce_fusion.1
  25.1 0.1 multiply_add_fusion
  25.3 2.5 %collective-permute-done.15 = bf16[2,32,2048]{2,1,0:T(8,128)(2,1)S(1)} collective-permute-done((bf16[2,32,2048]{2,1,0:T(8,128)(2,1)S(1)}, bf16[2,32,2048]{2,1,0:T(8,128)(2,1)S(1)}, u32[]{:S(2)}, u32[]{:S(2)}) %collective-permute-start.15) | collective-permute-done | bytes 262176 | tf_op jit(solution)/shard_map/ppermute | solution.py:30
  27.9 3.1 %collective-permute-start.16 = (bf16[32,2048]{1,0:T(8,128)(2,1)S(1)}, bf16[32,2048]{1,0:T(8,128)(2,1)S(1)}, u32[]{:S(2)}, u32[]{:S(2)}) collective-permute-start(bf16[32,2048]{1,0:T(8,128)(2,1)S(1)} %fusion.27), channel_id=1, source_target_pairs={{0,3},{1,2},{2,1},{3,0},{16,17},{17,16},{18,19},{19,18},{32,35},{3... | collective-permute-start | bytes 393224 | tf_op jit(solution)/shard_map/ppermute | solution.py:30
  31.1 2.7 %collective-permute-start.10 = (bf16[32,2048]{1,0:T(8,128)(2,1)S(1)}, bf16[32,2048]{1,0:T(8,128)(2,1)S(1)}, u32[]{:S(2)}, u32[]{:S(2)}) collective-permute-start(bf16[32,2048]{1,0:T(8,128)(2,1)S(1)} %fusion.26), channel_id=1, source_target_pairs={{0,3},{1,2},{2,1},{3,0},{16,17},{17,16},{18,19},{19,18},{32,35},{3... | collective-permute-start | bytes 393224 | tf_op jit(solution)/shard_map/ppermute | solution.py:30
  33.8 0.3 collective-permute-done.16
  34.2 3.4 %collective-permute-start.17 = (bf16[32,2048]{1,0:T(8,128)(2,1)S(1)}, bf16[32,2048]{1,0:T(8,128)(2,1)S(1)}, u32[]{:S(2)}, u32[]{:S(2)}) collective-permute-start(bf16[32,2048]{1,0:T(8,128)(2,1)S(1)} %fusion.30), channel_id=1, source_target_pairs={{0,4},{4,0},{8,12},{12,8},{16,28},{20,24},{24,20},{28,16},{32,36},... | collective-permute-start | bytes 393224 | tf_op jit(solution)/shard_map/ppermute | solution.py:30
  37.6 3.3 %collective-permute-start.11 = (bf16[32,2048]{1,0:T(8,128)(2,1)S(1)}, bf16[32,2048]{1,0:T(8,128)(2,1)S(1)}, u32[]{:S(2)}, u32[]{:S(2)}) collective-permute-start(bf16[32,2048]{1,0:T(8,128)(2,1)S(1)} %fusion.29), channel_id=1, source_target_pairs={{0,4},{4,0},{8,12},{12,8},{16,28},{20,24},{24,20},{28,16},{32,36},... | collective-permute-start | bytes 393224 | tf_op jit(solution)/shard_map/ppermute | solution.py:30
  40.9 0.2 collective-permute-done.17
  41.2 5.4 %collective-permute-start.18 = (bf16[32,2048]{1,0:T(8,128)(2,1)S(1)}, bf16[32,2048]{1,0:T(8,128)(2,1)S(1)}, u32[]{:S(2)}, u32[]{:S(2)}) collective-permute-start(bf16[32,2048]{1,0:T(8,128)(2,1)S(1)} %fusion.25), channel_id=1, source_target_pairs={{0,12},{4,8},{8,4},{12,0},{16,20},{20,16},{24,28},{28,24},{32,44},... | collective-permute-start | bytes 393224 | tf_op jit(solution)/shard_map/ppermute | solution.py:30
  46.6 0.6 collective-permute-done.11
  47.2 6.3 %collective-permute-start.12 = (bf16[32,2048]{1,0:T(8,128)(2,1)S(1)}, bf16[32,2048]{1,0:T(8,128)(2,1)S(1)}, u32[]{:S(2)}, u32[]{:S(2)}) collective-permute-start(bf16[32,2048]{1,0:T(8,128)(2,1)S(1)} %fusion.24), channel_id=1, source_target_pairs={{0,12},{4,8},{8,4},{12,0},{16,20},{20,16},{24,28},{28,24},{32,44},... | collective-permute-start | bytes 393224 | tf_op jit(solution)/shard_map/ppermute | solution.py:30
  53.5 0.1 add_convert_fusion
  53.6 4.5 %collective-permute-start.19 = (bf16[32,2048]{1,0:T(8,128)(2,1)S(1)}, bf16[32,2048]{1,0:T(8,128)(2,1)S(1)}, u32[]{:S(2)}, u32[]{:S(2)}) collective-permute-start(bf16[32,2048]{1,0:T(8,128)(2,1)S(1)} %add_convert_fusion), channel_id=1, source_target_pairs={{0,3},{1,2},{2,1},{3,0},{16,19},{17,18},{18,17},{19,16},{32,35},{3... | collective-permute-start | bytes 393224 | tf_op jit(solution)/shard_map/ppermute | solution.py:30
  58.1 0.1 add_convert_fusion.1
  58.2 3.6 %collective-permute-start.13 = (bf16[32,2048]{1,0:T(8,128)(2,1)S(1)}, bf16[32,2048]{1,0:T(8,128)(2,1)S(1)}, u32[]{:S(2)}, u32[]{:S(2)}) collective-permute-start(bf16[32,2048]{1,0:T(8,128)(2,1)S(1)} %add_convert_fusion.1), channel_id=1, source_target_pairs={{0,3},{1,2},{2,1},{3,0},{16,19},{17,18},{18,17},{19,16},{32,35},{3... | collective-permute-start | bytes 393224 | tf_op jit(solution)/shard_map/ppermute | solution.py:30
  61.8 0.1 collective-permute-start.20
  61.9 0.5 fusion.5
  62.5 0.1 collective-permute-start.21
  62.6 2.2 %collective-permute-done.13 = bf16[32,2048]{1,0:T(8,128)(2,1)S(1)} collective-permute-done((bf16[32,2048]{1,0:T(8,128)(2,1)S(1)}, bf16[32,2048]{1,0:T(8,128)(2,1)S(1)}, u32[]{:S(2)}, u32[]{:S(2)}) %collective-permute-start.13) | collective-permute-done | bytes 131104 | tf_op jit(solution)/shard_map/ppermute | solution.py:30
  64.8 0.1 collective-permute-start.14
  64.9 3.4 %collective-permute-done.20 = bf16[64,2048]{1,0:T(8,128)(2,1)S(1)} collective-permute-done((bf16[64,2048]{1,0:T(8,128)(2,1)S(1)}, bf16[64,2048]{1,0:T(8,128)(2,1)S(1)}, u32[]{:S(2)}, u32[]{:S(2)}) %collective-permute-start.20) | collective-permute-done | bytes 262176 | tf_op jit(solution)/shard_map/ppermute | solution.py:30
  68.3 0.5 fusion.4
  68.8 0.1 collective-permute-start.22
  69.0 2.3 %collective-permute-done.14 = bf16[64,2048]{1,0:T(8,128)(2,1)S(1)} collective-permute-done((bf16[64,2048]{1,0:T(8,128)(2,1)S(1)}, bf16[64,2048]{1,0:T(8,128)(2,1)S(1)}, u32[]{:S(2)}, u32[]{:S(2)}) %collective-permute-start.14) | collective-permute-done | bytes 262176 | tf_op jit(solution)/shard_map/ppermute | solution.py:30
  71.3 0.5 fusion.7
  71.9 1.3 %collective-permute-done.22 = bf16[64,512]{1,0:T(8,128)(2,1)S(1)} collective-permute-done((bf16[64,512]{1,0:T(8,128)(2,1)S(1)}, bf16[64,512]{1,0:T(8,128)(2,1)S(1)}, u32[]{:S(2)}, u32[]{:S(2)}) %collective-permute-start.22) | collective-permute-done | bytes 65568 | tf_op jit(solution)/shard_map/ppermute | solution.py:16
  73.4 0.8 %fusion.21 = (bf16[128,512]{1,0:T(8,128)(2,1)}, bf16[128,512]{1,0:T(8,128)(2,1)}) fusion(f32[2,2,32,512]{3,2,1,0:T(8,128)S(1)} %reverse_select_fusion, bf16[128,512]{1,0:T(8,128)(2,1)S(1)} %copy-done.3, bf16[128,512]{1,0:T(8,128)(2,1)S(1)} %copy-done.2, pred[]{:T(512)S(6)} %eq.29, f32[512]{0:T(512)S(1)} %fusion.31, f32[512]{0:T(512)S(1)} %get-tuple-element.14, ...), kind=kLoop, calls=%fused_computation.44 | loop fusion | flops 1179648 | bytes 1185793 | tf_op jit(solution)/shard_map/convert_element_type | solution.py:141
  (63 shorter events, 1.1 us)
Async XLA Ops:
  1.7 5.4 %collective-permute-start.1 = (bf16[128,512]{1,0:T(8,128)(2,1)S(1)}, bf16[128,512]{1,0:T(8,128)(2,1)S(1)}, u32[]{:S(2)}, u32[]{:S(2)}) collective-permute-start(bf16[128,512]{1,0:T(8,128)(2,1)S(1)} %get-tuple-element.22), channel_id=1, source_target_pairs={{0,32},{16,48},{32,0},{48,16},{64,96},{80,112},{96,64},{112,80},{1... | collective-permute-start | bytes 393224 | tf_op jit(solution)/shard_map/ppermute | solution.py:38
  1.9 8.4 %collective-permute-start.3 = (bf16[128,512]{1,0:T(8,128)(2,1)S(1)}, bf16[128,512]{1,0:T(8,128)(2,1)S(1)}, u32[]{:S(2)}, u32[]{:S(2)}) collective-permute-start(bf16[128,512]{1,0:T(8,128)(2,1)S(1)} %get-tuple-element.13), channel_id=1, source_target_pairs={{0,192},{16,208},{32,224},{48,240},{64,0},{80,16},{96,32},{112,48}... | collective-permute-start | bytes 393224 | tf_op jit(solution)/shard_map/ppermute | solution.py:38
  2.7 7.9 %collective-permute-start = (bf16[128,512]{1,0:T(8,128)(2,1)S(1)}, bf16[128,512]{1,0:T(8,128)(2,1)S(1)}, u32[]{:S(2)}, u32[]{:S(2)}) collective-permute-start(bf16[128,512]{1,0:T(8,128)(2,1)S(1)} %get-tuple-element.13), channel_id=1, source_target_pairs={{0,64},{16,80},{32,96},{48,112},{64,128},{80,144},{96,160},{112,17... | collective-permute-start | bytes 393224 | tf_op jit(solution)/shard_map/ppermute | solution.py:38
  5.1 8.5 %collective-permute-start.6 = (bf16[128,512]{1,0:T(8,128)(2,1)S(1)}, bf16[128,512]{1,0:T(8,128)(2,1)S(1)}, u32[]{:S(2)}, u32[]{:S(2)}) collective-permute-start(bf16[128,512]{1,0:T(8,128)(2,1)S(1)} %get-tuple-element.22), channel_id=1, source_target_pairs={{0,160},{16,176},{32,128},{48,144},{64,224},{80,240},{96,192},{112... | collective-permute-start | bytes 393224 | tf_op jit(solution)/shard_map/ppermute | solution.py:38
  7.1 8.4 %collective-permute-start.4 = (bf16[128,512]{1,0:T(8,128)(2,1)S(1)}, bf16[128,512]{1,0:T(8,128)(2,1)S(1)}, u32[]{:S(2)}, u32[]{:S(2)}) collective-permute-start(bf16[128,512]{1,0:T(8,128)(2,1)S(1)} %collective-permute-done.1), channel_id=1, source_target_pairs={{0,192},{16,208},{32,224},{48,240},{64,0},{80,16},{96,32},{112,48}... | collective-permute-start | bytes 393224 | tf_op jit(solution)/shard_map/ppermute | solution.py:38
  8.1 5.4 %collective-permute-start.2 = (bf16[128,512]{1,0:T(8,128)(2,1)S(1)}, bf16[128,512]{1,0:T(8,128)(2,1)S(1)}, u32[]{:S(2)}, u32[]{:S(2)}) collective-permute-start(bf16[128,512]{1,0:T(8,128)(2,1)S(1)} %collective-permute-done.1), channel_id=1, source_target_pairs={{0,64},{16,80},{32,96},{48,112},{64,128},{80,144},{96,160},{112,17... | collective-permute-start | bytes 393224 | tf_op jit(solution)/shard_map/ppermute | solution.py:38
  10.3 7.5 %collective-permute-start.5 = (bf16[128,512]{1,0:T(8,128)(2,1)S(1)}, bf16[128,512]{1,0:T(8,128)(2,1)S(1)}, u32[]{:S(2)}, u32[]{:S(2)}) collective-permute-start(bf16[128,512]{1,0:T(8,128)(2,1)S(1)} %collective-permute-done.3), channel_id=1, source_target_pairs={{0,192},{16,208},{32,224},{48,240},{64,0},{80,16},{96,32},{112,48}... | collective-permute-start | bytes 393224 | tf_op jit(solution)/shard_map/ppermute | solution.py:38
  13.5 4.5 %collective-permute-start.7 = (bf16[512,512]{1,0:T(8,128)(2,1)S(1)}, bf16[512,512]{1,0:T(8,128)(2,1)S(1)}, u32[]{:S(2)}, u32[]{:S(2)}) collective-permute-start(bf16[512,512]{1,0:T(8,128)(2,1)S(1)} %pad_maximum_fusion), channel_id=1, source_target_pairs={{0,16},{16,0},{32,48},{48,32},{64,80},{80,64},{96,112},{112,96},{1... | collective-permute-start | bytes 1572872 | tf_op jit(solution)/shard_map/ppermute | solution.py:16
  17.9 2.0 %collective-permute-start.8 = (bf16[512,512]{1,0:T(8,128)(2,1)S(1)}, bf16[512,512]{1,0:T(8,128)(2,1)S(1)}, u32[]{:S(2)}, u32[]{:S(2)}) collective-permute-start(bf16[512,512]{1,0:T(8,128)(2,1)S(1)} %pad_maximum_fusion.1), channel_id=1, source_target_pairs={{0,16},{16,0},{32,48},{48,32},{64,80},{80,64},{96,112},{112,96},{1... | collective-permute-start | bytes 1572872 | tf_op jit(solution)/shard_map/ppermute | solution.py:16
  21.2 2.6 %copy-start = (f32[128,2048]{1,0:T(8,128)}, f32[128,2048]{1,0:T(8,128)S(1)}, u32[]{:S(2)}) copy-start(f32[128,2048]{1,0:T(8,128)S(1)} %fusion.12) | copy-start | bytes 3145732
  21.4 6.5 %collective-permute-start.15 = (bf16[2,32,2048]{2,1,0:T(8,128)(2,1)S(1)}, bf16[2,32,2048]{2,1,0:T(8,128)(2,1)S(1)}, u32[]{:S(2)}, u32[]{:S(2)}) collective-permute-start(bf16[2,32,2048]{2,1,0:T(8,128)(2,1)S(1)} %bitcast.80), channel_id=1, source_target_pairs={{0,1},{1,0},{2,3},{3,2},{16,19},{17,18},{18,17},{19,16},{32,33},{3... | collective-permute-start | bytes 786440 | tf_op jit(solution)/shard_map/ppermute | solution.py:30
  23.9 1.3 %copy-start.1 = (f32[128,2048]{1,0:T(8,128)}, f32[128,2048]{1,0:T(8,128)S(1)}, u32[]{:S(2)}) copy-start(f32[128,2048]{1,0:T(8,128)S(1)} %fusion.10) | copy-start | bytes 3145732
  23.9 3.9 %slice-start = ((f32[128,2048]{1,0:T(8,128)}), f32[64,2048]{1,0:T(8,128)S(1)}, s32[]{:S(2)}) async-start(f32[128,2048]{1,0:T(8,128)} %copy-done), calls=%async_computation | async-start | bytes 1048576 | tf_op jit(solution)/shard_map/slice | solution.py:42
  23.9 7.1 %collective-permute-start.9 = (bf16[2,32,2048]{2,1,0:T(8,128)(2,1)S(1)}, bf16[2,32,2048]{2,1,0:T(8,128)(2,1)S(1)}, u32[]{:S(2)}, u32[]{:S(2)}) collective-permute-start(bf16[2,32,2048]{2,1,0:T(8,128)(2,1)S(1)} %bitcast.81), channel_id=1, source_target_pairs={{0,1},{1,0},{2,3},{3,2},{16,19},{17,18},{18,17},{19,16},{32,33},{3... | collective-permute-start | bytes 786440 | tf_op jit(solution)/shard_map/ppermute | solution.py:30
  25.2 5.8 %slice-start.1 = ((f32[128,2048]{1,0:T(8,128)}), f32[64,2048]{1,0:T(8,128)S(1)}, s32[]{:S(2)}) async-start(f32[128,2048]{1,0:T(8,128)} %copy-done.1), calls=%async_computation.1 | async-start | bytes 1048576 | tf_op jit(solution)/shard_map/slice | solution.py:42
  27.9 6.3 %collective-permute-start.16 = (bf16[32,2048]{1,0:T(8,128)(2,1)S(1)}, bf16[32,2048]{1,0:T(8,128)(2,1)S(1)}, u32[]{:S(2)}, u32[]{:S(2)}) collective-permute-start(bf16[32,2048]{1,0:T(8,128)(2,1)S(1)} %fusion.27), channel_id=1, source_target_pairs={{0,3},{1,2},{2,1},{3,0},{16,17},{17,16},{18,19},{19,18},{32,35},{3... | collective-permute-start | bytes 393224 | tf_op jit(solution)/shard_map/ppermute | solution.py:30
  31.1 6.5 %collective-permute-start.10 = (bf16[32,2048]{1,0:T(8,128)(2,1)S(1)}, bf16[32,2048]{1,0:T(8,128)(2,1)S(1)}, u32[]{:S(2)}, u32[]{:S(2)}) collective-permute-start(bf16[32,2048]{1,0:T(8,128)(2,1)S(1)} %fusion.26), channel_id=1, source_target_pairs={{0,3},{1,2},{2,1},{3,0},{16,17},{17,16},{18,19},{19,18},{32,35},{3... | collective-permute-start | bytes 393224 | tf_op jit(solution)/shard_map/ppermute | solution.py:30
  34.2 7.0 %collective-permute-start.17 = (bf16[32,2048]{1,0:T(8,128)(2,1)S(1)}, bf16[32,2048]{1,0:T(8,128)(2,1)S(1)}, u32[]{:S(2)}, u32[]{:S(2)}) collective-permute-start(bf16[32,2048]{1,0:T(8,128)(2,1)S(1)} %fusion.30), channel_id=1, source_target_pairs={{0,4},{4,0},{8,12},{12,8},{16,28},{20,24},{24,20},{28,16},{32,36},... | collective-permute-start | bytes 393224 | tf_op jit(solution)/shard_map/ppermute | solution.py:30
  37.6 9.6 %collective-permute-start.11 = (bf16[32,2048]{1,0:T(8,128)(2,1)S(1)}, bf16[32,2048]{1,0:T(8,128)(2,1)S(1)}, u32[]{:S(2)}, u32[]{:S(2)}) collective-permute-start(bf16[32,2048]{1,0:T(8,128)(2,1)S(1)} %fusion.29), channel_id=1, source_target_pairs={{0,4},{4,0},{8,12},{12,8},{16,28},{20,24},{24,20},{28,16},{32,36},... | collective-permute-start | bytes 393224 | tf_op jit(solution)/shard_map/ppermute | solution.py:30
  41.2 12.3 %collective-permute-start.18 = (bf16[32,2048]{1,0:T(8,128)(2,1)S(1)}, bf16[32,2048]{1,0:T(8,128)(2,1)S(1)}, u32[]{:S(2)}, u32[]{:S(2)}) collective-permute-start(bf16[32,2048]{1,0:T(8,128)(2,1)S(1)} %fusion.25), channel_id=1, source_target_pairs={{0,12},{4,8},{8,4},{12,0},{16,20},{20,16},{24,28},{28,24},{32,44},... | collective-permute-start | bytes 393224 | tf_op jit(solution)/shard_map/ppermute | solution.py:30
  47.2 10.9 %collective-permute-start.12 = (bf16[32,2048]{1,0:T(8,128)(2,1)S(1)}, bf16[32,2048]{1,0:T(8,128)(2,1)S(1)}, u32[]{:S(2)}, u32[]{:S(2)}) collective-permute-start(bf16[32,2048]{1,0:T(8,128)(2,1)S(1)} %fusion.24), channel_id=1, source_target_pairs={{0,12},{4,8},{8,4},{12,0},{16,20},{20,16},{24,28},{28,24},{32,44},... | collective-permute-start | bytes 393224 | tf_op jit(solution)/shard_map/ppermute | solution.py:30
  53.6 8.2 %collective-permute-start.19 = (bf16[32,2048]{1,0:T(8,128)(2,1)S(1)}, bf16[32,2048]{1,0:T(8,128)(2,1)S(1)}, u32[]{:S(2)}, u32[]{:S(2)}) collective-permute-start(bf16[32,2048]{1,0:T(8,128)(2,1)S(1)} %add_convert_fusion), channel_id=1, source_target_pairs={{0,3},{1,2},{2,1},{3,0},{16,19},{17,18},{18,17},{19,16},{32,35},{3... | collective-permute-start | bytes 393224 | tf_op jit(solution)/shard_map/ppermute | solution.py:30
  58.2 6.6 %collective-permute-start.13 = (bf16[32,2048]{1,0:T(8,128)(2,1)S(1)}, bf16[32,2048]{1,0:T(8,128)(2,1)S(1)}, u32[]{:S(2)}, u32[]{:S(2)}) collective-permute-start(bf16[32,2048]{1,0:T(8,128)(2,1)S(1)} %add_convert_fusion.1), channel_id=1, source_target_pairs={{0,3},{1,2},{2,1},{3,0},{16,19},{17,18},{18,17},{19,16},{32,35},{3... | collective-permute-start | bytes 393224 | tf_op jit(solution)/shard_map/ppermute | solution.py:30
  61.8 6.5 %collective-permute-start.20 = (bf16[64,2048]{1,0:T(8,128)(2,1)S(1)}, bf16[64,2048]{1,0:T(8,128)(2,1)S(1)}, u32[]{:S(2)}, u32[]{:S(2)}) collective-permute-start(bf16[64,2048]{1,0:T(8,128)(2,1)S(1)} %pad_maximum_fusion.4), channel_id=1, source_target_pairs={{0,1},{1,0},{2,3},{3,2},{16,17},{17,16},{18,19},{19,18},{32,33},{3... | collective-permute-start | bytes 786440 | tf_op jit(solution)/shard_map/ppermute | solution.py:30
  62.5 9.4 %collective-permute-start.21 = (bf16[64,512]{1,0:T(8,128)(2,1)S(1)}, bf16[64,512]{1,0:T(8,128)(2,1)S(1)}, u32[]{:S(2)}, u32[]{:S(2)}) collective-permute-start(bf16[64,512]{1,0:T(8,128)(2,1)S(1)} %fusion.5), channel_id=1, source_target_pairs={{0,32},{16,48},{32,0},{48,16},{64,96},{80,112},{96,64},{112,80},{1... | collective-permute-start | bytes 196616 | tf_op jit(solution)/shard_map/ppermute | solution.py:16
  64.8 6.5 %collective-permute-start.14 = (bf16[64,2048]{1,0:T(8,128)(2,1)S(1)}, bf16[64,2048]{1,0:T(8,128)(2,1)S(1)}, u32[]{:S(2)}, u32[]{:S(2)}) collective-permute-start(bf16[64,2048]{1,0:T(8,128)(2,1)S(1)} %pad_maximum_fusion.3), channel_id=1, source_target_pairs={{0,1},{1,0},{2,3},{3,2},{16,17},{17,16},{18,19},{19,18},{32,33},{3... | collective-permute-start | bytes 786440 | tf_op jit(solution)/shard_map/ppermute | solution.py:30
  68.8 4.4 %collective-permute-start.22 = (bf16[64,512]{1,0:T(8,128)(2,1)S(1)}, bf16[64,512]{1,0:T(8,128)(2,1)S(1)}, u32[]{:S(2)}, u32[]{:S(2)}) collective-permute-start(bf16[64,512]{1,0:T(8,128)(2,1)S(1)} %fusion.4), channel_id=1, source_target_pairs={{0,32},{16,48},{32,0},{48,16},{64,96},{80,112},{96,64},{112,80},{1... | collective-permute-start | bytes 196616 | tf_op jit(solution)/shard_map/ppermute | solution.py:16
  71.8 1.5 %copy-start.2 = (bf16[128,512]{1,0:T(8,128)(2,1)S(1)}, bf16[128,512]{1,0:T(8,128)(2,1)}, u32[]{:S(2)}) copy-start(bf16[128,512]{1,0:T(8,128)(2,1)} %param.2) | copy-start | bytes 393220
  71.8 1.5 %copy-start.3 = (bf16[128,512]{1,0:T(8,128)(2,1)S(1)}, bf16[128,512]{1,0:T(8,128)(2,1)}, u32[]{:S(2)}) copy-start(bf16[128,512]{1,0:T(8,128)(2,1)} %param.3) | copy-start | bytes 393220

commit v2 on v1

--- a/solution.py
+++ b/solution.py
@@ -135,9 +135,10 @@
     product = jnp.dot(whole, rounded, preferred_element_type=F32)
     product = ordered(product.reshape(4, quarter, width), "col", True, back=True)
     extra_mine = coef_cov * product.reshape(local_rows, width) - term_mine
-    diff = view_one.astype(F32) - view_two.astype(F32)
-    grad_one = diff + jnp.where(first, extra_mine, extra_other)
-    grad_two = jnp.where(first, extra_other, extra_mine) - diff
+    diff = mine.astype(F32) - other.astype(F32)
+    grad_mine, grad_other = diff + extra_mine, extra_other - diff
+    grad_one = jnp.where(first, grad_mine, grad_other)
+    grad_two = jnp.where(first, grad_other, grad_mine)
     return (grad_one.astype(BF), grad_two.astype(BF))
 
 

time: 74.3 us -> 74.3 us (level)
  no operation moved by 1% of the time
where the time goes in v2:
time: 74.3 us; the launch traced here: 74.2 us
  starting transfers between devices  43.3 us (58%)
  waiting for transfers between devices  22.4 us (30%)
  other arithmetic  3.77 us (5%)
  matrix products  3.28 us (4%)
  between operations  1.11 us (1%)
    ppermute x12, starting transfers between devices, exchange(): return lax.ppermute(x, ('batch', axis), pairs)  34.7 us
    ppermute x12, waiting for transfers between devices, exchange(): return lax.ppermute(x, ('batch', axis), pairs)  11.6 us
    ppermute x7, starting transfers between devices, move(): return lax.ppermute(x, 'batch', pairs)  8.22 us
    ppermute x7, waiting for transfers between devices, move(): return lax.ppermute(x, 'batch', pairs)  7.73 us
    ppermute x4, waiting for transfers between devices, swap(): lax.ppermute(x, 'batch', [(i, i ^ bit) for i in range(lax.axis_size('batc...  3.08 us
    dot_general x2, matrix products, gram_of(): gram = jnp.dot(blocks, rounded.T, preferred_element_type=F32)  1.67 us
  transfers between devices with their start and end apart: 23, of which 14 were waited for; matrix products, arithmetic and copies ran while one was open for 5% of the time, Pallas kernels for 0%

profile of v2, /device:TPU:38, one launch (start us, length us, event | category | flops | bytes accessed | tf_op | source)
XLA Modules:
  0.0 74.2 jit_solution(15612265623627202725)
XLA Ops:
  0.7 1.0 %constant_dynamic-update-slice_fusion.9 = (bf16[2048,512]{1,0:T(8,128)(2,1)S(1)}, bf16[128,512]{1,0:T(8,128)(2,1)S(1)}, bf16[128,512]{1,0:T(8,128)(2,1)S(1)}) fusion(bf16[128,512]{1,0:T(8,128)(2,1)} %param.2, bf16[128,512]{1,0:T(8,128)(2,1)} %param.3, pred[]{:T(512)S(6)} %eq.29), kind=kLoop, calls=%fused_computation.84 | loop fusion | flops 131071 | bytes 655361
  1.7 0.2 collective-permute-start.1
  1.9 0.8 %collective-permute-start.3 = (bf16[128,512]{1,0:T(8,128)(2,1)S(1)}, bf16[128,512]{1,0:T(8,128)(2,1)S(1)}, u32[]{:S(2)}, u32[]{:S(2)}) collective-permute-start(bf16[128,512]{1,0:T(8,128)(2,1)S(1)} %get-tuple-element.13), channel_id=1, source_target_pairs={{0,192},{16,208},{32,224},{48,240},{64,0},{80,16},{96,32},{112,48}... | collective-permute-start | bytes 393224 | tf_op jit(solution)/shard_map/ppermute | solution.py:38
  2.7 2.4 %collective-permute-start = (bf16[128,512]{1,0:T(8,128)(2,1)S(1)}, bf16[128,512]{1,0:T(8,128)(2,1)S(1)}, u32[]{:S(2)}, u32[]{:S(2)}) collective-permute-start(bf16[128,512]{1,0:T(8,128)(2,1)S(1)} %get-tuple-element.13), channel_id=1, source_target_pairs={{0,64},{16,80},{32,96},{48,112},{64,128},{80,144},{96,160},{112,17... | collective-permute-start | bytes 393224 | tf_op jit(solution)/shard_map/ppermute | solution.py:38
  5.1 1.5 %collective-permute-start.6 = (bf16[128,512]{1,0:T(8,128)(2,1)S(1)}, bf16[128,512]{1,0:T(8,128)(2,1)S(1)}, u32[]{:S(2)}, u32[]{:S(2)}) collective-permute-start(bf16[128,512]{1,0:T(8,128)(2,1)S(1)} %get-tuple-element.22), channel_id=1, source_target_pairs={{0,160},{16,176},{32,128},{48,144},{64,224},{80,240},{96,192},{112... | collective-permute-start | bytes 393224 | tf_op jit(solution)/shard_map/ppermute | solution.py:38
  6.7 0.4 collective-permute-done.1
  7.1 1.0 %collective-permute-start.4 = (bf16[128,512]{1,0:T(8,128)(2,1)S(1)}, bf16[128,512]{1,0:T(8,128)(2,1)S(1)}, u32[]{:S(2)}, u32[]{:S(2)}) collective-permute-start(bf16[128,512]{1,0:T(8,128)(2,1)S(1)} %collective-permute-done.1), channel_id=1, source_target_pairs={{0,192},{16,208},{32,224},{48,240},{64,0},{80,16},{96,32},{112,48}... | collective-permute-start | bytes 393224 | tf_op jit(solution)/shard_map/ppermute | solution.py:38
  8.1 2.2 %collective-permute-start.2 = (bf16[128,512]{1,0:T(8,128)(2,1)S(1)}, bf16[128,512]{1,0:T(8,128)(2,1)S(1)}, u32[]{:S(2)}, u32[]{:S(2)}) collective-permute-start(bf16[128,512]{1,0:T(8,128)(2,1)S(1)} %collective-permute-done.1), channel_id=1, source_target_pairs={{0,64},{16,80},{32,96},{48,112},{64,128},{80,144},{96,160},{112,17... | collective-permute-start | bytes 393224 | tf_op jit(solution)/shard_map/ppermute | solution.py:38
  10.3 0.3 collective-permute-done
  10.6 2.8 %collective-permute-done.2 = bf16[128,512]{1,0:T(8,128)(2,1)S(1)} collective-permute-done((bf16[128,512]{1,0:T(8,128)(2,1)S(1)}, bf16[128,512]{1,0:T(8,128)(2,1)S(1)}, u32[]{:S(2)}, u32[]{:S(2)}) %collective-permute-start.2) | collective-permute-done | bytes 131104 | tf_op jit(solution)/shard_map/ppermute | solution.py:38
  13.5 0.1 collective-permute-start.7
  13.6 1.8 %collective-permute-done.4 = bf16[128,512]{1,0:T(8,128)(2,1)S(1)} collective-permute-done((bf16[128,512]{1,0:T(8,128)(2,1)S(1)}, bf16[128,512]{1,0:T(8,128)(2,1)S(1)}, u32[]{:S(2)}, u32[]{:S(2)}) %collective-permute-start.4) | collective-permute-done | bytes 131104 | tf_op jit(solution)/shard_map/ppermute | solution.py:38
  15.4 2.4 %collective-permute-done.5 = bf16[128,512]{1,0:T(8,128)(2,1)S(1)} collective-permute-done((bf16[128,512]{1,0:T(8,128)(2,1)S(1)}, bf16[128,512]{1,0:T(8,128)(2,1)S(1)}, u32[]{:S(2)}, u32[]{:S(2)}) %collective-permute-start.5) | collective-permute-done | bytes 131104 | tf_op jit(solution)/shard_map/ppermute | solution.py:38
  17.9 0.1 collective-permute-start.8
  18.1 1.7 %collective-permute-done.8 = bf16[512,512]{1,0:T(8,128)(2,1)S(1)} collective-permute-done((bf16[512,512]{1,0:T(8,128)(2,1)S(1)}, bf16[512,512]{1,0:T(8,128)(2,1)S(1)}, u32[]{:S(2)}, u32[]{:S(2)}) %collective-permute-start.8) | collective-permute-done | bytes 524320 | tf_op jit(solution)/shard_map/ppermute | solution.py:16
  19.9 0.3 convert_reduce_fusion
  20.4 0.8 %fusion.12 = f32[128,2048]{1,0:T(8,128)S(1)} fusion(bf16[128,512]{1,0:T(8,128)(2,1)S(1)} %bitcast.81, bf16[2048,512]{1,0:T(8,128)(2,1)S(1)} %constant_dynamic-update-slice_fusion, f32[512]{0:T(512)S(1)} %broadcast_multiply_fusion), kind=kOutput, calls=%fused_computation.15 | convolution fusion | flops 271581184 | bytes 3278848 | tf_op jit(solution)/shard_map/dot_general | solution.py:96
  21.3 1.7 %collective-permute-start.15 = (bf16[2,32,2048]{2,1,0:T(8,128)(2,1)S(1)}, bf16[2,32,2048]{2,1,0:T(8,128)(2,1)S(1)}, u32[]{:S(2)}, u32[]{:S(2)}) collective-permute-start(bf16[2,32,2048]{2,1,0:T(8,128)(2,1)S(1)} %bitcast.77), channel_id=1, source_target_pairs={{0,1},{1,0},{2,3},{3,2},{16,19},{17,18},{18,17},{19,16},{32,33},{3... | collective-permute-start | bytes 786440 | tf_op jit(solution)/shard_map/ppermute | solution.py:30
  23.0 0.8 %fusion.10 = f32[128,2048]{1,0:T(8,128)S(1)} fusion(bf16[128,512]{1,0:T(8,128)(2,1)S(1)} %bitcast.80, bf16[2048,512]{1,0:T(8,128)(2,1)S(1)} %constant_dynamic-update-slice_fusion, f32[512]{0:T(512)S(1)} %broadcast_multiply_fusion), kind=kOutput, calls=%fused_computation.14 | convolution fusion | flops 271581184 | bytes 3278848 | tf_op jit(solution)/shard_map/dot_general | solution.py:96
  23.9 0.5 collective-permute-start.9
  24.5 0.6 multiply_reduce_fusion.1
  25.1 0.1 multiply_add_fusion
  25.3 2.5 %collective-permute-done.15 = bf16[2,32,2048]{2,1,0:T(8,128)(2,1)S(1)} collective-permute-done((bf16[2,32,2048]{2,1,0:T(8,128)(2,1)S(1)}, bf16[2,32,2048]{2,1,0:T(8,128)(2,1)S(1)}, u32[]{:S(2)}, u32[]{:S(2)}) %collective-permute-start.15) | collective-permute-done | bytes 262176 | tf_op jit(solution)/shard_map/ppermute | solution.py:30
  27.9 3.1 %collective-permute-start.16 = (bf16[32,2048]{1,0:T(8,128)(2,1)S(1)}, bf16[32,2048]{1,0:T(8,128)(2,1)S(1)}, u32[]{:S(2)}, u32[]{:S(2)}) collective-permute-start(bf16[32,2048]{1,0:T(8,128)(2,1)S(1)} %fusion.25), channel_id=1, source_target_pairs={{0,3},{1,2},{2,1},{3,0},{16,17},{17,16},{18,19},{19,18},{32,35},{3... | collective-permute-start | bytes 393224 | tf_op jit(solution)/shard_map/ppermute | solution.py:30
  31.1 2.7 %collective-permute-start.10 = (bf16[32,2048]{1,0:T(8,128)(2,1)S(1)}, bf16[32,2048]{1,0:T(8,128)(2,1)S(1)}, u32[]{:S(2)}, u32[]{:S(2)}) collective-permute-start(bf16[32,2048]{1,0:T(8,128)(2,1)S(1)} %fusion.24), channel_id=1, source_target_pairs={{0,3},{1,2},{2,1},{3,0},{16,17},{17,16},{18,19},{19,18},{32,35},{3... | collective-permute-start | bytes 393224 | tf_op jit(solution)/shard_map/ppermute | solution.py:30
  33.8 0.3 collective-permute-done.16
  34.2 3.4 %collective-permute-start.17 = (bf16[32,2048]{1,0:T(8,128)(2,1)S(1)}, bf16[32,2048]{1,0:T(8,128)(2,1)S(1)}, u32[]{:S(2)}, u32[]{:S(2)}) collective-permute-start(bf16[32,2048]{1,0:T(8,128)(2,1)S(1)} %fusion.28), channel_id=1, source_target_pairs={{0,4},{4,0},{8,12},{12,8},{16,28},{20,24},{24,20},{28,16},{32,36},... | collective-permute-start | bytes 393224 | tf_op jit(solution)/shard_map/ppermute | solution.py:30
  37.6 3.3 %collective-permute-start.11 = (bf16[32,2048]{1,0:T(8,128)(2,1)S(1)}, bf16[32,2048]{1,0:T(8,128)(2,1)S(1)}, u32[]{:S(2)}, u32[]{:S(2)}) collective-permute-start(bf16[32,2048]{1,0:T(8,128)(2,1)S(1)} %fusion.27), channel_id=1, source_target_pairs={{0,4},{4,0},{8,12},{12,8},{16,28},{20,24},{24,20},{28,16},{32,36},... | collective-permute-start | bytes 393224 | tf_op jit(solution)/shard_map/ppermute | solution.py:30
  40.9 0.2 collective-permute-done.17
  41.2 5.4 %collective-permute-start.18 = (bf16[32,2048]{1,0:T(8,128)(2,1)S(1)}, bf16[32,2048]{1,0:T(8,128)(2,1)S(1)}, u32[]{:S(2)}, u32[]{:S(2)}) collective-permute-start(bf16[32,2048]{1,0:T(8,128)(2,1)S(1)} %fusion.23), channel_id=1, source_target_pairs={{0,12},{4,8},{8,4},{12,0},{16,20},{20,16},{24,28},{28,24},{32,44},... | collective-permute-start | bytes 393224 | tf_op jit(solution)/shard_map/ppermute | solution.py:30
  46.6 0.6 collective-permute-done.11
  47.2 6.3 %collective-permute-start.12 = (bf16[32,2048]{1,0:T(8,128)(2,1)S(1)}, bf16[32,2048]{1,0:T(8,128)(2,1)S(1)}, u32[]{:S(2)}, u32[]{:S(2)}) collective-permute-start(bf16[32,2048]{1,0:T(8,128)(2,1)S(1)} %fusion.22), channel_id=1, source_target_pairs={{0,12},{4,8},{8,4},{12,0},{16,20},{20,16},{24,28},{28,24},{32,44},... | collective-permute-start | bytes 393224 | tf_op jit(solution)/shard_map/ppermute | solution.py:30
  53.5 0.1 add_convert_fusion
  53.6 4.5 %collective-permute-start.19 = (bf16[32,2048]{1,0:T(8,128)(2,1)S(1)}, bf16[32,2048]{1,0:T(8,128)(2,1)S(1)}, u32[]{:S(2)}, u32[]{:S(2)}) collective-permute-start(bf16[32,2048]{1,0:T(8,128)(2,1)S(1)} %add_convert_fusion), channel_id=1, source_target_pairs={{0,3},{1,2},{2,1},{3,0},{16,19},{17,18},{18,17},{19,16},{32,35},{3... | collective-permute-start | bytes 393224 | tf_op jit(solution)/shard_map/ppermute | solution.py:30
  58.1 0.1 add_convert_fusion.1
  58.2 3.6 %collective-permute-start.13 = (bf16[32,2048]{1,0:T(8,128)(2,1)S(1)}, bf16[32,2048]{1,0:T(8,128)(2,1)S(1)}, u32[]{:S(2)}, u32[]{:S(2)}) collective-permute-start(bf16[32,2048]{1,0:T(8,128)(2,1)S(1)} %add_convert_fusion.1), channel_id=1, source_target_pairs={{0,3},{1,2},{2,1},{3,0},{16,19},{17,18},{18,17},{19,16},{32,35},{3... | collective-permute-start | bytes 393224 | tf_op jit(solution)/shard_map/ppermute | solution.py:30
  61.8 0.1 collective-permute-start.20
  61.9 0.5 fusion.5
  62.5 0.1 collective-permute-start.21
  62.6 2.2 %collective-permute-done.13 = bf16[32,2048]{1,0:T(8,128)(2,1)S(1)} collective-permute-done((bf16[32,2048]{1,0:T(8,128)(2,1)S(1)}, bf16[32,2048]{1,0:T(8,128)(2,1)S(1)}, u32[]{:S(2)}, u32[]{:S(2)}) %collective-permute-start.13) | collective-permute-done | bytes 131104 | tf_op jit(solution)/shard_map/ppermute | solution.py:30
  64.8 0.1 collective-permute-start.14
  64.9 3.4 %collective-permute-done.20 = bf16[64,2048]{1,0:T(8,128)(2,1)S(1)} collective-permute-done((bf16[64,2048]{1,0:T(8,128)(2,1)S(1)}, bf16[64,2048]{1,0:T(8,128)(2,1)S(1)}, u32[]{:S(2)}, u32[]{:S(2)}) %collective-permute-start.20) | collective-permute-done | bytes 262176 | tf_op jit(solution)/shard_map/ppermute | solution.py:30
  68.3 0.5 fusion.4
  68.8 0.1 collective-permute-start.22
  68.9 2.3 %collective-permute-done.14 = bf16[64,2048]{1,0:T(8,128)(2,1)S(1)} collective-permute-done((bf16[64,2048]{1,0:T(8,128)(2,1)S(1)}, bf16[64,2048]{1,0:T(8,128)(2,1)S(1)}, u32[]{:S(2)}, u32[]{:S(2)}) %collective-permute-start.14) | collective-permute-done | bytes 262176 | tf_op jit(solution)/shard_map/ppermute | solution.py:30
  71.3 0.5 fusion.7
  71.8 1.3 %collective-permute-done.22 = bf16[64,512]{1,0:T(8,128)(2,1)S(1)} collective-permute-done((bf16[64,512]{1,0:T(8,128)(2,1)S(1)}, bf16[64,512]{1,0:T(8,128)(2,1)S(1)}, u32[]{:S(2)}, u32[]{:S(2)}) %collective-permute-start.22) | collective-permute-done | bytes 65568 | tf_op jit(solution)/shard_map/ppermute | solution.py:16
  73.3 0.8 %select_convert_fusion = (bf16[128,512]{1,0:T(8,128)(2,1)}, bf16[128,512]{1,0:T(8,128)(2,1)}) fusion(pred[]{:T(512)S(6)} %eq.29, bf16[128,512]{1,0:T(8,128)(2,1)S(1)} %get-tuple-element.22, bf16[128,512]{1,0:T(8,128)(2,1)S(1)} %get-tuple-element.13, f32[2,2,32,512]{3,2,1,0:T(8,128)S(1)} %reverse_select_fusion, f32[512]{0:T(512)S(1)} %fusion.29, ...), kind=kLoop, calls=%fused_computation.47 | loop fusion | flops 1179648 | bytes 1054721 | tf_op jit(solution)/shard_map/convert_element_type | solution.py:142
  (59 shorter events, 1.1 us)
Async XLA Ops:
  1.7 5.4 %collective-permute-start.1 = (bf16[128,512]{1,0:T(8,128)(2,1)S(1)}, bf16[128,512]{1,0:T(8,128)(2,1)S(1)}, u32[]{:S(2)}, u32[]{:S(2)}) collective-permute-start(bf16[128,512]{1,0:T(8,128)(2,1)S(1)} %get-tuple-element.22), channel_id=1, source_target_pairs={{0,32},{16,48},{32,0},{48,16},{64,96},{80,112},{96,64},{112,80},{1... | collective-permute-start | bytes 393224 | tf_op jit(solution)/shard_map/ppermute | solution.py:38
  1.9 8.4 %collective-permute-start.3 = (bf16[128,512]{1,0:T(8,128)(2,1)S(1)}, bf16[128,512]{1,0:T(8,128)(2,1)S(1)}, u32[]{:S(2)}, u32[]{:S(2)}) collective-permute-start(bf16[128,512]{1,0:T(8,128)(2,1)S(1)} %get-tuple-element.13), channel_id=1, source_target_pairs={{0,192},{16,208},{32,224},{48,240},{64,0},{80,16},{96,32},{112,48}... | collective-permute-start | bytes 393224 | tf_op jit(solution)/shard_map/ppermute | solution.py:38
  2.7 7.9 %collective-permute-start = (bf16[128,512]{1,0:T(8,128)(2,1)S(1)}, bf16[128,512]{1,0:T(8,128)(2,1)S(1)}, u32[]{:S(2)}, u32[]{:S(2)}) collective-permute-start(bf16[128,512]{1,0:T(8,128)(2,1)S(1)} %get-tuple-element.13), channel_id=1, source_target_pairs={{0,64},{16,80},{32,96},{48,112},{64,128},{80,144},{96,160},{112,17... | collective-permute-start | bytes 393224 | tf_op jit(solution)/shard_map/ppermute | solution.py:38
  5.1 8.5 %collective-permute-start.6 = (bf16[128,512]{1,0:T(8,128)(2,1)S(1)}, bf16[128,512]{1,0:T(8,128)(2,1)S(1)}, u32[]{:S(2)}, u32[]{:S(2)}) collective-permute-start(bf16[128,512]{1,0:T(8,128)(2,1)S(1)} %get-tuple-element.22), channel_id=1, source_target_pairs={{0,160},{16,176},{32,128},{48,144},{64,224},{80,240},{96,192},{112... | collective-permute-start | bytes 393224 | tf_op jit(solution)/shard_map/ppermute | solution.py:38
  7.1 8.4 %collective-permute-start.4 = (bf16[128,512]{1,0:T(8,128)(2,1)S(1)}, bf16[128,512]{1,0:T(8,128)(2,1)S(1)}, u32[]{:S(2)}, u32[]{:S(2)}) collective-permute-start(bf16[128,512]{1,0:T(8,128)(2,1)S(1)} %collective-permute-done.1), channel_id=1, source_target_pairs={{0,192},{16,208},{32,224},{48,240},{64,0},{80,16},{96,32},{112,48}... | collective-permute-start | bytes 393224 | tf_op jit(solution)/shard_map/ppermute | solution.py:38
  8.1 5.4 %collective-permute-start.2 = (bf16[128,512]{1,0:T(8,128)(2,1)S(1)}, bf16[128,512]{1,0:T(8,128)(2,1)S(1)}, u32[]{:S(2)}, u32[]{:S(2)}) collective-permute-start(bf16[128,512]{1,0:T(8,128)(2,1)S(1)} %collective-permute-done.1), channel_id=1, source_target_pairs={{0,64},{16,80},{32,96},{48,112},{64,128},{80,144},{96,160},{112,17... | collective-permute-start | bytes 393224 | tf_op jit(solution)/shard_map/ppermute | solution.py:38
  10.3 7.5 %collective-permute-start.5 = (bf16[128,512]{1,0:T(8,128)(2,1)S(1)}, bf16[128,512]{1,0:T(8,128)(2,1)S(1)}, u32[]{:S(2)}, u32[]{:S(2)}) collective-permute-start(bf16[128,512]{1,0:T(8,128)(2,1)S(1)} %collective-permute-done.3), channel_id=1, source_target_pairs={{0,192},{16,208},{32,224},{48,240},{64,0},{80,16},{96,32},{112,48}... | collective-permute-start | bytes 393224 | tf_op jit(solution)/shard_map/ppermute | solution.py:38
  13.5 4.5 %collective-permute-start.7 = (bf16[512,512]{1,0:T(8,128)(2,1)S(1)}, bf16[512,512]{1,0:T(8,128)(2,1)S(1)}, u32[]{:S(2)}, u32[]{:S(2)}) collective-permute-start(bf16[512,512]{1,0:T(8,128)(2,1)S(1)} %pad_maximum_fusion), channel_id=1, source_target_pairs={{0,16},{16,0},{32,48},{48,32},{64,80},{80,64},{96,112},{112,96},{1... | collective-permute-start | bytes 1572872 | tf_op jit(solution)/shard_map/ppermute | solution.py:16
  17.9 2.0 %collective-permute-start.8 = (bf16[512,512]{1,0:T(8,128)(2,1)S(1)}, bf16[512,512]{1,0:T(8,128)(2,1)S(1)}, u32[]{:S(2)}, u32[]{:S(2)}) collective-permute-start(bf16[512,512]{1,0:T(8,128)(2,1)S(1)} %pad_maximum_fusion.1), channel_id=1, source_target_pairs={{0,16},{16,0},{32,48},{48,32},{64,80},{80,64},{96,112},{112,96},{1... | collective-permute-start | bytes 1572872 | tf_op jit(solution)/shard_map/ppermute | solution.py:16
  21.2 2.6 %copy-start = (f32[128,2048]{1,0:T(8,128)}, f32[128,2048]{1,0:T(8,128)S(1)}, u32[]{:S(2)}) copy-start(f32[128,2048]{1,0:T(8,128)S(1)} %fusion.12) | copy-start | bytes 3145732
  21.3 6.5 %collective-permute-start.15 = (bf16[2,32,2048]{2,1,0:T(8,128)(2,1)S(1)}, bf16[2,32,2048]{2,1,0:T(8,128)(2,1)S(1)}, u32[]{:S(2)}, u32[]{:S(2)}) collective-permute-start(bf16[2,32,2048]{2,1,0:T(8,128)(2,1)S(1)} %bitcast.77), channel_id=1, source_target_pairs={{0,1},{1,0},{2,3},{3,2},{16,19},{17,18},{18,17},{19,16},{32,33},{3... | collective-permute-start | bytes 786440 | tf_op jit(solution)/shard_map/ppermute | solution.py:30
  23.9 1.3 %copy-start.1 = (f32[128,2048]{1,0:T(8,128)}, f32[128,2048]{1,0:T(8,128)S(1)}, u32[]{:S(2)}) copy-start(f32[128,2048]{1,0:T(8,128)S(1)} %fusion.10) | copy-start | bytes 3145732
  23.9 3.9 %slice-start = ((f32[128,2048]{1,0:T(8,128)}), f32[64,2048]{1,0:T(8,128)S(1)}, s32[]{:S(2)}) async-start(f32[128,2048]{1,0:T(8,128)} %copy-done), calls=%async_computation | async-start | bytes 1048576 | tf_op jit(solution)/shard_map/slice | solution.py:42
  23.9 7.1 %collective-permute-start.9 = (bf16[2,32,2048]{2,1,0:T(8,128)(2,1)S(1)}, bf16[2,32,2048]{2,1,0:T(8,128)(2,1)S(1)}, u32[]{:S(2)}, u32[]{:S(2)}) collective-permute-start(bf16[2,32,2048]{2,1,0:T(8,128)(2,1)S(1)} %bitcast.78), channel_id=1, source_target_pairs={{0,1},{1,0},{2,3},{3,2},{16,19},{17,18},{18,17},{19,16},{32,33},{3... | collective-permute-start | bytes 786440 | tf_op jit(solution)/shard_map/ppermute | solution.py:30
  25.2 5.8 %slice-start.1 = ((f32[128,2048]{1,0:T(8,128)}), f32[64,2048]{1,0:T(8,128)S(1)}, s32[]{:S(2)}) async-start(f32[128,2048]{1,0:T(8,128)} %copy-done.1), calls=%async_computation.1 | async-start | bytes 1048576 | tf_op jit(solution)/shard_map/slice | solution.py:42
  27.9 6.3 %collective-permute-start.16 = (bf16[32,2048]{1,0:T(8,128)(2,1)S(1)}, bf16[32,2048]{1,0:T(8,128)(2,1)S(1)}, u32[]{:S(2)}, u32[]{:S(2)}) collective-permute-start(bf16[32,2048]{1,0:T(8,128)(2,1)S(1)} %fusion.25), channel_id=1, source_target_pairs={{0,3},{1,2},{2,1},{3,0},{16,17},{17,16},{18,19},{19,18},{32,35},{3... | collective-permute-start | bytes 393224 | tf_op jit(solution)/shard_map/ppermute | solution.py:30
  31.1 6.5 %collective-permute-start.10 = (bf16[32,2048]{1,0:T(8,128)(2,1)S(1)}, bf16[32,2048]{1,0:T(8,128)(2,1)S(1)}, u32[]{:S(2)}, u32[]{:S(2)}) collective-permute-start(bf16[32,2048]{1,0:T(8,128)(2,1)S(1)} %fusion.24), channel_id=1, source_target_pairs={{0,3},{1,2},{2,1},{3,0},{16,17},{17,16},{18,19},{19,18},{32,35},{3... | collective-permute-start | bytes 393224 | tf_op jit(solution)/shard_map/ppermute | solution.py:30
  34.2 7.0 %collective-permute-start.17 = (bf16[32,2048]{1,0:T(8,128)(2,1)S(1)}, bf16[32,2048]{1,0:T(8,128)(2,1)S(1)}, u32[]{:S(2)}, u32[]{:S(2)}) collective-permute-start(bf16[32,2048]{1,0:T(8,128)(2,1)S(1)} %fusion.28), channel_id=1, source_target_pairs={{0,4},{4,0},{8,12},{12,8},{16,28},{20,24},{24,20},{28,16},{32,36},... | collective-permute-start | bytes 393224 | tf_op jit(solution)/shard_map/ppermute | solution.py:30
  37.6 9.6 %collective-permute-start.11 = (bf16[32,2048]{1,0:T(8,128)(2,1)S(1)}, bf16[32,2048]{1,0:T(8,128)(2,1)S(1)}, u32[]{:S(2)}, u32[]{:S(2)}) collective-permute-start(bf16[32,2048]{1,0:T(8,128)(2,1)S(1)} %fusion.27), channel_id=1, source_target_pairs={{0,4},{4,0},{8,12},{12,8},{16,28},{20,24},{24,20},{28,16},{32,36},... | collective-permute-start | bytes 393224 | tf_op jit(solution)/shard_map/ppermute | solution.py:30
  41.2 12.3 %collective-permute-start.18 = (bf16[32,2048]{1,0:T(8,128)(2,1)S(1)}, bf16[32,2048]{1,0:T(8,128)(2,1)S(1)}, u32[]{:S(2)}, u32[]{:S(2)}) collective-permute-start(bf16[32,2048]{1,0:T(8,128)(2,1)S(1)} %fusion.23), channel_id=1, source_target_pairs={{0,12},{4,8},{8,4},{12,0},{16,20},{20,16},{24,28},{28,24},{32,44},... | collective-permute-start | bytes 393224 | tf_op jit(solution)/shard_map/ppermute | solution.py:30
  47.2 10.9 %collective-permute-start.12 = (bf16[32,2048]{1,0:T(8,128)(2,1)S(1)}, bf16[32,2048]{1,0:T(8,128)(2,1)S(1)}, u32[]{:S(2)}, u32[]{:S(2)}) collective-permute-start(bf16[32,2048]{1,0:T(8,128)(2,1)S(1)} %fusion.22), channel_id=1, source_target_pairs={{0,12},{4,8},{8,4},{12,0},{16,20},{20,16},{24,28},{28,24},{32,44},... | collective-permute-start | bytes 393224 | tf_op jit(solution)/shard_map/ppermute | solution.py:30
  53.6 8.2 %collective-permute-start.19 = (bf16[32,2048]{1,0:T(8,128)(2,1)S(1)}, bf16[32,2048]{1,0:T(8,128)(2,1)S(1)}, u32[]{:S(2)}, u32[]{:S(2)}) collective-permute-start(bf16[32,2048]{1,0:T(8,128)(2,1)S(1)} %add_convert_fusion), channel_id=1, source_target_pairs={{0,3},{1,2},{2,1},{3,0},{16,19},{17,18},{18,17},{19,16},{32,35},{3... | collective-permute-start | bytes 393224 | tf_op jit(solution)/shard_map/ppermute | solution.py:30
  58.2 6.6 %collective-permute-start.13 = (bf16[32,2048]{1,0:T(8,128)(2,1)S(1)}, bf16[32,2048]{1,0:T(8,128)(2,1)S(1)}, u32[]{:S(2)}, u32[]{:S(2)}) collective-permute-start(bf16[32,2048]{1,0:T(8,128)(2,1)S(1)} %add_convert_fusion.1), channel_id=1, source_target_pairs={{0,3},{1,2},{2,1},{3,0},{16,19},{17,18},{18,17},{19,16},{32,35},{3... | collective-permute-start | bytes 393224 | tf_op jit(solution)/shard_map/ppermute | solution.py:30
  61.8 6.5 %collective-permute-start.20 = (bf16[64,2048]{1,0:T(8,128)(2,1)S(1)}, bf16[64,2048]{1,0:T(8,128)(2,1)S(1)}, u32[]{:S(2)}, u32[]{:S(2)}) collective-permute-start(bf16[64,2048]{1,0:T(8,128)(2,1)S(1)} %pad_maximum_fusion.4), channel_id=1, source_target_pairs={{0,1},{1,0},{2,3},{3,2},{16,17},{17,16},{18,19},{19,18},{32,33},{3... | collective-permute-start | bytes 786440 | tf_op jit(solution)/shard_map/ppermute | solution.py:30
  62.5 9.4 %collective-permute-start.21 = (bf16[64,512]{1,0:T(8,128)(2,1)S(1)}, bf16[64,512]{1,0:T(8,128)(2,1)S(1)}, u32[]{:S(2)}, u32[]{:S(2)}) collective-permute-start(bf16[64,512]{1,0:T(8,128)(2,1)S(1)} %fusion.5), channel_id=1, source_target_pairs={{0,32},{16,48},{32,0},{48,16},{64,96},{80,112},{96,64},{112,80},{1... | collective-permute-start | bytes 196616 | tf_op jit(solution)/shard_map/ppermute | solution.py:16
  64.8 6.5 %collective-permute-start.14 = (bf16[64,2048]{1,0:T(8,128)(2,1)S(1)}, bf16[64,2048]{1,0:T(8,128)(2,1)S(1)}, u32[]{:S(2)}, u32[]{:S(2)}) collective-permute-start(bf16[64,2048]{1,0:T(8,128)(2,1)S(1)} %pad_maximum_fusion.3), channel_id=1, source_target_pairs={{0,1},{1,0},{2,3},{3,2},{16,17},{17,16},{18,19},{19,18},{32,33},{3... | collective-permute-start | bytes 786440 | tf_op jit(solution)/shard_map/ppermute | solution.py:30
  68.8 4.4 %collective-permute-start.22 = (bf16[64,512]{1,0:T(8,128)(2,1)S(1)}, bf16[64,512]{1,0:T(8,128)(2,1)S(1)}, u32[]{:S(2)}, u32[]{:S(2)}) collective-permute-start(bf16[64,512]{1,0:T(8,128)(2,1)S(1)} %fusion.4), channel_id=1, source_target_pairs={{0,32},{16,48},{32,0},{48,16},{64,96},{80,112},{96,64},{112,80},{1... | collective-permute-start | bytes 196616 | tf_op jit(solution)/shard_map/ppermute | solution.py:16

commit v3 on v2

--- a/solution.py
+++ b/solution.py
@@ -43,8 +43,8 @@
     return keep[0] + exchange(keep[1].astype(BF), axis, 1).astype(F32)
 
 
-def gather_pair(x, axis):
-    return jnp.concatenate([x, exchange(x, axis, 1, same=True)], axis=0)
+def gather_pair(x, axis, same):
+    return jnp.concatenate([x, exchange(x, axis, 1, same=same)], axis=0)
 
 
 def full_sum(x, axis):
@@ -78,8 +78,9 @@
     mine = jnp.where(first, view_one, view_two)
     away, away_far = move(other, 0, flip=1), move(other, 2, flip=1)
     low, high = move(mine, 1), move(mine, -1)
+    onward = move(jnp.concatenate([away, high], axis=0), -1)
     near = jnp.concatenate([mine, low, away, move(away, 1)], axis=0)
-    rest = jnp.concatenate([high, move(away, -1), move(high, -1), away_far], axis=0)
+    rest = jnp.concatenate([high, onward, away_far], axis=0)
     full = jnp.concatenate([near, rest, swap(near, 1), swap(rest, 1)], axis=0)
     mean_val = jnp.sum(full.astype(F32), axis=0, keepdims=True) / sample_count
     rounded = (full.astype(F32) - mean_val).astype(BF)
@@ -102,9 +103,9 @@
         own = own_cent.astype(BF)
         return own.astype(F32) * feature_squares * coef_cov + coef_var * hinge * own_cent
 
-    def pair_of(parts, send):
+    def pair_of(parts, send, same):
         total = full_sum(scatter_sum(parts, "col", send), "row").astype(BF)
-        return gather_pair(total, "col")
+        return gather_pair(total, "col", same)
 
     def away_part(rows, term):
         return (coef_cov * jnp.dot(rows, rounded, preferred_element_type=F32) - term).astype(BF)
@@ -122,18 +123,18 @@
     term_away, term_mine = term_of(away_late), term_of(mine_late)
     term_away = ordered(term_away.reshape(4, quarter, width), "col", True)
     term_away = term_away.reshape(2, 2 * quarter, width)
-    pair_away = pair_of(parts_away, send_away)
+    pair_away = pair_of(parts_away, send_away, True)
     wide_away = exchange(pair_away, "col", 0, same=True)
     early = away_part(pair_away, term_away[0])
     late = away_part(wide_away, term_away[1])
     extra_other = jnp.concatenate([swap(early, 2), swap(late, 2)], axis=0)
     extra_other = extra_other.astype(F32).reshape(4, quarter, width)
     extra_other = ordered(extra_other, "col", True, back=True).reshape(local_rows, width)
-    pair_mine = pair_of(parts_mine, send_mine)
-    wide_mine = exchange(pair_mine, "col", 0, same=True)
+    pair_mine = pair_of(parts_mine, send_mine, False)
+    wide_mine = exchange(pair_mine, "col", 0)
     whole, _ = lax.optimization_barrier((jnp.concatenate([pair_mine, wide_mine], axis=0), late))
     product = jnp.dot(whole, rounded, preferred_element_type=F32)
-    product = ordered(product.reshape(4, quarter, width), "col", True, back=True)
+    product = ordered(product.reshape(4, quarter, width), "col", core == 0, back=True)
     extra_mine = coef_cov * product.reshape(local_rows, width) - term_mine
     diff = mine.astype(F32) - other.astype(F32)
     grad_mine, grad_other = diff + extra_mine, extra_other - diff

time: 74.3 us -> 75.1 us (1.011)
    ppermute x7 -> x6, waiting for transfers between devices: 7.73 us -> 7.93 us  [move(): return lax.ppermute(x, 'batch', pairs)]
    ppermute x7 -> x6, starting transfers between devices: 8.22 us -> 8.29 us  [move(): return lax.ppermute(x, 'batch', pairs)]
  transfers between devices with their start and end apart: 23 -> 22, of which waited for: 14 -> 13; matrix products, arithmetic and copies ran while one was open for 5% -> 5% of each run, Pallas kernels for 0% -> 0%
where the time goes in v3:
time: 75.1 us; the launch traced here: 74.8 us
  starting transfers between devices  43.8 us (58%)
  waiting for transfers between devices  22.5 us (30%)
  other arithmetic  3.82 us (5%)
  matrix products  3.26 us (4%)
  between operations  1.1 us (1%)
    ppermute x12, starting transfers between devices, exchange(): return lax.ppermute(x, ('batch', axis), pairs)  35.2 us
    ppermute x12, waiting for transfers between devices, exchange(): return lax.ppermute(x, ('batch', axis), pairs)  11.4 us
    ppermute x6, starting transfers between devices, move(): return lax.ppermute(x, 'batch', pairs)  8.29 us
    ppermute x6, waiting for transfers between devices, move(): return lax.ppermute(x, 'batch', pairs)  7.93 us
    ppermute x4, waiting for transfers between devices, swap(): lax.ppermute(x, 'batch', [(i, i ^ bit) for i in range(lax.axis_size('batc...  3.19 us
    dot_general x2, matrix products, gram_of(): gram = jnp.dot(blocks, rounded.T, preferred_element_type=F32)  1.67 us
  transfers between devices with their start and end apart: 22, of which 13 were waited for; matrix products, arithmetic and copies ran while one was open for 5% of the time, Pallas kernels for 0%

profile of v3, /device:TPU:38, one launch (start us, length us, event | category | flops | bytes accessed | tf_op | source)
XLA Modules:
  0.0 74.8 jit_solution(12420119317166677796)
XLA Ops:
  0.7 1.0 %constant_dynamic-update-slice_fusion.8 = (bf16[2048,512]{1,0:T(8,128)(2,1)S(1)}, bf16[128,512]{1,0:T(8,128)(2,1)S(1)}, bf16[128,512]{1,0:T(8,128)(2,1)S(1)}) fusion(bf16[128,512]{1,0:T(8,128)(2,1)} %param.2, bf16[128,512]{1,0:T(8,128)(2,1)} %param.3, pred[]{:T(512)S(6)} %eq.30), kind=kLoop, calls=%fused_computation.85 | loop fusion | flops 131071 | bytes 655361
  1.7 0.2 collective-permute-start.1
  1.9 0.8 %collective-permute-start.3 = (bf16[128,512]{1,0:T(8,128)(2,1)S(1)}, bf16[128,512]{1,0:T(8,128)(2,1)S(1)}, u32[]{:S(2)}, u32[]{:S(2)}) collective-permute-start(bf16[128,512]{1,0:T(8,128)(2,1)S(1)} %get-tuple-element.13), channel_id=1, source_target_pairs={{0,192},{16,208},{32,224},{48,240},{64,0},{80,16},{96,32},{112,48}... | collective-permute-start | bytes 393224 | tf_op jit(solution)/shard_map/ppermute | solution.py:38
  2.7 2.4 %collective-permute-start = (bf16[128,512]{1,0:T(8,128)(2,1)S(1)}, bf16[128,512]{1,0:T(8,128)(2,1)S(1)}, u32[]{:S(2)}, u32[]{:S(2)}) collective-permute-start(bf16[128,512]{1,0:T(8,128)(2,1)S(1)} %get-tuple-element.13), channel_id=1, source_target_pairs={{0,64},{16,80},{32,96},{48,112},{64,128},{80,144},{96,160},{112,17... | collective-permute-start | bytes 393224 | tf_op jit(solution)/shard_map/ppermute | solution.py:38
  5.1 1.5 %collective-permute-start.5 = (bf16[128,512]{1,0:T(8,128)(2,1)S(1)}, bf16[128,512]{1,0:T(8,128)(2,1)S(1)}, u32[]{:S(2)}, u32[]{:S(2)}) collective-permute-start(bf16[128,512]{1,0:T(8,128)(2,1)S(1)} %get-tuple-element.22), channel_id=1, source_target_pairs={{0,160},{16,176},{32,128},{48,144},{64,224},{80,240},{96,192},{112... | collective-permute-start | bytes 393224 | tf_op jit(solution)/shard_map/ppermute | solution.py:38
  6.7 0.4 collective-permute-done.1
  7.1 1.2 %collective-permute-done.3 = bf16[128,512]{1,0:T(8,128)(2,1)S(1)} collective-permute-done((bf16[128,512]{1,0:T(8,128)(2,1)S(1)}, bf16[128,512]{1,0:T(8,128)(2,1)S(1)}, u32[]{:S(2)}, u32[]{:S(2)}) %collective-permute-start.3) | collective-permute-done | bytes 131104 | tf_op jit(solution)/shard_map/ppermute | solution.py:38
  8.3 0.1 collective-permute-start.4
  8.4 3.2 %collective-permute-start.2 = (bf16[128,512]{1,0:T(8,128)(2,1)S(1)}, bf16[128,512]{1,0:T(8,128)(2,1)S(1)}, u32[]{:S(2)}, u32[]{:S(2)}) collective-permute-start(bf16[128,512]{1,0:T(8,128)(2,1)S(1)} %collective-permute-done.1), channel_id=1, source_target_pairs={{0,64},{16,80},{32,96},{48,112},{64,128},{80,144},{96,160},{112,17... | collective-permute-start | bytes 393224 | tf_op jit(solution)/shard_map/ppermute | solution.py:38
  11.7 2.5 %collective-permute-done.2 = bf16[128,512]{1,0:T(8,128)(2,1)S(1)} collective-permute-done((bf16[128,512]{1,0:T(8,128)(2,1)S(1)}, bf16[128,512]{1,0:T(8,128)(2,1)S(1)}, u32[]{:S(2)}, u32[]{:S(2)}) %collective-permute-start.2) | collective-permute-done | bytes 131104 | tf_op jit(solution)/shard_map/ppermute | solution.py:38
  14.2 0.1 collective-permute-start.6
  14.3 3.8 %collective-permute-done.4 = bf16[256,512]{1,0:T(8,128)(2,1)S(1)} collective-permute-done((bf16[256,512]{1,0:T(8,128)(2,1)S(1)}, bf16[256,512]{1,0:T(8,128)(2,1)S(1)}, u32[]{:S(2)}, u32[]{:S(2)}) %collective-permute-start.4) | collective-permute-done | bytes 262176 | tf_op jit(solution)/shard_map/ppermute | solution.py:38
  18.2 0.1 collective-permute-start.7
  18.4 1.8 %collective-permute-done.7 = bf16[512,512]{1,0:T(8,128)(2,1)S(1)} collective-permute-done((bf16[512,512]{1,0:T(8,128)(2,1)S(1)}, bf16[512,512]{1,0:T(8,128)(2,1)S(1)}, u32[]{:S(2)}, u32[]{:S(2)}) %collective-permute-start.7) | collective-permute-done | bytes 524320 | tf_op jit(solution)/shard_map/ppermute | solution.py:16
  20.2 0.3 convert_reduce_fusion
  20.7 0.8 %fusion.12 = f32[128,2048]{1,0:T(8,128)S(1)} fusion(bf16[128,512]{1,0:T(8,128)(2,1)S(1)} %bitcast.81, bf16[2048,512]{1,0:T(8,128)(2,1)S(1)} %constant_dynamic-update-slice_fusion, f32[512]{0:T(512)S(1)} %broadcast_multiply_fusion), kind=kOutput, calls=%fused_computation.15 | convolution fusion | flops 271581184 | bytes 3278848 | tf_op jit(solution)/shard_map/dot_general | solution.py:97
  21.6 1.7 %collective-permute-start.14 = (bf16[2,32,2048]{2,1,0:T(8,128)(2,1)S(1)}, bf16[2,32,2048]{2,1,0:T(8,128)(2,1)S(1)}, u32[]{:S(2)}, u32[]{:S(2)}) collective-permute-start(bf16[2,32,2048]{2,1,0:T(8,128)(2,1)S(1)} %bitcast.78), channel_id=1, source_target_pairs={{0,1},{1,0},{2,3},{3,2},{16,19},{17,18},{18,17},{19,16},{32,33},{3... | collective-permute-start | bytes 786440 | tf_op jit(solution)/shard_map/ppermute | solution.py:30
  23.3 0.8 %fusion.10 = f32[128,2048]{1,0:T(8,128)S(1)} fusion(bf16[128,512]{1,0:T(8,128)(2,1)S(1)} %bitcast.80, bf16[2048,512]{1,0:T(8,128)(2,1)S(1)} %constant_dynamic-update-slice_fusion, f32[512]{0:T(512)S(1)} %broadcast_multiply_fusion), kind=kOutput, calls=%fused_computation.14 | convolution fusion | flops 271581184 | bytes 3278848 | tf_op jit(solution)/shard_map/dot_general | solution.py:97
  24.2 0.5 collective-permute-start.8
  24.7 0.6 multiply_reduce_fusion.1
  25.4 0.1 multiply_add_fusion
  25.5 2.5 %collective-permute-done.14 = bf16[2,32,2048]{2,1,0:T(8,128)(2,1)S(1)} collective-permute-done((bf16[2,32,2048]{2,1,0:T(8,128)(2,1)S(1)}, bf16[2,32,2048]{2,1,0:T(8,128)(2,1)S(1)}, u32[]{:S(2)}, u32[]{:S(2)}) %collective-permute-start.14) | collective-permute-done | bytes 262176 | tf_op jit(solution)/shard_map/ppermute | solution.py:30
  28.2 3.1 %collective-permute-start.15 = (bf16[32,2048]{1,0:T(8,128)(2,1)S(1)}, bf16[32,2048]{1,0:T(8,128)(2,1)S(1)}, u32[]{:S(2)}, u32[]{:S(2)}) collective-permute-start(bf16[32,2048]{1,0:T(8,128)(2,1)S(1)} %fusion.25), channel_id=1, source_target_pairs={{0,3},{1,2},{2,1},{3,0},{16,17},{17,16},{18,19},{19,18},{32,35},{3... | collective-permute-start | bytes 393224 | tf_op jit(solution)/shard_map/ppermute | solution.py:30
  31.3 0.1 convert_add_fusion.1
  31.4 2.7 %collective-permute-start.9 = (bf16[32,2048]{1,0:T(8,128)(2,1)S(1)}, bf16[32,2048]{1,0:T(8,128)(2,1)S(1)}, u32[]{:S(2)}, u32[]{:S(2)}) collective-permute-start(bf16[32,2048]{1,0:T(8,128)(2,1)S(1)} %fusion.24), channel_id=1, source_target_pairs={{0,3},{1,2},{2,1},{3,0},{16,17},{17,16},{18,19},{19,18},{32,35},{3... | collective-permute-start | bytes 393224 | tf_op jit(solution)/shard_map/ppermute | solution.py:30
  34.1 0.3 collective-permute-done.15
  34.5 3.4 %collective-permute-start.16 = (bf16[32,2048]{1,0:T(8,128)(2,1)S(1)}, bf16[32,2048]{1,0:T(8,128)(2,1)S(1)}, u32[]{:S(2)}, u32[]{:S(2)}) collective-permute-start(bf16[32,2048]{1,0:T(8,128)(2,1)S(1)} %fusion.29), channel_id=1, source_target_pairs={{0,4},{4,0},{8,12},{12,8},{16,28},{20,24},{24,20},{28,16},{32,36},... | collective-permute-start | bytes 393224 | tf_op jit(solution)/shard_map/ppermute | solution.py:30
  37.9 3.2 %collective-permute-start.10 = (bf16[32,2048]{1,0:T(8,128)(2,1)S(1)}, bf16[32,2048]{1,0:T(8,128)(2,1)S(1)}, u32[]{:S(2)}, u32[]{:S(2)}) collective-permute-start(bf16[32,2048]{1,0:T(8,128)(2,1)S(1)} %fusion.28), channel_id=1, source_target_pairs={{0,4},{4,0},{8,12},{12,8},{16,28},{20,24},{24,20},{28,16},{32,36},... | collective-permute-start | bytes 393224 | tf_op jit(solution)/shard_map/ppermute | solution.py:30
  41.1 6.9 %collective-permute-start.17 = (bf16[32,2048]{1,0:T(8,128)(2,1)S(1)}, bf16[32,2048]{1,0:T(8,128)(2,1)S(1)}, u32[]{:S(2)}, u32[]{:S(2)}) collective-permute-start(bf16[32,2048]{1,0:T(8,128)(2,1)S(1)} %fusion.23), channel_id=1, source_target_pairs={{0,12},{4,8},{8,4},{12,0},{16,20},{20,16},{24,28},{28,24},{32,44},... | collective-permute-start | bytes 393224 | tf_op jit(solution)/shard_map/ppermute | solution.py:30
  48.0 6.5 %collective-permute-start.11 = (bf16[32,2048]{1,0:T(8,128)(2,1)S(1)}, bf16[32,2048]{1,0:T(8,128)(2,1)S(1)}, u32[]{:S(2)}, u32[]{:S(2)}) collective-permute-start(bf16[32,2048]{1,0:T(8,128)(2,1)S(1)} %fusion.22), channel_id=1, source_target_pairs={{0,12},{4,8},{8,4},{12,0},{16,20},{20,16},{24,28},{28,24},{32,44},... | collective-permute-start | bytes 393224 | tf_op jit(solution)/shard_map/ppermute | solution.py:30
  54.5 0.1 add_convert_fusion
  54.6 3.5 %collective-permute-start.18 = (bf16[32,2048]{1,0:T(8,128)(2,1)S(1)}, bf16[32,2048]{1,0:T(8,128)(2,1)S(1)}, u32[]{:S(2)}, u32[]{:S(2)}) collective-permute-start(bf16[32,2048]{1,0:T(8,128)(2,1)S(1)} %add_convert_fusion), channel_id=1, source_target_pairs={{0,3},{1,2},{2,1},{3,0},{16,19},{17,18},{18,17},{19,16},{32,35},{3... | collective-permute-start | bytes 393224 | tf_op jit(solution)/shard_map/ppermute | solution.py:30
  58.1 0.3 collective-permute-done.11
  58.4 0.1 add_convert_fusion.1
  58.5 3.3 %collective-permute-start.12 = (bf16[32,2048]{1,0:T(8,128)(2,1)S(1)}, bf16[32,2048]{1,0:T(8,128)(2,1)S(1)}, u32[]{:S(2)}, u32[]{:S(2)}) collective-permute-start(bf16[32,2048]{1,0:T(8,128)(2,1)S(1)} %add_convert_fusion.1), channel_id=1, source_target_pairs={{0,3},{1,2},{2,1},{3,0},{16,17},{17,16},{18,19},{19,18},{32,35},{3... | collective-permute-start | bytes 393224 | tf_op jit(solution)/shard_map/ppermute | solution.py:30
  61.8 0.6 collective-permute-done.18
  62.5 0.1 collective-permute-start.19
  62.6 0.5 fusion.5
  63.1 0.1 collective-permute-start.20
  63.2 1.7 %collective-permute-done.12 = bf16[32,2048]{1,0:T(8,128)(2,1)S(1)} collective-permute-done((bf16[32,2048]{1,0:T(8,128)(2,1)S(1)}, bf16[32,2048]{1,0:T(8,128)(2,1)S(1)}, u32[]{:S(2)}, u32[]{:S(2)}) %collective-permute-start.12) | collective-permute-done | bytes 131104 | tf_op jit(solution)/shard_map/ppermute | solution.py:30
  65.0 0.4 collective-permute-start.13
  65.3 3.6 %collective-permute-done.19 = bf16[64,2048]{1,0:T(8,128)(2,1)S(1)} collective-permute-done((bf16[64,2048]{1,0:T(8,128)(2,1)S(1)}, bf16[64,2048]{1,0:T(8,128)(2,1)S(1)}, u32[]{:S(2)}, u32[]{:S(2)}) %collective-permute-start.19) | collective-permute-done | bytes 262176 | tf_op jit(solution)/shard_map/ppermute | solution.py:30
  68.9 0.5 fusion.4
  69.5 0.1 collective-permute-start.21
  69.6 2.2 %collective-permute-done.13 = bf16[64,2048]{1,0:T(8,128)(2,1)S(1)} collective-permute-done((bf16[64,2048]{1,0:T(8,128)(2,1)S(1)}, bf16[64,2048]{1,0:T(8,128)(2,1)S(1)}, u32[]{:S(2)}, u32[]{:S(2)}) %collective-permute-start.13) | collective-permute-done | bytes 262176 | tf_op jit(solution)/shard_map/ppermute | solution.py:30
  71.8 0.5 fusion.7
  72.4 1.4 %collective-permute-done.21 = bf16[64,512]{1,0:T(8,128)(2,1)S(1)} collective-permute-done((bf16[64,512]{1,0:T(8,128)(2,1)S(1)}, bf16[64,512]{1,0:T(8,128)(2,1)S(1)}, u32[]{:S(2)}, u32[]{:S(2)}) %collective-permute-start.21) | collective-permute-done | bytes 65568 | tf_op jit(solution)/shard_map/ppermute | solution.py:16
  74.0 0.8 %select_convert_fusion = (bf16[128,512]{1,0:T(8,128)(2,1)}, bf16[128,512]{1,0:T(8,128)(2,1)}) fusion(pred[]{:T(512)S(6)} %eq.30, bf16[128,512]{1,0:T(8,128)(2,1)S(1)} %get-tuple-element.22, bf16[128,512]{1,0:T(8,128)(2,1)S(1)} %get-tuple-element.13, f32[2,2,32,512]{3,2,1,0:T(8,128)S(1)} %reverse_select_fusion, f32[512]{0:T(512)S(1)} %fusion.30, ...), kind=kLoop, calls=%fused_computation.48 | loop fusion | flops 1179648 | bytes 1054721 | tf_op jit(solution)/shard_map/convert_element_type | solution.py:143
  (56 shorter events, 1.1 us)
Async XLA Ops:
  1.7 5.4 %collective-permute-start.1 = (bf16[128,512]{1,0:T(8,128)(2,1)S(1)}, bf16[128,512]{1,0:T(8,128)(2,1)S(1)}, u32[]{:S(2)}, u32[]{:S(2)}) collective-permute-start(bf16[128,512]{1,0:T(8,128)(2,1)S(1)} %get-tuple-element.22), channel_id=1, source_target_pairs={{0,32},{16,48},{32,0},{48,16},{64,96},{80,112},{96,64},{112,80},{1... | collective-permute-start | bytes 393224 | tf_op jit(solution)/shard_map/ppermute | solution.py:38
  1.9 6.4 %collective-permute-start.3 = (bf16[128,512]{1,0:T(8,128)(2,1)S(1)}, bf16[128,512]{1,0:T(8,128)(2,1)S(1)}, u32[]{:S(2)}, u32[]{:S(2)}) collective-permute-start(bf16[128,512]{1,0:T(8,128)(2,1)S(1)} %get-tuple-element.13), channel_id=1, source_target_pairs={{0,192},{16,208},{32,224},{48,240},{64,0},{80,16},{96,32},{112,48}... | collective-permute-start | bytes 393224 | tf_op jit(solution)/shard_map/ppermute | solution.py:38
  2.7 8.9 %collective-permute-start = (bf16[128,512]{1,0:T(8,128)(2,1)S(1)}, bf16[128,512]{1,0:T(8,128)(2,1)S(1)}, u32[]{:S(2)}, u32[]{:S(2)}) collective-permute-start(bf16[128,512]{1,0:T(8,128)(2,1)S(1)} %get-tuple-element.13), channel_id=1, source_target_pairs={{0,64},{16,80},{32,96},{48,112},{64,128},{80,144},{96,160},{112,17... | collective-permute-start | bytes 393224 | tf_op jit(solution)/shard_map/ppermute | solution.py:38
  5.1 9.2 %collective-permute-start.5 = (bf16[128,512]{1,0:T(8,128)(2,1)S(1)}, bf16[128,512]{1,0:T(8,128)(2,1)S(1)}, u32[]{:S(2)}, u32[]{:S(2)}) collective-permute-start(bf16[128,512]{1,0:T(8,128)(2,1)S(1)} %get-tuple-element.22), channel_id=1, source_target_pairs={{0,160},{16,176},{32,128},{48,144},{64,224},{80,240},{96,192},{112... | collective-permute-start | bytes 393224 | tf_op jit(solution)/shard_map/ppermute | solution.py:38
  8.3 9.8 %collective-permute-start.4 = (bf16[256,512]{1,0:T(8,128)(2,1)S(1)}, bf16[256,512]{1,0:T(8,128)(2,1)S(1)}, u32[]{:S(2)}, u32[]{:S(2)}) collective-permute-start(bf16[256,512]{1,0:T(8,128)(2,1)S(1)} %pad_maximum_fusion.3), channel_id=1, source_target_pairs={{0,192},{16,208},{32,224},{48,240},{64,0},{80,16},{96,32},{112,48}... | collective-permute-start | bytes 786440 | tf_op jit(solution)/shard_map/ppermute | solution.py:38
  8.4 5.7 %collective-permute-start.2 = (bf16[128,512]{1,0:T(8,128)(2,1)S(1)}, bf16[128,512]{1,0:T(8,128)(2,1)S(1)}, u32[]{:S(2)}, u32[]{:S(2)}) collective-permute-start(bf16[128,512]{1,0:T(8,128)(2,1)S(1)} %collective-permute-done.1), channel_id=1, source_target_pairs={{0,64},{16,80},{32,96},{48,112},{64,128},{80,144},{96,160},{112,17... | collective-permute-start | bytes 393224 | tf_op jit(solution)/shard_map/ppermute | solution.py:38
  14.2 4.1 %collective-permute-start.6 = (bf16[512,512]{1,0:T(8,128)(2,1)S(1)}, bf16[512,512]{1,0:T(8,128)(2,1)S(1)}, u32[]{:S(2)}, u32[]{:S(2)}) collective-permute-start(bf16[512,512]{1,0:T(8,128)(2,1)S(1)} %pad_maximum_fusion), channel_id=1, source_target_pairs={{0,16},{16,0},{32,48},{48,32},{64,80},{80,64},{96,112},{112,96},{1... | collective-permute-start | bytes 1572872 | tf_op jit(solution)/shard_map/ppermute | solution.py:16
  18.2 2.0 %collective-permute-start.7 = (bf16[512,512]{1,0:T(8,128)(2,1)S(1)}, bf16[512,512]{1,0:T(8,128)(2,1)S(1)}, u32[]{:S(2)}, u32[]{:S(2)}) collective-permute-start(bf16[512,512]{1,0:T(8,128)(2,1)S(1)} %pad_maximum_fusion.1), channel_id=1, source_target_pairs={{0,16},{16,0},{32,48},{48,32},{64,80},{80,64},{96,112},{112,96},{1... | collective-permute-start | bytes 1572872 | tf_op jit(solution)/shard_map/ppermute | solution.py:16
  21.5 2.6 %copy-start = (f32[128,2048]{1,0:T(8,128)}, f32[128,2048]{1,0:T(8,128)S(1)}, u32[]{:S(2)}) copy-start(f32[128,2048]{1,0:T(8,128)S(1)} %fusion.12) | copy-start | bytes 3145732
  21.6 6.5 %collective-permute-start.14 = (bf16[2,32,2048]{2,1,0:T(8,128)(2,1)S(1)}, bf16[2,32,2048]{2,1,0:T(8,128)(2,1)S(1)}, u32[]{:S(2)}, u32[]{:S(2)}) collective-permute-start(bf16[2,32,2048]{2,1,0:T(8,128)(2,1)S(1)} %bitcast.78), channel_id=1, source_target_pairs={{0,1},{1,0},{2,3},{3,2},{16,19},{17,18},{18,17},{19,16},{32,33},{3... | collective-permute-start | bytes 786440 | tf_op jit(solution)/shard_map/ppermute | solution.py:30
  24.1 1.3 %copy-start.1 = (f32[128,2048]{1,0:T(8,128)}, f32[128,2048]{1,0:T(8,128)S(1)}, u32[]{:S(2)}) copy-start(f32[128,2048]{1,0:T(8,128)S(1)} %fusion.10) | copy-start | bytes 3145732
  24.2 3.9 %slice-start = ((f32[128,2048]{1,0:T(8,128)}), f32[64,2048]{1,0:T(8,128)S(1)}, s32[]{:S(2)}) async-start(f32[128,2048]{1,0:T(8,128)} %copy-done), calls=%async_computation | async-start | bytes 1048576 | tf_op jit(solution)/shard_map/slice | solution.py:42
  24.2 7.1 %collective-permute-start.8 = (bf16[2,32,2048]{2,1,0:T(8,128)(2,1)S(1)}, bf16[2,32,2048]{2,1,0:T(8,128)(2,1)S(1)}, u32[]{:S(2)}, u32[]{:S(2)}) collective-permute-start(bf16[2,32,2048]{2,1,0:T(8,128)(2,1)S(1)} %bitcast.79), channel_id=1, source_target_pairs={{0,1},{1,0},{2,3},{3,2},{16,19},{17,18},{18,17},{19,16},{32,33},{3... | collective-permute-start | bytes 786440 | tf_op jit(solution)/shard_map/ppermute | solution.py:30
  25.5 5.8 %slice-start.1 = ((f32[128,2048]{1,0:T(8,128)}), f32[64,2048]{1,0:T(8,128)S(1)}, s32[]{:S(2)}) async-start(f32[128,2048]{1,0:T(8,128)} %copy-done.1), calls=%async_computation.1 | async-start | bytes 1048576 | tf_op jit(solution)/shard_map/slice | solution.py:42
  28.2 6.3 %collective-permute-start.15 = (bf16[32,2048]{1,0:T(8,128)(2,1)S(1)}, bf16[32,2048]{1,0:T(8,128)(2,1)S(1)}, u32[]{:S(2)}, u32[]{:S(2)}) collective-permute-start(bf16[32,2048]{1,0:T(8,128)(2,1)S(1)} %fusion.25), channel_id=1, source_target_pairs={{0,3},{1,2},{2,1},{3,0},{16,17},{17,16},{18,19},{19,18},{32,35},{3... | collective-permute-start | bytes 393224 | tf_op jit(solution)/shard_map/ppermute | solution.py:30
  31.4 6.5 %collective-permute-start.9 = (bf16[32,2048]{1,0:T(8,128)(2,1)S(1)}, bf16[32,2048]{1,0:T(8,128)(2,1)S(1)}, u32[]{:S(2)}, u32[]{:S(2)}) collective-permute-start(bf16[32,2048]{1,0:T(8,128)(2,1)S(1)} %fusion.24), channel_id=1, source_target_pairs={{0,3},{1,2},{2,1},{3,0},{16,17},{17,16},{18,19},{19,18},{32,35},{3... | collective-permute-start | bytes 393224 | tf_op jit(solution)/shard_map/ppermute | solution.py:30
  34.5 6.6 %collective-permute-start.16 = (bf16[32,2048]{1,0:T(8,128)(2,1)S(1)}, bf16[32,2048]{1,0:T(8,128)(2,1)S(1)}, u32[]{:S(2)}, u32[]{:S(2)}) collective-permute-start(bf16[32,2048]{1,0:T(8,128)(2,1)S(1)} %fusion.29), channel_id=1, source_target_pairs={{0,4},{4,0},{8,12},{12,8},{16,28},{20,24},{24,20},{28,16},{32,36},... | collective-permute-start | bytes 393224 | tf_op jit(solution)/shard_map/ppermute | solution.py:30
  37.9 10.1 %collective-permute-start.10 = (bf16[32,2048]{1,0:T(8,128)(2,1)S(1)}, bf16[32,2048]{1,0:T(8,128)(2,1)S(1)}, u32[]{:S(2)}, u32[]{:S(2)}) collective-permute-start(bf16[32,2048]{1,0:T(8,128)(2,1)S(1)} %fusion.28), channel_id=1, source_target_pairs={{0,4},{4,0},{8,12},{12,8},{16,28},{20,24},{24,20},{28,16},{32,36},... | collective-permute-start | bytes 393224 | tf_op jit(solution)/shard_map/ppermute | solution.py:30
  41.1 13.4 %collective-permute-start.17 = (bf16[32,2048]{1,0:T(8,128)(2,1)S(1)}, bf16[32,2048]{1,0:T(8,128)(2,1)S(1)}, u32[]{:S(2)}, u32[]{:S(2)}) collective-permute-start(bf16[32,2048]{1,0:T(8,128)(2,1)S(1)} %fusion.23), channel_id=1, source_target_pairs={{0,12},{4,8},{8,4},{12,0},{16,20},{20,16},{24,28},{28,24},{32,44},... | collective-permute-start | bytes 393224 | tf_op jit(solution)/shard_map/ppermute | solution.py:30
  48.0 10.4 %collective-permute-start.11 = (bf16[32,2048]{1,0:T(8,128)(2,1)S(1)}, bf16[32,2048]{1,0:T(8,128)(2,1)S(1)}, u32[]{:S(2)}, u32[]{:S(2)}) collective-permute-start(bf16[32,2048]{1,0:T(8,128)(2,1)S(1)} %fusion.22), channel_id=1, source_target_pairs={{0,12},{4,8},{8,4},{12,0},{16,20},{20,16},{24,28},{28,24},{32,44},... | collective-permute-start | bytes 393224 | tf_op jit(solution)/shard_map/ppermute | solution.py:30
  54.6 7.8 %collective-permute-start.18 = (bf16[32,2048]{1,0:T(8,128)(2,1)S(1)}, bf16[32,2048]{1,0:T(8,128)(2,1)S(1)}, u32[]{:S(2)}, u32[]{:S(2)}) collective-permute-start(bf16[32,2048]{1,0:T(8,128)(2,1)S(1)} %add_convert_fusion), channel_id=1, source_target_pairs={{0,3},{1,2},{2,1},{3,0},{16,19},{17,18},{18,17},{19,16},{32,35},{3... | collective-permute-start | bytes 393224 | tf_op jit(solution)/shard_map/ppermute | solution.py:30
  58.5 6.5 %collective-permute-start.12 = (bf16[32,2048]{1,0:T(8,128)(2,1)S(1)}, bf16[32,2048]{1,0:T(8,128)(2,1)S(1)}, u32[]{:S(2)}, u32[]{:S(2)}) collective-permute-start(bf16[32,2048]{1,0:T(8,128)(2,1)S(1)} %add_convert_fusion.1), channel_id=1, source_target_pairs={{0,3},{1,2},{2,1},{3,0},{16,17},{17,16},{18,19},{19,18},{32,35},{3... | collective-permute-start | bytes 393224 | tf_op jit(solution)/shard_map/ppermute | solution.py:30
  62.5 6.5 %collective-permute-start.19 = (bf16[64,2048]{1,0:T(8,128)(2,1)S(1)}, bf16[64,2048]{1,0:T(8,128)(2,1)S(1)}, u32[]{:S(2)}, u32[]{:S(2)}) collective-permute-start(bf16[64,2048]{1,0:T(8,128)(2,1)S(1)} %pad_maximum_fusion.5), channel_id=1, source_target_pairs={{0,1},{1,0},{2,3},{3,2},{16,17},{17,16},{18,19},{19,18},{32,33},{3... | collective-permute-start | bytes 786440 | tf_op jit(solution)/shard_map/ppermute | solution.py:30
  63.1 9.3 %collective-permute-start.20 = (bf16[64,512]{1,0:T(8,128)(2,1)S(1)}, bf16[64,512]{1,0:T(8,128)(2,1)S(1)}, u32[]{:S(2)}, u32[]{:S(2)}) collective-permute-start(bf16[64,512]{1,0:T(8,128)(2,1)S(1)} %fusion.5), channel_id=1, source_target_pairs={{0,32},{16,48},{32,0},{48,16},{64,96},{80,112},{96,64},{112,80},{1... | collective-permute-start | bytes 196616 | tf_op jit(solution)/shard_map/ppermute | solution.py:16
  65.0 6.8 %collective-permute-start.13 = (bf16[64,2048]{1,0:T(8,128)(2,1)S(1)}, bf16[64,2048]{1,0:T(8,128)(2,1)S(1)}, u32[]{:S(2)}, u32[]{:S(2)}) collective-permute-start(bf16[64,2048]{1,0:T(8,128)(2,1)S(1)} %pad_maximum_fusion.4), channel_id=1, source_target_pairs={{0,1},{1,0},{2,3},{3,2},{16,19},{17,18},{18,17},{19,16},{32,33},{3... | collective-permute-start | bytes 786440 | tf_op jit(solution)/shard_map/ppermute | solution.py:30
  69.5 4.4 %collective-permute-start.21 = (bf16[64,512]{1,0:T(8,128)(2,1)S(1)}, bf16[64,512]{1,0:T(8,128)(2,1)S(1)}, u32[]{:S(2)}, u32[]{:S(2)}) collective-permute-start(bf16[64,512]{1,0:T(8,128)(2,1)S(1)} %fusion.4), channel_id=1, source_target_pairs={{0,32},{16,48},{32,0},{48,16},{64,96},{80,112},{96,64},{112,80},{1... | collective-permute-start | bytes 196616 | tf_op jit(solution)/shard_map/ppermute | solution.py:16

commit v4 on v2

--- a/solution.py
+++ b/solution.py
@@ -78,8 +78,9 @@
     mine = jnp.where(first, view_one, view_two)
     away, away_far = move(other, 0, flip=1), move(other, 2, flip=1)
     low, high = move(mine, 1), move(mine, -1)
+    onward = move(jnp.concatenate([away, high], axis=0), -1)
     near = jnp.concatenate([mine, low, away, move(away, 1)], axis=0)
-    rest = jnp.concatenate([high, move(away, -1), move(high, -1), away_far], axis=0)
+    rest = jnp.concatenate([high, onward, away_far], axis=0)
     full = jnp.concatenate([near, rest, swap(near, 1), swap(rest, 1)], axis=0)
     mean_val = jnp.sum(full.astype(F32), axis=0, keepdims=True) / sample_count
     rounded = (full.astype(F32) - mean_val).astype(BF)
@@ -87,15 +88,12 @@
     coef_cov = 2.0 * sample_count / (25.0 * (sample_count - 1) * (sample_count - 1))
     quarter = local_rows // 4
 
-    def gram_of(raw, earlier=None):
-        own_cent = raw.astype(F32) - mean_val
-        own = own_cent.astype(BF)
-        blocks = ordered(own.reshape(4, quarter, width), "col", core == 0).reshape(local_rows, width)
-        if earlier is not None:
-            blocks, earlier = lax.optimization_barrier((blocks, earlier))
-        gram = jnp.dot(blocks, rounded.T, preferred_element_type=F32)
-        parts = gram.reshape(4, quarter, sample_count)
-        return parts, parts[2:].astype(BF)
+    own = [(raw.astype(F32) - mean_val).astype(BF) for raw in (away, mine)]
+    blocks = [ordered(x.reshape(4, quarter, width), "col", core == 0) for x in own]
+    blocks = jnp.concatenate(blocks, axis=0).reshape(2 * local_rows, width)
+    gram = jnp.dot(blocks, rounded.T, preferred_element_type=F32)
+    parts_away, parts_mine = gram.reshape(2, 4, quarter, sample_count)
+    send_away, send_mine = parts_away[2:].astype(BF), parts_mine[2:].astype(BF)
 
     def term_of(raw):
         own_cent = raw.astype(F32) - mean_late
@@ -109,16 +107,15 @@
     def away_part(rows, term):
         return (coef_cov * jnp.dot(rows, rounded, preferred_element_type=F32) - term).astype(BF)
 
-    parts_away, send_away = gram_of(away)
-    parts_mine, send_mine = gram_of(mine, send_away)
     full_late, mean_late, away_late, mine_late, _ = lax.optimization_barrier(
-        (full, mean_val, away, mine, send_mine)
+        (full, mean_val, away, mine, send_away)
     )
     cent = full_late.astype(F32) - mean_late
     variance = jnp.sum(cent * cent, axis=0, keepdims=True) / (sample_count - 1)
     hinge = hinge_of(variance)
     wide = cent.astype(BF).astype(F32)
     feature_squares = jnp.sum(wide * wide, axis=0, keepdims=True)
+    send_mine, feature_squares = lax.optimization_barrier((send_mine, feature_squares))
     term_away, term_mine = term_of(away_late), term_of(mine_late)
     term_away = ordered(term_away.reshape(4, quarter, width), "col", True)
     term_away = term_away.reshape(2, 2 * quarter, width)

time: 74.3 us -> 74.3 us (level)
  matrix products: 3.28 us -> 2.37 us
    dot_general x2 -> x1, matrix products: 1.67 us -> 0.76 us  [on_device(): gram = jnp.dot(blocks, rounded.T, preferred_element_type=F32)]
    ppermute x7 -> x6, waiting for transfers between devices: 7.73 us -> 7.93 us  [move(): return lax.ppermute(x, 'batch', pairs)]
    ppermute x7 -> x6, starting transfers between devices: 8.22 us -> 8.29 us  [move(): return lax.ppermute(x, 'batch', pairs)]
  transfers between devices with their start and end apart: 23 -> 22, of which waited for: 14 -> 13; matrix products, arithmetic and copies ran while one was open for 5% -> 4% of each run, Pallas kernels for 0% -> 0%
where the time goes in v4:
time: 74.3 us; the launch traced here: 74.2 us
  starting transfers between devices  43.6 us (59%)
  waiting for transfers between devices  23 us (31%)
  other arithmetic  3.8 us (5%)
  matrix products  2.37 us (3%)
  between operations  1.07 us (1%)
    ppermute x12, starting transfers between devices, exchange(): return lax.ppermute(x, ('batch', axis), pairs)  35 us
    ppermute x12, waiting for transfers between devices, exchange(): return lax.ppermute(x, ('batch', axis), pairs)  12 us
    ppermute x6, starting transfers between devices, move(): return lax.ppermute(x, 'batch', pairs)  8.29 us
    ppermute x6, waiting for transfers between devices, move(): return lax.ppermute(x, 'batch', pairs)  7.93 us
    ppermute x4, waiting for transfers between devices, swap(): lax.ppermute(x, 'batch', [(i, i ^ bit) for i in range(lax.axis_size('batc...  3.09 us
  transfers between devices with their start and end apart: 22, of which 13 were waited for; matrix products, arithmetic and copies ran while one was open for 4% of the time, Pallas kernels for 0%

profile of v4, /device:TPU:38, one launch (start us, length us, event | category | flops | bytes accessed | tf_op | source)
XLA Modules:
  0.0 74.2 jit_solution(6171177183319106842)
XLA Ops:
  0.7 1.0 %constant_dynamic-update-slice_fusion.8 = (bf16[2048,512]{1,0:T(8,128)(2,1)S(1)}, bf16[128,512]{1,0:T(8,128)(2,1)S(1)}, bf16[128,512]{1,0:T(8,128)(2,1)S(1)}) fusion(bf16[128,512]{1,0:T(8,128)(2,1)} %param.2, bf16[128,512]{1,0:T(8,128)(2,1)} %param.3, pred[]{:T(512)S(6)} %eq.29), kind=kLoop, calls=%fused_computation.84 | loop fusion | flops 131071 | bytes 655361
  1.7 0.2 collective-permute-start
  1.9 0.8 %collective-permute-start.3 = (bf16[128,512]{1,0:T(8,128)(2,1)S(1)}, bf16[128,512]{1,0:T(8,128)(2,1)S(1)}, u32[]{:S(2)}, u32[]{:S(2)}) collective-permute-start(bf16[128,512]{1,0:T(8,128)(2,1)S(1)} %get-tuple-element.15), channel_id=1, source_target_pairs={{0,192},{16,208},{32,224},{48,240},{64,0},{80,16},{96,32},{112,48}... | collective-permute-start | bytes 393224 | tf_op jit(solution)/shard_map/ppermute | solution.py:38
  2.7 2.4 %collective-permute-start.1 = (bf16[128,512]{1,0:T(8,128)(2,1)S(1)}, bf16[128,512]{1,0:T(8,128)(2,1)S(1)}, u32[]{:S(2)}, u32[]{:S(2)}) collective-permute-start(bf16[128,512]{1,0:T(8,128)(2,1)S(1)} %get-tuple-element.15), channel_id=1, source_target_pairs={{0,64},{16,80},{32,96},{48,112},{64,128},{80,144},{96,160},{112,17... | collective-permute-start | bytes 393224 | tf_op jit(solution)/shard_map/ppermute | solution.py:38
  5.1 1.5 %collective-permute-start.5 = (bf16[128,512]{1,0:T(8,128)(2,1)S(1)}, bf16[128,512]{1,0:T(8,128)(2,1)S(1)}, u32[]{:S(2)}, u32[]{:S(2)}) collective-permute-start(bf16[128,512]{1,0:T(8,128)(2,1)S(1)} %get-tuple-element.28), channel_id=1, source_target_pairs={{0,160},{16,176},{32,128},{48,144},{64,224},{80,240},{96,192},{112... | collective-permute-start | bytes 393224 | tf_op jit(solution)/shard_map/ppermute | solution.py:38
  6.7 0.4 collective-permute-done
  7.1 1.2 %collective-permute-done.3 = bf16[128,512]{1,0:T(8,128)(2,1)S(1)} collective-permute-done((bf16[128,512]{1,0:T(8,128)(2,1)S(1)}, bf16[128,512]{1,0:T(8,128)(2,1)S(1)}, u32[]{:S(2)}, u32[]{:S(2)}) %collective-permute-start.3) | collective-permute-done | bytes 131104 | tf_op jit(solution)/shard_map/ppermute | solution.py:38
  8.3 0.1 collective-permute-start.4
  8.4 3.2 %collective-permute-start.2 = (bf16[128,512]{1,0:T(8,128)(2,1)S(1)}, bf16[128,512]{1,0:T(8,128)(2,1)S(1)}, u32[]{:S(2)}, u32[]{:S(2)}) collective-permute-start(bf16[128,512]{1,0:T(8,128)(2,1)S(1)} %collective-permute-done), channel_id=1, source_target_pairs={{0,64},{16,80},{32,96},{48,112},{64,128},{80,144},{96,160},{112,17... | collective-permute-start | bytes 393224 | tf_op jit(solution)/shard_map/ppermute | solution.py:38
  11.6 0.0 collective-permute-done.1
  11.7 2.5 %collective-permute-done.2 = bf16[128,512]{1,0:T(8,128)(2,1)S(1)} collective-permute-done((bf16[128,512]{1,0:T(8,128)(2,1)S(1)}, bf16[128,512]{1,0:T(8,128)(2,1)S(1)}, u32[]{:S(2)}, u32[]{:S(2)}) %collective-permute-start.2) | collective-permute-done | bytes 131104 | tf_op jit(solution)/shard_map/ppermute | solution.py:38
  14.2 0.1 collective-permute-start.6
  14.3 3.8 %collective-permute-done.4 = bf16[256,512]{1,0:T(8,128)(2,1)S(1)} collective-permute-done((bf16[256,512]{1,0:T(8,128)(2,1)S(1)}, bf16[256,512]{1,0:T(8,128)(2,1)S(1)}, u32[]{:S(2)}, u32[]{:S(2)}) %collective-permute-start.4) | collective-permute-done | bytes 262176 | tf_op jit(solution)/shard_map/ppermute | solution.py:38
  18.2 0.1 collective-permute-start.7
  18.4 1.8 %collective-permute-done.7 = bf16[512,512]{1,0:T(8,128)(2,1)S(1)} collective-permute-done((bf16[512,512]{1,0:T(8,128)(2,1)S(1)}, bf16[512,512]{1,0:T(8,128)(2,1)S(1)}, u32[]{:S(2)}, u32[]{:S(2)}) %collective-permute-start.7) | collective-permute-done | bytes 524320 | tf_op jit(solution)/shard_map/ppermute | solution.py:16
  20.2 0.3 convert_reduce_fusion
  20.8 0.8 %fusion.47 = (bf16[256,2048]{1,0:T(8,128)(2,1)S(1)}, f32[256,2048]{1,0:T(8,128)S(1)}) fusion(bf16[256,512]{1,0:T(8,128)(2,1)S(1)} %bitcast.74, bf16[2048,512]{1,0:T(8,128)(2,1)S(1)} %constant_dynamic-update-slice_fusion, f32[512]{0:T(512)S(1)} %broadcast_multiply_fusion), kind=kOutput, calls=%fused_computation.92 | convolution fusion | flops 540540928 | bytes 5507072 | tf_op jit(solution)/shard_map/dot_general | solution.py:94
  21.6 1.7 %collective-permute-start.14 = (bf16[2,32,2048]{2,1,0:T(8,128)(2,1)S(1)}, bf16[2,32,2048]{2,1,0:T(8,128)(2,1)S(1)}, u32[]{:S(2)}, u32[]{:S(2)}) collective-permute-start(bf16[2,32,2048]{2,1,0:T(8,128)(2,1)S(1)} %bitcast.84), channel_id=1, source_target_pairs={{0,1},{1,0},{2,3},{3,2},{16,19},{17,18},{18,17},{19,16},{32,33},{3... | collective-permute-start | bytes 786440 | tf_op jit(solution)/shard_map/ppermute | solution.py:30
  23.3 0.6 multiply_reduce_fusion.1
  23.9 0.1 multiply_add_fusion
  24.0 0.5 collective-permute-start.8
  24.5 0.1 fusion.44
  24.7 3.4 %collective-permute-done.14 = bf16[2,32,2048]{2,1,0:T(8,128)(2,1)S(1)} collective-permute-done((bf16[2,32,2048]{2,1,0:T(8,128)(2,1)S(1)}, bf16[2,32,2048]{2,1,0:T(8,128)(2,1)S(1)}, u32[]{:S(2)}, u32[]{:S(2)}) %collective-permute-start.14) | collective-permute-done | bytes 262176 | tf_op jit(solution)/shard_map/ppermute | solution.py:30
  28.1 3.1 %collective-permute-start.15 = (bf16[32,2048]{1,0:T(8,128)(2,1)S(1)}, bf16[32,2048]{1,0:T(8,128)(2,1)S(1)}, u32[]{:S(2)}, u32[]{:S(2)}) collective-permute-start(bf16[32,2048]{1,0:T(8,128)(2,1)S(1)} %fusion.39), channel_id=1, source_target_pairs={{0,3},{1,2},{2,1},{3,0},{16,17},{17,16},{18,19},{19,18},{32,35},{3... | collective-permute-start | bytes 393224 | tf_op jit(solution)/shard_map/ppermute | solution.py:30
  31.3 2.7 %collective-permute-start.9 = (bf16[32,2048]{1,0:T(8,128)(2,1)S(1)}, bf16[32,2048]{1,0:T(8,128)(2,1)S(1)}, u32[]{:S(2)}, u32[]{:S(2)}) collective-permute-start(bf16[32,2048]{1,0:T(8,128)(2,1)S(1)} %fusion.38), channel_id=1, source_target_pairs={{0,3},{1,2},{2,1},{3,0},{16,17},{17,16},{18,19},{19,18},{32,35},{3... | collective-permute-start | bytes 393224 | tf_op jit(solution)/shard_map/ppermute | solution.py:30
  34.0 0.4 collective-permute-done.15
  34.4 3.3 %collective-permute-start.16 = (bf16[32,2048]{1,0:T(8,128)(2,1)S(1)}, bf16[32,2048]{1,0:T(8,128)(2,1)S(1)}, u32[]{:S(2)}, u32[]{:S(2)}) collective-permute-start(bf16[32,2048]{1,0:T(8,128)(2,1)S(1)} %fusion.42), channel_id=1, source_target_pairs={{0,4},{4,0},{8,12},{12,8},{16,28},{20,24},{24,20},{28,16},{32,36},... | collective-permute-start | bytes 393224 | tf_op jit(solution)/shard_map/ppermute | solution.py:30
  37.8 3.1 %collective-permute-start.10 = (bf16[32,2048]{1,0:T(8,128)(2,1)S(1)}, bf16[32,2048]{1,0:T(8,128)(2,1)S(1)}, u32[]{:S(2)}, u32[]{:S(2)}) collective-permute-start(bf16[32,2048]{1,0:T(8,128)(2,1)S(1)} %fusion.41), channel_id=1, source_target_pairs={{0,4},{4,0},{8,12},{12,8},{16,28},{20,24},{24,20},{28,16},{32,36},... | collective-permute-start | bytes 393224 | tf_op jit(solution)/shard_map/ppermute | solution.py:30
  41.0 0.1 collective-permute-done.16
  41.1 5.6 %collective-permute-start.17 = (bf16[32,2048]{1,0:T(8,128)(2,1)S(1)}, bf16[32,2048]{1,0:T(8,128)(2,1)S(1)}, u32[]{:S(2)}, u32[]{:S(2)}) collective-permute-start(bf16[32,2048]{1,0:T(8,128)(2,1)S(1)} %fusion.37), channel_id=1, source_target_pairs={{0,12},{4,8},{8,4},{12,0},{16,20},{20,16},{24,28},{28,24},{32,44},... | collective-permute-start | bytes 393224 | tf_op jit(solution)/shard_map/ppermute | solution.py:30
  46.7 0.2 collective-permute-done.10
  46.9 7.4 %collective-permute-start.11 = (bf16[32,2048]{1,0:T(8,128)(2,1)S(1)}, bf16[32,2048]{1,0:T(8,128)(2,1)S(1)}, u32[]{:S(2)}, u32[]{:S(2)}) collective-permute-start(bf16[32,2048]{1,0:T(8,128)(2,1)S(1)} %fusion.36), channel_id=1, source_target_pairs={{0,12},{4,8},{8,4},{12,0},{16,20},{20,16},{24,28},{28,24},{32,44},... | collective-permute-start | bytes 393224 | tf_op jit(solution)/shard_map/ppermute | solution.py:30
  54.3 0.1 add_convert_fusion
  54.4 3.9 %collective-permute-start.18 = (bf16[32,2048]{1,0:T(8,128)(2,1)S(1)}, bf16[32,2048]{1,0:T(8,128)(2,1)S(1)}, u32[]{:S(2)}, u32[]{:S(2)}) collective-permute-start(bf16[32,2048]{1,0:T(8,128)(2,1)S(1)} %add_convert_fusion), channel_id=1, source_target_pairs={{0,3},{1,2},{2,1},{3,0},{16,19},{17,18},{18,17},{19,16},{32,35},{3... | collective-permute-start | bytes 393224 | tf_op jit(solution)/shard_map/ppermute | solution.py:30
  58.3 0.1 add_convert_fusion.1
  58.4 3.4 %collective-permute-start.12 = (bf16[32,2048]{1,0:T(8,128)(2,1)S(1)}, bf16[32,2048]{1,0:T(8,128)(2,1)S(1)}, u32[]{:S(2)}, u32[]{:S(2)}) collective-permute-start(bf16[32,2048]{1,0:T(8,128)(2,1)S(1)} %add_convert_fusion.1), channel_id=1, source_target_pairs={{0,3},{1,2},{2,1},{3,0},{16,19},{17,18},{18,17},{19,16},{32,35},{3... | collective-permute-start | bytes 393224 | tf_op jit(solution)/shard_map/ppermute | solution.py:30
  61.8 0.1 collective-permute-start.19
  61.9 0.5 fusion.22
  62.5 0.1 collective-permute-start.20
  62.6 2.2 %collective-permute-done.12 = bf16[32,2048]{1,0:T(8,128)(2,1)S(1)} collective-permute-done((bf16[32,2048]{1,0:T(8,128)(2,1)S(1)}, bf16[32,2048]{1,0:T(8,128)(2,1)S(1)}, u32[]{:S(2)}, u32[]{:S(2)}) %collective-permute-start.12) | collective-permute-done | bytes 131104 | tf_op jit(solution)/shard_map/ppermute | solution.py:30
  64.8 0.1 collective-permute-start.13
  64.9 3.4 %collective-permute-done.19 = bf16[64,2048]{1,0:T(8,128)(2,1)S(1)} collective-permute-done((bf16[64,2048]{1,0:T(8,128)(2,1)S(1)}, bf16[64,2048]{1,0:T(8,128)(2,1)S(1)}, u32[]{:S(2)}, u32[]{:S(2)}) %collective-permute-start.19) | collective-permute-done | bytes 262176 | tf_op jit(solution)/shard_map/ppermute | solution.py:30
  68.3 0.5 fusion.25
  68.8 0.1 collective-permute-start.21
  68.9 2.3 %collective-permute-done.13 = bf16[64,2048]{1,0:T(8,128)(2,1)S(1)} collective-permute-done((bf16[64,2048]{1,0:T(8,128)(2,1)S(1)}, bf16[64,2048]{1,0:T(8,128)(2,1)S(1)}, u32[]{:S(2)}, u32[]{:S(2)}) %collective-permute-start.13) | collective-permute-done | bytes 262176 | tf_op jit(solution)/shard_map/ppermute | solution.py:30
  71.3 0.5 fusion.4
  71.8 1.3 %collective-permute-done.21 = bf16[64,512]{1,0:T(8,128)(2,1)S(1)} collective-permute-done((bf16[64,512]{1,0:T(8,128)(2,1)S(1)}, bf16[64,512]{1,0:T(8,128)(2,1)S(1)}, u32[]{:S(2)}, u32[]{:S(2)}) %collective-permute-start.21) | collective-permute-done | bytes 65568 | tf_op jit(solution)/shard_map/ppermute | solution.py:16
  73.3 0.8 %select_convert_fusion = (bf16[128,512]{1,0:T(8,128)(2,1)}, bf16[128,512]{1,0:T(8,128)(2,1)}) fusion(pred[]{:T(512)S(6)} %eq.29, bf16[128,512]{1,0:T(8,128)(2,1)S(1)} %get-tuple-element.28, bf16[128,512]{1,0:T(8,128)(2,1)S(1)} %get-tuple-element.15, f32[2,2,32,512]{3,2,1,0:T(8,128)S(1)} %reverse_select_fusion, f32[512]{0:T(512)S(1)} %fusion.43, ...), kind=kLoop, calls=%fused_computation.48 | loop fusion | flops 1179648 | bytes 1054721 | tf_op jit(solution)/shard_map/convert_element_type | solution.py:139
  (49 shorter events, 1.1 us)
Async XLA Ops:
  1.7 5.4 %collective-permute-start = (bf16[128,512]{1,0:T(8,128)(2,1)S(1)}, bf16[128,512]{1,0:T(8,128)(2,1)S(1)}, u32[]{:S(2)}, u32[]{:S(2)}) collective-permute-start(bf16[128,512]{1,0:T(8,128)(2,1)S(1)} %get-tuple-element.28), channel_id=1, source_target_pairs={{0,32},{16,48},{32,0},{48,16},{64,96},{80,112},{96,64},{112,80},{1... | collective-permute-start | bytes 393224 | tf_op jit(solution)/shard_map/ppermute | solution.py:38
  1.9 6.4 %collective-permute-start.3 = (bf16[128,512]{1,0:T(8,128)(2,1)S(1)}, bf16[128,512]{1,0:T(8,128)(2,1)S(1)}, u32[]{:S(2)}, u32[]{:S(2)}) collective-permute-start(bf16[128,512]{1,0:T(8,128)(2,1)S(1)} %get-tuple-element.15), channel_id=1, source_target_pairs={{0,192},{16,208},{32,224},{48,240},{64,0},{80,16},{96,32},{112,48}... | collective-permute-start | bytes 393224 | tf_op jit(solution)/shard_map/ppermute | solution.py:38
  2.7 8.9 %collective-permute-start.1 = (bf16[128,512]{1,0:T(8,128)(2,1)S(1)}, bf16[128,512]{1,0:T(8,128)(2,1)S(1)}, u32[]{:S(2)}, u32[]{:S(2)}) collective-permute-start(bf16[128,512]{1,0:T(8,128)(2,1)S(1)} %get-tuple-element.15), channel_id=1, source_target_pairs={{0,64},{16,80},{32,96},{48,112},{64,128},{80,144},{96,160},{112,17... | collective-permute-start | bytes 393224 | tf_op jit(solution)/shard_map/ppermute | solution.py:38
  5.1 9.2 %collective-permute-start.5 = (bf16[128,512]{1,0:T(8,128)(2,1)S(1)}, bf16[128,512]{1,0:T(8,128)(2,1)S(1)}, u32[]{:S(2)}, u32[]{:S(2)}) collective-permute-start(bf16[128,512]{1,0:T(8,128)(2,1)S(1)} %get-tuple-element.28), channel_id=1, source_target_pairs={{0,160},{16,176},{32,128},{48,144},{64,224},{80,240},{96,192},{112... | collective-permute-start | bytes 393224 | tf_op jit(solution)/shard_map/ppermute | solution.py:38
  8.3 9.8 %collective-permute-start.4 = (bf16[256,512]{1,0:T(8,128)(2,1)S(1)}, bf16[256,512]{1,0:T(8,128)(2,1)S(1)}, u32[]{:S(2)}, u32[]{:S(2)}) collective-permute-start(bf16[256,512]{1,0:T(8,128)(2,1)S(1)} %pad_maximum_fusion.3), channel_id=1, source_target_pairs={{0,192},{16,208},{32,224},{48,240},{64,0},{80,16},{96,32},{112,48}... | collective-permute-start | bytes 786440 | tf_op jit(solution)/shard_map/ppermute | solution.py:38
  8.4 5.7 %collective-permute-start.2 = (bf16[128,512]{1,0:T(8,128)(2,1)S(1)}, bf16[128,512]{1,0:T(8,128)(2,1)S(1)}, u32[]{:S(2)}, u32[]{:S(2)}) collective-permute-start(bf16[128,512]{1,0:T(8,128)(2,1)S(1)} %collective-permute-done), channel_id=1, source_target_pairs={{0,64},{16,80},{32,96},{48,112},{64,128},{80,144},{96,160},{112,17... | collective-permute-start | bytes 393224 | tf_op jit(solution)/shard_map/ppermute | solution.py:38
  14.2 4.1 %collective-permute-start.6 = (bf16[512,512]{1,0:T(8,128)(2,1)S(1)}, bf16[512,512]{1,0:T(8,128)(2,1)S(1)}, u32[]{:S(2)}, u32[]{:S(2)}) collective-permute-start(bf16[512,512]{1,0:T(8,128)(2,1)S(1)} %pad_maximum_fusion), channel_id=1, source_target_pairs={{0,16},{16,0},{32,48},{48,32},{64,80},{80,64},{96,112},{112,96},{1... | collective-permute-start | bytes 1572872 | tf_op jit(solution)/shard_map/ppermute | solution.py:16
  18.2 2.0 %collective-permute-start.7 = (bf16[512,512]{1,0:T(8,128)(2,1)S(1)}, bf16[512,512]{1,0:T(8,128)(2,1)S(1)}, u32[]{:S(2)}, u32[]{:S(2)}) collective-permute-start(bf16[512,512]{1,0:T(8,128)(2,1)S(1)} %pad_maximum_fusion.1), channel_id=1, source_target_pairs={{0,16},{16,0},{32,48},{48,32},{64,80},{80,64},{96,112},{112,96},{1... | collective-permute-start | bytes 1572872 | tf_op jit(solution)/shard_map/ppermute | solution.py:16
  21.6 6.5 %collective-permute-start.14 = (bf16[2,32,2048]{2,1,0:T(8,128)(2,1)S(1)}, bf16[2,32,2048]{2,1,0:T(8,128)(2,1)S(1)}, u32[]{:S(2)}, u32[]{:S(2)}) collective-permute-start(bf16[2,32,2048]{2,1,0:T(8,128)(2,1)S(1)} %bitcast.84), channel_id=1, source_target_pairs={{0,1},{1,0},{2,3},{3,2},{16,19},{17,18},{18,17},{19,16},{32,33},{3... | collective-permute-start | bytes 786440 | tf_op jit(solution)/shard_map/ppermute | solution.py:30
  24.0 7.2 %collective-permute-start.8 = (bf16[2,32,2048]{2,1,0:T(8,128)(2,1)S(1)}, bf16[2,32,2048]{2,1,0:T(8,128)(2,1)S(1)}, u32[]{:S(2)}, u32[]{:S(2)}) collective-permute-start(bf16[2,32,2048]{2,1,0:T(8,128)(2,1)S(1)} %bitcast.83), channel_id=1, source_target_pairs={{0,1},{1,0},{2,3},{3,2},{16,19},{17,18},{18,17},{19,16},{32,33},{3... | collective-permute-start | bytes 786440 | tf_op jit(solution)/shard_map/ppermute | solution.py:30
  28.1 6.3 %collective-permute-start.15 = (bf16[32,2048]{1,0:T(8,128)(2,1)S(1)}, bf16[32,2048]{1,0:T(8,128)(2,1)S(1)}, u32[]{:S(2)}, u32[]{:S(2)}) collective-permute-start(bf16[32,2048]{1,0:T(8,128)(2,1)S(1)} %fusion.39), channel_id=1, source_target_pairs={{0,3},{1,2},{2,1},{3,0},{16,17},{17,16},{18,19},{19,18},{32,35},{3... | collective-permute-start | bytes 393224 | tf_op jit(solution)/shard_map/ppermute | solution.py:30
  31.3 6.5 %collective-permute-start.9 = (bf16[32,2048]{1,0:T(8,128)(2,1)S(1)}, bf16[32,2048]{1,0:T(8,128)(2,1)S(1)}, u32[]{:S(2)}, u32[]{:S(2)}) collective-permute-start(bf16[32,2048]{1,0:T(8,128)(2,1)S(1)} %fusion.38), channel_id=1, source_target_pairs={{0,3},{1,2},{2,1},{3,0},{16,17},{17,16},{18,19},{19,18},{32,35},{3... | collective-permute-start | bytes 393224 | tf_op jit(solution)/shard_map/ppermute | solution.py:30
  34.4 6.6 %collective-permute-start.16 = (bf16[32,2048]{1,0:T(8,128)(2,1)S(1)}, bf16[32,2048]{1,0:T(8,128)(2,1)S(1)}, u32[]{:S(2)}, u32[]{:S(2)}) collective-permute-start(bf16[32,2048]{1,0:T(8,128)(2,1)S(1)} %fusion.42), channel_id=1, source_target_pairs={{0,4},{4,0},{8,12},{12,8},{16,28},{20,24},{24,20},{28,16},{32,36},... | collective-permute-start | bytes 393224 | tf_op jit(solution)/shard_map/ppermute | solution.py:30
  37.8 9.1 %collective-permute-start.10 = (bf16[32,2048]{1,0:T(8,128)(2,1)S(1)}, bf16[32,2048]{1,0:T(8,128)(2,1)S(1)}, u32[]{:S(2)}, u32[]{:S(2)}) collective-permute-start(bf16[32,2048]{1,0:T(8,128)(2,1)S(1)} %fusion.41), channel_id=1, source_target_pairs={{0,4},{4,0},{8,12},{12,8},{16,28},{20,24},{24,20},{28,16},{32,36},... | collective-permute-start | bytes 393224 | tf_op jit(solution)/shard_map/ppermute | solution.py:30
  41.1 13.3 %collective-permute-start.17 = (bf16[32,2048]{1,0:T(8,128)(2,1)S(1)}, bf16[32,2048]{1,0:T(8,128)(2,1)S(1)}, u32[]{:S(2)}, u32[]{:S(2)}) collective-permute-start(bf16[32,2048]{1,0:T(8,128)(2,1)S(1)} %fusion.37), channel_id=1, source_target_pairs={{0,12},{4,8},{8,4},{12,0},{16,20},{20,16},{24,28},{28,24},{32,44},... | collective-permute-start | bytes 393224 | tf_op jit(solution)/shard_map/ppermute | solution.py:30
  46.9 11.4 %collective-permute-start.11 = (bf16[32,2048]{1,0:T(8,128)(2,1)S(1)}, bf16[32,2048]{1,0:T(8,128)(2,1)S(1)}, u32[]{:S(2)}, u32[]{:S(2)}) collective-permute-start(bf16[32,2048]{1,0:T(8,128)(2,1)S(1)} %fusion.36), channel_id=1, source_target_pairs={{0,12},{4,8},{8,4},{12,0},{16,20},{20,16},{24,28},{28,24},{32,44},... | collective-permute-start | bytes 393224 | tf_op jit(solution)/shard_map/ppermute | solution.py:30
  54.4 7.4 %collective-permute-start.18 = (bf16[32,2048]{1,0:T(8,128)(2,1)S(1)}, bf16[32,2048]{1,0:T(8,128)(2,1)S(1)}, u32[]{:S(2)}, u32[]{:S(2)}) collective-permute-start(bf16[32,2048]{1,0:T(8,128)(2,1)S(1)} %add_convert_fusion), channel_id=1, source_target_pairs={{0,3},{1,2},{2,1},{3,0},{16,19},{17,18},{18,17},{19,16},{32,35},{3... | collective-permute-start | bytes 393224 | tf_op jit(solution)/shard_map/ppermute | solution.py:30
  58.4 6.3 %collective-permute-start.12 = (bf16[32,2048]{1,0:T(8,128)(2,1)S(1)}, bf16[32,2048]{1,0:T(8,128)(2,1)S(1)}, u32[]{:S(2)}, u32[]{:S(2)}) collective-permute-start(bf16[32,2048]{1,0:T(8,128)(2,1)S(1)} %add_convert_fusion.1), channel_id=1, source_target_pairs={{0,3},{1,2},{2,1},{3,0},{16,19},{17,18},{18,17},{19,16},{32,35},{3... | collective-permute-start | bytes 393224 | tf_op jit(solution)/shard_map/ppermute | solution.py:30
  61.8 6.5 %collective-permute-start.19 = (bf16[64,2048]{1,0:T(8,128)(2,1)S(1)}, bf16[64,2048]{1,0:T(8,128)(2,1)S(1)}, u32[]{:S(2)}, u32[]{:S(2)}) collective-permute-start(bf16[64,2048]{1,0:T(8,128)(2,1)S(1)} %pad_maximum_fusion.6), channel_id=1, source_target_pairs={{0,1},{1,0},{2,3},{3,2},{16,17},{17,16},{18,19},{19,18},{32,33},{3... | collective-permute-start | bytes 786440 | tf_op jit(solution)/shard_map/ppermute | solution.py:30
  62.5 9.4 %collective-permute-start.20 = (bf16[64,512]{1,0:T(8,128)(2,1)S(1)}, bf16[64,512]{1,0:T(8,128)(2,1)S(1)}, u32[]{:S(2)}, u32[]{:S(2)}) collective-permute-start(bf16[64,512]{1,0:T(8,128)(2,1)S(1)} %fusion.22), channel_id=1, source_target_pairs={{0,32},{16,48},{32,0},{48,16},{64,96},{80,112},{96,64},{112,80},{1... | collective-permute-start | bytes 196616 | tf_op jit(solution)/shard_map/ppermute | solution.py:16
  64.8 6.5 %collective-permute-start.13 = (bf16[64,2048]{1,0:T(8,128)(2,1)S(1)}, bf16[64,2048]{1,0:T(8,128)(2,1)S(1)}, u32[]{:S(2)}, u32[]{:S(2)}) collective-permute-start(bf16[64,2048]{1,0:T(8,128)(2,1)S(1)} %pad_maximum_fusion.5), channel_id=1, source_target_pairs={{0,1},{1,0},{2,3},{3,2},{16,17},{17,16},{18,19},{19,18},{32,33},{3... | collective-permute-start | bytes 786440 | tf_op jit(solution)/shard_map/ppermute | solution.py:30
  68.8 4.4 %collective-permute-start.21 = (bf16[64,512]{1,0:T(8,128)(2,1)S(1)}, bf16[64,512]{1,0:T(8,128)(2,1)S(1)}, u32[]{:S(2)}, u32[]{:S(2)}) collective-permute-start(bf16[64,512]{1,0:T(8,128)(2,1)S(1)} %fusion.25), channel_id=1, source_target_pairs={{0,32},{16,48},{32,0},{48,16},{64,96},{80,112},{96,64},{112,80},{1... | collective-permute-start | bytes 196616 | tf_op jit(solution)/shard_map/ppermute | solution.py:16

commit v5 on v4

--- a/solution.py
+++ b/solution.py
@@ -78,9 +78,8 @@
     mine = jnp.where(first, view_one, view_two)
     away, away_far = move(other, 0, flip=1), move(other, 2, flip=1)
     low, high = move(mine, 1), move(mine, -1)
-    onward = move(jnp.concatenate([away, high], axis=0), -1)
     near = jnp.concatenate([mine, low, away, move(away, 1)], axis=0)
-    rest = jnp.concatenate([high, onward, away_far], axis=0)
+    rest = jnp.concatenate([high, move(away, -1), move(high, -1), away_far], axis=0)
     full = jnp.concatenate([near, rest, swap(near, 1), swap(rest, 1)], axis=0)
     mean_val = jnp.sum(full.astype(F32), axis=0, keepdims=True) / sample_count
     rounded = (full.astype(F32) - mean_val).astype(BF)

time: 74.3 us -> 74.3 us (level)
    ppermute x6 -> x7, waiting for transfers between devices: 7.93 us -> 7.73 us  [move(): return lax.ppermute(x, 'batch', pairs)]
    ppermute x6 -> x7, starting transfers between devices: 8.29 us -> 8.22 us  [move(): return lax.ppermute(x, 'batch', pairs)]
  transfers between devices with their start and end apart: 22 -> 23, of which waited for: 13 -> 13; matrix products, arithmetic and copies ran while one was open for 4% -> 4% of each run, Pallas kernels for 0% -> 0%
where the time goes in v5:
time: 74.3 us; the launch traced here: 74.2 us
  starting transfers between devices  43.9 us (59%)
  waiting for transfers between devices  22.7 us (31%)
  other arithmetic  3.78 us (5%)
  matrix products  2.36 us (3%)
  between operations  1.07 us (1%)
    ppermute x12, starting transfers between devices, exchange(): return lax.ppermute(x, ('batch', axis), pairs)  35.3 us
    ppermute x12, waiting for transfers between devices, exchange(): return lax.ppermute(x, ('batch', axis), pairs)  11.9 us
    ppermute x7, starting transfers between devices, move(): return lax.ppermute(x, 'batch', pairs)  8.22 us
    ppermute x7, waiting for transfers between devices, move(): return lax.ppermute(x, 'batch', pairs)  7.73 us
    ppermute x4, waiting for transfers between devices, swap(): lax.ppermute(x, 'batch', [(i, i ^ bit) for i in range(lax.axis_size('batc...  3.08 us
  transfers between devices with their start and end apart: 23, of which 13 were waited for; matrix products, arithmetic and copies ran while one was open for 4% of the time, Pallas kernels for 0%

profile of v5, /device:TPU:38, one launch (start us, length us, event | category | flops | bytes accessed | tf_op | source)
XLA Modules:
  0.0 74.2 jit_solution(17764875438021101709)
XLA Ops:
  0.7 1.0 %constant_dynamic-update-slice_fusion.9 = (bf16[2048,512]{1,0:T(8,128)(2,1)S(1)}, bf16[128,512]{1,0:T(8,128)(2,1)S(1)}, bf16[128,512]{1,0:T(8,128)(2,1)S(1)}) fusion(bf16[128,512]{1,0:T(8,128)(2,1)} %param.2, bf16[128,512]{1,0:T(8,128)(2,1)} %param.3, pred[]{:T(512)S(6)} %eq.29), kind=kLoop, calls=%fused_computation.84 | loop fusion | flops 131071 | bytes 655361
  1.7 0.2 collective-permute-start
  1.9 0.8 %collective-permute-start.3 = (bf16[128,512]{1,0:T(8,128)(2,1)S(1)}, bf16[128,512]{1,0:T(8,128)(2,1)S(1)}, u32[]{:S(2)}, u32[]{:S(2)}) collective-permute-start(bf16[128,512]{1,0:T(8,128)(2,1)S(1)} %get-tuple-element.15), channel_id=1, source_target_pairs={{0,192},{16,208},{32,224},{48,240},{64,0},{80,16},{96,32},{112,48}... | collective-permute-start | bytes 393224 | tf_op jit(solution)/shard_map/ppermute | solution.py:38
  2.7 2.4 %collective-permute-start.1 = (bf16[128,512]{1,0:T(8,128)(2,1)S(1)}, bf16[128,512]{1,0:T(8,128)(2,1)S(1)}, u32[]{:S(2)}, u32[]{:S(2)}) collective-permute-start(bf16[128,512]{1,0:T(8,128)(2,1)S(1)} %get-tuple-element.15), channel_id=1, source_target_pairs={{0,64},{16,80},{32,96},{48,112},{64,128},{80,144},{96,160},{112,17... | collective-permute-start | bytes 393224 | tf_op jit(solution)/shard_map/ppermute | solution.py:38
  5.1 1.5 %collective-permute-start.6 = (bf16[128,512]{1,0:T(8,128)(2,1)S(1)}, bf16[128,512]{1,0:T(8,128)(2,1)S(1)}, u32[]{:S(2)}, u32[]{:S(2)}) collective-permute-start(bf16[128,512]{1,0:T(8,128)(2,1)S(1)} %get-tuple-element.28), channel_id=1, source_target_pairs={{0,160},{16,176},{32,128},{48,144},{64,224},{80,240},{96,192},{112... | collective-permute-start | bytes 393224 | tf_op jit(solution)/shard_map/ppermute | solution.py:38
  6.7 0.4 collective-permute-done
  7.1 1.0 %collective-permute-start.4 = (bf16[128,512]{1,0:T(8,128)(2,1)S(1)}, bf16[128,512]{1,0:T(8,128)(2,1)S(1)}, u32[]{:S(2)}, u32[]{:S(2)}) collective-permute-start(bf16[128,512]{1,0:T(8,128)(2,1)S(1)} %collective-permute-done), channel_id=1, source_target_pairs={{0,192},{16,208},{32,224},{48,240},{64,0},{80,16},{96,32},{112,48}... | collective-permute-start | bytes 393224 | tf_op jit(solution)/shard_map/ppermute | solution.py:38
  8.1 2.2 %collective-permute-start.2 = (bf16[128,512]{1,0:T(8,128)(2,1)S(1)}, bf16[128,512]{1,0:T(8,128)(2,1)S(1)}, u32[]{:S(2)}, u32[]{:S(2)}) collective-permute-start(bf16[128,512]{1,0:T(8,128)(2,1)S(1)} %collective-permute-done), channel_id=1, source_target_pairs={{0,64},{16,80},{32,96},{48,112},{64,128},{80,144},{96,160},{112,17... | collective-permute-start | bytes 393224 | tf_op jit(solution)/shard_map/ppermute | solution.py:38
  10.3 0.0 collective-permute-done.3
  10.3 0.3 collective-permute-done.1
  10.6 2.8 %collective-permute-done.2 = bf16[128,512]{1,0:T(8,128)(2,1)S(1)} collective-permute-done((bf16[128,512]{1,0:T(8,128)(2,1)S(1)}, bf16[128,512]{1,0:T(8,128)(2,1)S(1)}, u32[]{:S(2)}, u32[]{:S(2)}) %collective-permute-start.2) | collective-permute-done | bytes 131104 | tf_op jit(solution)/shard_map/ppermute | solution.py:38
  13.5 0.1 collective-permute-start.7
  13.6 1.8 %collective-permute-done.4 = bf16[128,512]{1,0:T(8,128)(2,1)S(1)} collective-permute-done((bf16[128,512]{1,0:T(8,128)(2,1)S(1)}, bf16[128,512]{1,0:T(8,128)(2,1)S(1)}, u32[]{:S(2)}, u32[]{:S(2)}) %collective-permute-start.4) | collective-permute-done | bytes 131104 | tf_op jit(solution)/shard_map/ppermute | solution.py:38
  15.4 2.4 %collective-permute-done.5 = bf16[128,512]{1,0:T(8,128)(2,1)S(1)} collective-permute-done((bf16[128,512]{1,0:T(8,128)(2,1)S(1)}, bf16[128,512]{1,0:T(8,128)(2,1)S(1)}, u32[]{:S(2)}, u32[]{:S(2)}) %collective-permute-start.5) | collective-permute-done | bytes 131104 | tf_op jit(solution)/shard_map/ppermute | solution.py:38
  17.9 0.1 collective-permute-start.8
  18.1 1.7 %collective-permute-done.8 = bf16[512,512]{1,0:T(8,128)(2,1)S(1)} collective-permute-done((bf16[512,512]{1,0:T(8,128)(2,1)S(1)}, bf16[512,512]{1,0:T(8,128)(2,1)S(1)}, u32[]{:S(2)}, u32[]{:S(2)}) %collective-permute-start.8) | collective-permute-done | bytes 524320 | tf_op jit(solution)/shard_map/ppermute | solution.py:16
  19.9 0.3 convert_reduce_fusion
  20.5 0.8 %fusion.47 = (bf16[256,2048]{1,0:T(8,128)(2,1)S(1)}, f32[256,2048]{1,0:T(8,128)S(1)}) fusion(bf16[256,512]{1,0:T(8,128)(2,1)S(1)} %bitcast.74, bf16[2048,512]{1,0:T(8,128)(2,1)S(1)} %constant_dynamic-update-slice_fusion, f32[512]{0:T(512)S(1)} %broadcast_multiply_fusion), kind=kOutput, calls=%fused_computation.92 | convolution fusion | flops 540540928 | bytes 5507072 | tf_op jit(solution)/shard_map/dot_general | solution.py:93
  21.3 1.7 %collective-permute-start.15 = (bf16[2,32,2048]{2,1,0:T(8,128)(2,1)S(1)}, bf16[2,32,2048]{2,1,0:T(8,128)(2,1)S(1)}, u32[]{:S(2)}, u32[]{:S(2)}) collective-permute-start(bf16[2,32,2048]{2,1,0:T(8,128)(2,1)S(1)} %bitcast.84), channel_id=1, source_target_pairs={{0,1},{1,0},{2,3},{3,2},{16,19},{17,18},{18,17},{19,16},{32,33},{3... | collective-permute-start | bytes 786440 | tf_op jit(solution)/shard_map/ppermute | solution.py:30
  23.0 0.6 multiply_reduce_fusion.1
  23.6 0.1 multiply_add_fusion
  23.7 0.5 collective-permute-start.9
  24.2 0.1 fusion.44
  24.4 3.4 %collective-permute-done.15 = bf16[2,32,2048]{2,1,0:T(8,128)(2,1)S(1)} collective-permute-done((bf16[2,32,2048]{2,1,0:T(8,128)(2,1)S(1)}, bf16[2,32,2048]{2,1,0:T(8,128)(2,1)S(1)}, u32[]{:S(2)}, u32[]{:S(2)}) %collective-permute-start.15) | collective-permute-done | bytes 262176 | tf_op jit(solution)/shard_map/ppermute | solution.py:30
  27.8 3.1 %collective-permute-start.16 = (bf16[32,2048]{1,0:T(8,128)(2,1)S(1)}, bf16[32,2048]{1,0:T(8,128)(2,1)S(1)}, u32[]{:S(2)}, u32[]{:S(2)}) collective-permute-start(bf16[32,2048]{1,0:T(8,128)(2,1)S(1)} %fusion.39), channel_id=1, source_target_pairs={{0,3},{1,2},{2,1},{3,0},{16,17},{17,16},{18,19},{19,18},{32,35},{3... | collective-permute-start | bytes 393224 | tf_op jit(solution)/shard_map/ppermute | solution.py:30
  31.0 2.7 %collective-permute-start.10 = (bf16[32,2048]{1,0:T(8,128)(2,1)S(1)}, bf16[32,2048]{1,0:T(8,128)(2,1)S(1)}, u32[]{:S(2)}, u32[]{:S(2)}) collective-permute-start(bf16[32,2048]{1,0:T(8,128)(2,1)S(1)} %fusion.38), channel_id=1, source_target_pairs={{0,3},{1,2},{2,1},{3,0},{16,17},{17,16},{18,19},{19,18},{32,35},{3... | collective-permute-start | bytes 393224 | tf_op jit(solution)/shard_map/ppermute | solution.py:30
  33.7 0.4 collective-permute-done.16
  34.1 3.4 %collective-permute-start.17 = (bf16[32,2048]{1,0:T(8,128)(2,1)S(1)}, bf16[32,2048]{1,0:T(8,128)(2,1)S(1)}, u32[]{:S(2)}, u32[]{:S(2)}) collective-permute-start(bf16[32,2048]{1,0:T(8,128)(2,1)S(1)} %fusion.42), channel_id=1, source_target_pairs={{0,4},{4,0},{8,12},{12,8},{16,28},{20,24},{24,20},{28,16},{32,36},... | collective-permute-start | bytes 393224 | tf_op jit(solution)/shard_map/ppermute | solution.py:30
  37.5 3.3 %collective-permute-start.11 = (bf16[32,2048]{1,0:T(8,128)(2,1)S(1)}, bf16[32,2048]{1,0:T(8,128)(2,1)S(1)}, u32[]{:S(2)}, u32[]{:S(2)}) collective-permute-start(bf16[32,2048]{1,0:T(8,128)(2,1)S(1)} %fusion.41), channel_id=1, source_target_pairs={{0,4},{4,0},{8,12},{12,8},{16,28},{20,24},{24,20},{28,16},{32,36},... | collective-permute-start | bytes 393224 | tf_op jit(solution)/shard_map/ppermute | solution.py:30
  40.8 0.2 collective-permute-done.17
  41.1 6.3 %collective-permute-start.18 = (bf16[32,2048]{1,0:T(8,128)(2,1)S(1)}, bf16[32,2048]{1,0:T(8,128)(2,1)S(1)}, u32[]{:S(2)}, u32[]{:S(2)}) collective-permute-start(bf16[32,2048]{1,0:T(8,128)(2,1)S(1)} %fusion.37), channel_id=1, source_target_pairs={{0,12},{4,8},{8,4},{12,0},{16,20},{20,16},{24,28},{28,24},{32,44},... | collective-permute-start | bytes 393224 | tf_op jit(solution)/shard_map/ppermute | solution.py:30
  47.5 5.9 %collective-permute-start.12 = (bf16[32,2048]{1,0:T(8,128)(2,1)S(1)}, bf16[32,2048]{1,0:T(8,128)(2,1)S(1)}, u32[]{:S(2)}, u32[]{:S(2)}) collective-permute-start(bf16[32,2048]{1,0:T(8,128)(2,1)S(1)} %fusion.36), channel_id=1, source_target_pairs={{0,12},{4,8},{8,4},{12,0},{16,20},{20,16},{24,28},{28,24},{32,44},... | collective-permute-start | bytes 393224 | tf_op jit(solution)/shard_map/ppermute | solution.py:30
  53.4 0.1 add_convert_fusion
  53.5 4.6 %collective-permute-start.19 = (bf16[32,2048]{1,0:T(8,128)(2,1)S(1)}, bf16[32,2048]{1,0:T(8,128)(2,1)S(1)}, u32[]{:S(2)}, u32[]{:S(2)}) collective-permute-start(bf16[32,2048]{1,0:T(8,128)(2,1)S(1)} %add_convert_fusion), channel_id=1, source_target_pairs={{0,3},{1,2},{2,1},{3,0},{16,19},{17,18},{18,17},{19,16},{32,35},{3... | collective-permute-start | bytes 393224 | tf_op jit(solution)/shard_map/ppermute | solution.py:30
  58.1 0.1 add_convert_fusion.1
  58.2 3.6 %collective-permute-start.13 = (bf16[32,2048]{1,0:T(8,128)(2,1)S(1)}, bf16[32,2048]{1,0:T(8,128)(2,1)S(1)}, u32[]{:S(2)}, u32[]{:S(2)}) collective-permute-start(bf16[32,2048]{1,0:T(8,128)(2,1)S(1)} %add_convert_fusion.1), channel_id=1, source_target_pairs={{0,3},{1,2},{2,1},{3,0},{16,19},{17,18},{18,17},{19,16},{32,35},{3... | collective-permute-start | bytes 393224 | tf_op jit(solution)/shard_map/ppermute | solution.py:30
  61.8 0.1 collective-permute-start.20
  61.9 0.5 fusion.22
  62.5 0.1 collective-permute-start.21
  62.6 2.2 %collective-permute-done.13 = bf16[32,2048]{1,0:T(8,128)(2,1)S(1)} collective-permute-done((bf16[32,2048]{1,0:T(8,128)(2,1)S(1)}, bf16[32,2048]{1,0:T(8,128)(2,1)S(1)}, u32[]{:S(2)}, u32[]{:S(2)}) %collective-permute-start.13) | collective-permute-done | bytes 131104 | tf_op jit(solution)/shard_map/ppermute | solution.py:30
  64.8 0.1 collective-permute-start.14
  64.9 3.4 %collective-permute-done.20 = bf16[64,2048]{1,0:T(8,128)(2,1)S(1)} collective-permute-done((bf16[64,2048]{1,0:T(8,128)(2,1)S(1)}, bf16[64,2048]{1,0:T(8,128)(2,1)S(1)}, u32[]{:S(2)}, u32[]{:S(2)}) %collective-permute-start.20) | collective-permute-done | bytes 262176 | tf_op jit(solution)/shard_map/ppermute | solution.py:30
  68.3 0.5 fusion.25
  68.8 0.1 collective-permute-start.22
  68.9 2.3 %collective-permute-done.14 = bf16[64,2048]{1,0:T(8,128)(2,1)S(1)} collective-permute-done((bf16[64,2048]{1,0:T(8,128)(2,1)S(1)}, bf16[64,2048]{1,0:T(8,128)(2,1)S(1)}, u32[]{:S(2)}, u32[]{:S(2)}) %collective-permute-start.14) | collective-permute-done | bytes 262176 | tf_op jit(solution)/shard_map/ppermute | solution.py:30
  71.3 0.5 fusion.4
  71.8 1.3 %collective-permute-done.22 = bf16[64,512]{1,0:T(8,128)(2,1)S(1)} collective-permute-done((bf16[64,512]{1,0:T(8,128)(2,1)S(1)}, bf16[64,512]{1,0:T(8,128)(2,1)S(1)}, u32[]{:S(2)}, u32[]{:S(2)}) %collective-permute-start.22) | collective-permute-done | bytes 65568 | tf_op jit(solution)/shard_map/ppermute | solution.py:16
  73.3 0.8 %select_convert_fusion = (bf16[128,512]{1,0:T(8,128)(2,1)}, bf16[128,512]{1,0:T(8,128)(2,1)}) fusion(pred[]{:T(512)S(6)} %eq.29, bf16[128,512]{1,0:T(8,128)(2,1)S(1)} %get-tuple-element.28, bf16[128,512]{1,0:T(8,128)(2,1)S(1)} %get-tuple-element.15, f32[2,2,32,512]{3,2,1,0:T(8,128)S(1)} %reverse_select_fusion, f32[512]{0:T(512)S(1)} %fusion.43, ...), kind=kLoop, calls=%fused_computation.47 | loop fusion | flops 1179648 | bytes 1054721 | tf_op jit(solution)/shard_map/convert_element_type | solution.py:138
  (51 shorter events, 1.1 us)
Async XLA Ops:
  1.7 5.4 %collective-permute-start = (bf16[128,512]{1,0:T(8,128)(2,1)S(1)}, bf16[128,512]{1,0:T(8,128)(2,1)S(1)}, u32[]{:S(2)}, u32[]{:S(2)}) collective-permute-start(bf16[128,512]{1,0:T(8,128)(2,1)S(1)} %get-tuple-element.28), channel_id=1, source_target_pairs={{0,32},{16,48},{32,0},{48,16},{64,96},{80,112},{96,64},{112,80},{1... | collective-permute-start | bytes 393224 | tf_op jit(solution)/shard_map/ppermute | solution.py:38
  1.9 8.4 %collective-permute-start.3 = (bf16[128,512]{1,0:T(8,128)(2,1)S(1)}, bf16[128,512]{1,0:T(8,128)(2,1)S(1)}, u32[]{:S(2)}, u32[]{:S(2)}) collective-permute-start(bf16[128,512]{1,0:T(8,128)(2,1)S(1)} %get-tuple-element.15), channel_id=1, source_target_pairs={{0,192},{16,208},{32,224},{48,240},{64,0},{80,16},{96,32},{112,48}... | collective-permute-start | bytes 393224 | tf_op jit(solution)/shard_map/ppermute | solution.py:38
  2.7 7.9 %collective-permute-start.1 = (bf16[128,512]{1,0:T(8,128)(2,1)S(1)}, bf16[128,512]{1,0:T(8,128)(2,1)S(1)}, u32[]{:S(2)}, u32[]{:S(2)}) collective-permute-start(bf16[128,512]{1,0:T(8,128)(2,1)S(1)} %get-tuple-element.15), channel_id=1, source_target_pairs={{0,64},{16,80},{32,96},{48,112},{64,128},{80,144},{96,160},{112,17... | collective-permute-start | bytes 393224 | tf_op jit(solution)/shard_map/ppermute | solution.py:38
  5.1 8.5 %collective-permute-start.6 = (bf16[128,512]{1,0:T(8,128)(2,1)S(1)}, bf16[128,512]{1,0:T(8,128)(2,1)S(1)}, u32[]{:S(2)}, u32[]{:S(2)}) collective-permute-start(bf16[128,512]{1,0:T(8,128)(2,1)S(1)} %get-tuple-element.28), channel_id=1, source_target_pairs={{0,160},{16,176},{32,128},{48,144},{64,224},{80,240},{96,192},{112... | collective-permute-start | bytes 393224 | tf_op jit(solution)/shard_map/ppermute | solution.py:38
  7.1 8.4 %collective-permute-start.4 = (bf16[128,512]{1,0:T(8,128)(2,1)S(1)}, bf16[128,512]{1,0:T(8,128)(2,1)S(1)}, u32[]{:S(2)}, u32[]{:S(2)}) collective-permute-start(bf16[128,512]{1,0:T(8,128)(2,1)S(1)} %collective-permute-done), channel_id=1, source_target_pairs={{0,192},{16,208},{32,224},{48,240},{64,0},{80,16},{96,32},{112,48}... | collective-permute-start | bytes 393224 | tf_op jit(solution)/shard_map/ppermute | solution.py:38
  8.1 5.4 %collective-permute-start.2 = (bf16[128,512]{1,0:T(8,128)(2,1)S(1)}, bf16[128,512]{1,0:T(8,128)(2,1)S(1)}, u32[]{:S(2)}, u32[]{:S(2)}) collective-permute-start(bf16[128,512]{1,0:T(8,128)(2,1)S(1)} %collective-permute-done), channel_id=1, source_target_pairs={{0,64},{16,80},{32,96},{48,112},{64,128},{80,144},{96,160},{112,17... | collective-permute-start | bytes 393224 | tf_op jit(solution)/shard_map/ppermute | solution.py:38
  10.3 7.5 %collective-permute-start.5 = (bf16[128,512]{1,0:T(8,128)(2,1)S(1)}, bf16[128,512]{1,0:T(8,128)(2,1)S(1)}, u32[]{:S(2)}, u32[]{:S(2)}) collective-permute-start(bf16[128,512]{1,0:T(8,128)(2,1)S(1)} %collective-permute-done.3), channel_id=1, source_target_pairs={{0,192},{16,208},{32,224},{48,240},{64,0},{80,16},{96,32},{112,48}... | collective-permute-start | bytes 393224 | tf_op jit(solution)/shard_map/ppermute | solution.py:38
  13.5 4.5 %collective-permute-start.7 = (bf16[512,512]{1,0:T(8,128)(2,1)S(1)}, bf16[512,512]{1,0:T(8,128)(2,1)S(1)}, u32[]{:S(2)}, u32[]{:S(2)}) collective-permute-start(bf16[512,512]{1,0:T(8,128)(2,1)S(1)} %pad_maximum_fusion), channel_id=1, source_target_pairs={{0,16},{16,0},{32,48},{48,32},{64,80},{80,64},{96,112},{112,96},{1... | collective-permute-start | bytes 1572872 | tf_op jit(solution)/shard_map/ppermute | solution.py:16
  17.9 2.0 %collective-permute-start.8 = (bf16[512,512]{1,0:T(8,128)(2,1)S(1)}, bf16[512,512]{1,0:T(8,128)(2,1)S(1)}, u32[]{:S(2)}, u32[]{:S(2)}) collective-permute-start(bf16[512,512]{1,0:T(8,128)(2,1)S(1)} %pad_maximum_fusion.1), channel_id=1, source_target_pairs={{0,16},{16,0},{32,48},{48,32},{64,80},{80,64},{96,112},{112,96},{1... | collective-permute-start | bytes 1572872 | tf_op jit(solution)/shard_map/ppermute | solution.py:16
  21.3 6.5 %collective-permute-start.15 = (bf16[2,32,2048]{2,1,0:T(8,128)(2,1)S(1)}, bf16[2,32,2048]{2,1,0:T(8,128)(2,1)S(1)}, u32[]{:S(2)}, u32[]{:S(2)}) collective-permute-start(bf16[2,32,2048]{2,1,0:T(8,128)(2,1)S(1)} %bitcast.84), channel_id=1, source_target_pairs={{0,1},{1,0},{2,3},{3,2},{16,19},{17,18},{18,17},{19,16},{32,33},{3... | collective-permute-start | bytes 786440 | tf_op jit(solution)/shard_map/ppermute | solution.py:30
  23.7 7.2 %collective-permute-start.9 = (bf16[2,32,2048]{2,1,0:T(8,128)(2,1)S(1)}, bf16[2,32,2048]{2,1,0:T(8,128)(2,1)S(1)}, u32[]{:S(2)}, u32[]{:S(2)}) collective-permute-start(bf16[2,32,2048]{2,1,0:T(8,128)(2,1)S(1)} %bitcast.83), channel_id=1, source_target_pairs={{0,1},{1,0},{2,3},{3,2},{16,19},{17,18},{18,17},{19,16},{32,33},{3... | collective-permute-start | bytes 786440 | tf_op jit(solution)/shard_map/ppermute | solution.py:30
  27.8 6.3 %collective-permute-start.16 = (bf16[32,2048]{1,0:T(8,128)(2,1)S(1)}, bf16[32,2048]{1,0:T(8,128)(2,1)S(1)}, u32[]{:S(2)}, u32[]{:S(2)}) collective-permute-start(bf16[32,2048]{1,0:T(8,128)(2,1)S(1)} %fusion.39), channel_id=1, source_target_pairs={{0,3},{1,2},{2,1},{3,0},{16,17},{17,16},{18,19},{19,18},{32,35},{3... | collective-permute-start | bytes 393224 | tf_op jit(solution)/shard_map/ppermute | solution.py:30
  31.0 6.5 %collective-permute-start.10 = (bf16[32,2048]{1,0:T(8,128)(2,1)S(1)}, bf16[32,2048]{1,0:T(8,128)(2,1)S(1)}, u32[]{:S(2)}, u32[]{:S(2)}) collective-permute-start(bf16[32,2048]{1,0:T(8,128)(2,1)S(1)} %fusion.38), channel_id=1, source_target_pairs={{0,3},{1,2},{2,1},{3,0},{16,17},{17,16},{18,19},{19,18},{32,35},{3... | collective-permute-start | bytes 393224 | tf_op jit(solution)/shard_map/ppermute | solution.py:30
  34.1 7.0 %collective-permute-start.17 = (bf16[32,2048]{1,0:T(8,128)(2,1)S(1)}, bf16[32,2048]{1,0:T(8,128)(2,1)S(1)}, u32[]{:S(2)}, u32[]{:S(2)}) collective-permute-start(bf16[32,2048]{1,0:T(8,128)(2,1)S(1)} %fusion.42), channel_id=1, source_target_pairs={{0,4},{4,0},{8,12},{12,8},{16,28},{20,24},{24,20},{28,16},{32,36},... | collective-permute-start | bytes 393224 | tf_op jit(solution)/shard_map/ppermute | solution.py:30
  37.5 9.9 %collective-permute-start.11 = (bf16[32,2048]{1,0:T(8,128)(2,1)S(1)}, bf16[32,2048]{1,0:T(8,128)(2,1)S(1)}, u32[]{:S(2)}, u32[]{:S(2)}) collective-permute-start(bf16[32,2048]{1,0:T(8,128)(2,1)S(1)} %fusion.41), channel_id=1, source_target_pairs={{0,4},{4,0},{8,12},{12,8},{16,28},{20,24},{24,20},{28,16},{32,36},... | collective-permute-start | bytes 393224 | tf_op jit(solution)/shard_map/ppermute | solution.py:30
  41.1 12.3 %collective-permute-start.18 = (bf16[32,2048]{1,0:T(8,128)(2,1)S(1)}, bf16[32,2048]{1,0:T(8,128)(2,1)S(1)}, u32[]{:S(2)}, u32[]{:S(2)}) collective-permute-start(bf16[32,2048]{1,0:T(8,128)(2,1)S(1)} %fusion.37), channel_id=1, source_target_pairs={{0,12},{4,8},{8,4},{12,0},{16,20},{20,16},{24,28},{28,24},{32,44},... | collective-permute-start | bytes 393224 | tf_op jit(solution)/shard_map/ppermute | solution.py:30
  47.5 10.6 %collective-permute-start.12 = (bf16[32,2048]{1,0:T(8,128)(2,1)S(1)}, bf16[32,2048]{1,0:T(8,128)(2,1)S(1)}, u32[]{:S(2)}, u32[]{:S(2)}) collective-permute-start(bf16[32,2048]{1,0:T(8,128)(2,1)S(1)} %fusion.36), channel_id=1, source_target_pairs={{0,12},{4,8},{8,4},{12,0},{16,20},{20,16},{24,28},{28,24},{32,44},... | collective-permute-start | bytes 393224 | tf_op jit(solution)/shard_map/ppermute | solution.py:30
  53.5 8.3 %collective-permute-start.19 = (bf16[32,2048]{1,0:T(8,128)(2,1)S(1)}, bf16[32,2048]{1,0:T(8,128)(2,1)S(1)}, u32[]{:S(2)}, u32[]{:S(2)}) collective-permute-start(bf16[32,2048]{1,0:T(8,128)(2,1)S(1)} %add_convert_fusion), channel_id=1, source_target_pairs={{0,3},{1,2},{2,1},{3,0},{16,19},{17,18},{18,17},{19,16},{32,35},{3... | collective-permute-start | bytes 393224 | tf_op jit(solution)/shard_map/ppermute | solution.py:30
  58.2 6.6 %collective-permute-start.13 = (bf16[32,2048]{1,0:T(8,128)(2,1)S(1)}, bf16[32,2048]{1,0:T(8,128)(2,1)S(1)}, u32[]{:S(2)}, u32[]{:S(2)}) collective-permute-start(bf16[32,2048]{1,0:T(8,128)(2,1)S(1)} %add_convert_fusion.1), channel_id=1, source_target_pairs={{0,3},{1,2},{2,1},{3,0},{16,19},{17,18},{18,17},{19,16},{32,35},{3... | collective-permute-start | bytes 393224 | tf_op jit(solution)/shard_map/ppermute | solution.py:30
  61.8 6.5 %collective-permute-start.20 = (bf16[64,2048]{1,0:T(8,128)(2,1)S(1)}, bf16[64,2048]{1,0:T(8,128)(2,1)S(1)}, u32[]{:S(2)}, u32[]{:S(2)}) collective-permute-start(bf16[64,2048]{1,0:T(8,128)(2,1)S(1)} %pad_maximum_fusion.5), channel_id=1, source_target_pairs={{0,1},{1,0},{2,3},{3,2},{16,17},{17,16},{18,19},{19,18},{32,33},{3... | collective-permute-start | bytes 786440 | tf_op jit(solution)/shard_map/ppermute | solution.py:30
  62.5 9.4 %collective-permute-start.21 = (bf16[64,512]{1,0:T(8,128)(2,1)S(1)}, bf16[64,512]{1,0:T(8,128)(2,1)S(1)}, u32[]{:S(2)}, u32[]{:S(2)}) collective-permute-start(bf16[64,512]{1,0:T(8,128)(2,1)S(1)} %fusion.22), channel_id=1, source_target_pairs={{0,32},{16,48},{32,0},{48,16},{64,96},{80,112},{96,64},{112,80},{1... | collective-permute-start | bytes 196616 | tf_op jit(solution)/shard_map/ppermute | solution.py:16
  64.8 6.5 %collective-permute-start.14 = (bf16[64,2048]{1,0:T(8,128)(2,1)S(1)}, bf16[64,2048]{1,0:T(8,128)(2,1)S(1)}, u32[]{:S(2)}, u32[]{:S(2)}) collective-permute-start(bf16[64,2048]{1,0:T(8,128)(2,1)S(1)} %pad_maximum_fusion.4), channel_id=1, source_target_pairs={{0,1},{1,0},{2,3},{3,2},{16,17},{17,16},{18,19},{19,18},{32,33},{3... | collective-permute-start | bytes 786440 | tf_op jit(solution)/shard_map/ppermute | solution.py:30
  68.8 4.4 %collective-permute-start.22 = (bf16[64,512]{1,0:T(8,128)(2,1)S(1)}, bf16[64,512]{1,0:T(8,128)(2,1)S(1)}, u32[]{:S(2)}, u32[]{:S(2)}) collective-permute-start(bf16[64,512]{1,0:T(8,128)(2,1)S(1)} %fusion.25), channel_id=1, source_target_pairs={{0,32},{16,48},{32,0},{48,16},{64,96},{80,112},{96,64},{112,80},{1... | collective-permute-start | bytes 196616 | tf_op jit(solution)/shard_map/ppermute | solution.py:16

commit v6 on v4

--- a/solution.py
+++ b/solution.py
@@ -115,7 +115,6 @@
     hinge = hinge_of(variance)
     wide = cent.astype(BF).astype(F32)
     feature_squares = jnp.sum(wide * wide, axis=0, keepdims=True)
-    send_mine, feature_squares = lax.optimization_barrier((send_mine, feature_squares))
     term_away, term_mine = term_of(away_late), term_of(mine_late)
     term_away = ordered(term_away.reshape(4, quarter, width), "col", True)
     term_away = term_away.reshape(2, 2 * quarter, width)

time: 74.3 us -> 74.3 us (level)
  no operation moved by 1% of the time
where the time goes in v6:
time: 74.3 us; the launch traced here: 74.2 us
  starting transfers between devices  43.6 us (59%)
  waiting for transfers between devices  23 us (31%)
  other arithmetic  3.8 us (5%)
  matrix products  2.37 us (3%)
  between operations  1.07 us (1%)
    ppermute x12, starting transfers between devices, exchange(): return lax.ppermute(x, ('batch', axis), pairs)  35 us
    ppermute x12, waiting for transfers between devices, exchange(): return lax.ppermute(x, ('batch', axis), pairs)  12 us
    ppermute x6, starting transfers between devices, move(): return lax.ppermute(x, 'batch', pairs)  8.29 us
    ppermute x6, waiting for transfers between devices, move(): return lax.ppermute(x, 'batch', pairs)  7.93 us
    ppermute x4, waiting for transfers between devices, swap(): lax.ppermute(x, 'batch', [(i, i ^ bit) for i in range(lax.axis_size('batc...  3.09 us
  transfers between devices with their start and end apart: 22, of which 13 were waited for; matrix products, arithmetic and copies ran while one was open for 4% of the time, Pallas kernels for 0%

profile of v6, /device:TPU:38, one launch (start us, length us, event | category | flops | bytes accessed | tf_op | source)
XLA Modules:
  0.0 74.2 jit_solution(4492403795054524868)
XLA Ops:
  0.7 1.0 %constant_dynamic-update-slice_fusion.8 = (bf16[2048,512]{1,0:T(8,128)(2,1)S(1)}, bf16[128,512]{1,0:T(8,128)(2,1)S(1)}, bf16[128,512]{1,0:T(8,128)(2,1)S(1)}) fusion(bf16[128,512]{1,0:T(8,128)(2,1)} %param.2, bf16[128,512]{1,0:T(8,128)(2,1)} %param.3, pred[]{:T(512)S(6)} %eq.29), kind=kLoop, calls=%fused_computation.84 | loop fusion | flops 131071 | bytes 655361
  1.7 0.2 collective-permute-start
  1.9 0.8 %collective-permute-start.3 = (bf16[128,512]{1,0:T(8,128)(2,1)S(1)}, bf16[128,512]{1,0:T(8,128)(2,1)S(1)}, u32[]{:S(2)}, u32[]{:S(2)}) collective-permute-start(bf16[128,512]{1,0:T(8,128)(2,1)S(1)} %get-tuple-element.11), channel_id=1, source_target_pairs={{0,192},{16,208},{32,224},{48,240},{64,0},{80,16},{96,32},{112,48}... | collective-permute-start | bytes 393224 | tf_op jit(solution)/shard_map/ppermute | solution.py:38
  2.7 2.4 %collective-permute-start.1 = (bf16[128,512]{1,0:T(8,128)(2,1)S(1)}, bf16[128,512]{1,0:T(8,128)(2,1)S(1)}, u32[]{:S(2)}, u32[]{:S(2)}) collective-permute-start(bf16[128,512]{1,0:T(8,128)(2,1)S(1)} %get-tuple-element.11), channel_id=1, source_target_pairs={{0,64},{16,80},{32,96},{48,112},{64,128},{80,144},{96,160},{112,17... | collective-permute-start | bytes 393224 | tf_op jit(solution)/shard_map/ppermute | solution.py:38
  5.1 1.5 %collective-permute-start.5 = (bf16[128,512]{1,0:T(8,128)(2,1)S(1)}, bf16[128,512]{1,0:T(8,128)(2,1)S(1)}, u32[]{:S(2)}, u32[]{:S(2)}) collective-permute-start(bf16[128,512]{1,0:T(8,128)(2,1)S(1)} %get-tuple-element.24), channel_id=1, source_target_pairs={{0,160},{16,176},{32,128},{48,144},{64,224},{80,240},{96,192},{112... | collective-permute-start | bytes 393224 | tf_op jit(solution)/shard_map/ppermute | solution.py:38
  6.7 0.4 collective-permute-done
  7.1 1.2 %collective-permute-done.3 = bf16[128,512]{1,0:T(8,128)(2,1)S(1)} collective-permute-done((bf16[128,512]{1,0:T(8,128)(2,1)S(1)}, bf16[128,512]{1,0:T(8,128)(2,1)S(1)}, u32[]{:S(2)}, u32[]{:S(2)}) %collective-permute-start.3) | collective-permute-done | bytes 131104 | tf_op jit(solution)/shard_map/ppermute | solution.py:38
  8.3 0.1 collective-permute-start.4
  8.4 3.2 %collective-permute-start.2 = (bf16[128,512]{1,0:T(8,128)(2,1)S(1)}, bf16[128,512]{1,0:T(8,128)(2,1)S(1)}, u32[]{:S(2)}, u32[]{:S(2)}) collective-permute-start(bf16[128,512]{1,0:T(8,128)(2,1)S(1)} %collective-permute-done), channel_id=1, source_target_pairs={{0,64},{16,80},{32,96},{48,112},{64,128},{80,144},{96,160},{112,17... | collective-permute-start | bytes 393224 | tf_op jit(solution)/shard_map/ppermute | solution.py:38
  11.6 0.0 collective-permute-done.1
  11.7 2.5 %collective-permute-done.2 = bf16[128,512]{1,0:T(8,128)(2,1)S(1)} collective-permute-done((bf16[128,512]{1,0:T(8,128)(2,1)S(1)}, bf16[128,512]{1,0:T(8,128)(2,1)S(1)}, u32[]{:S(2)}, u32[]{:S(2)}) %collective-permute-start.2) | collective-permute-done | bytes 131104 | tf_op jit(solution)/shard_map/ppermute | solution.py:38
  14.2 0.1 collective-permute-start.6
  14.3 3.8 %collective-permute-done.4 = bf16[256,512]{1,0:T(8,128)(2,1)S(1)} collective-permute-done((bf16[256,512]{1,0:T(8,128)(2,1)S(1)}, bf16[256,512]{1,0:T(8,128)(2,1)S(1)}, u32[]{:S(2)}, u32[]{:S(2)}) %collective-permute-start.4) | collective-permute-done | bytes 262176 | tf_op jit(solution)/shard_map/ppermute | solution.py:38
  18.2 0.1 collective-permute-start.7
  18.4 1.8 %collective-permute-done.7 = bf16[512,512]{1,0:T(8,128)(2,1)S(1)} collective-permute-done((bf16[512,512]{1,0:T(8,128)(2,1)S(1)}, bf16[512,512]{1,0:T(8,128)(2,1)S(1)}, u32[]{:S(2)}, u32[]{:S(2)}) %collective-permute-start.7) | collective-permute-done | bytes 524320 | tf_op jit(solution)/shard_map/ppermute | solution.py:16
  20.2 0.3 convert_reduce_fusion
  20.8 0.8 %fusion.47 = (bf16[256,2048]{1,0:T(8,128)(2,1)S(1)}, f32[256,2048]{1,0:T(8,128)S(1)}) fusion(bf16[256,512]{1,0:T(8,128)(2,1)S(1)} %bitcast.72, bf16[2048,512]{1,0:T(8,128)(2,1)S(1)} %constant_dynamic-update-slice_fusion, f32[512]{0:T(512)S(1)} %broadcast_multiply_fusion), kind=kOutput, calls=%fused_computation.92 | convolution fusion | flops 540540928 | bytes 5507072 | tf_op jit(solution)/shard_map/dot_general | solution.py:94
  21.6 1.7 %collective-permute-start.14 = (bf16[2,32,2048]{2,1,0:T(8,128)(2,1)S(1)}, bf16[2,32,2048]{2,1,0:T(8,128)(2,1)S(1)}, u32[]{:S(2)}, u32[]{:S(2)}) collective-permute-start(bf16[2,32,2048]{2,1,0:T(8,128)(2,1)S(1)} %bitcast.82), channel_id=1, source_target_pairs={{0,1},{1,0},{2,3},{3,2},{16,19},{17,18},{18,17},{19,16},{32,33},{3... | collective-permute-start | bytes 786440 | tf_op jit(solution)/shard_map/ppermute | solution.py:30
  23.3 0.6 multiply_reduce_fusion.1
  23.9 0.1 multiply_add_fusion
  24.0 0.5 collective-permute-start.8
  24.5 0.1 fusion.44
  24.7 3.4 %collective-permute-done.14 = bf16[2,32,2048]{2,1,0:T(8,128)(2,1)S(1)} collective-permute-done((bf16[2,32,2048]{2,1,0:T(8,128)(2,1)S(1)}, bf16[2,32,2048]{2,1,0:T(8,128)(2,1)S(1)}, u32[]{:S(2)}, u32[]{:S(2)}) %collective-permute-start.14) | collective-permute-done | bytes 262176 | tf_op jit(solution)/shard_map/ppermute | solution.py:30
  28.1 3.1 %collective-permute-start.15 = (bf16[32,2048]{1,0:T(8,128)(2,1)S(1)}, bf16[32,2048]{1,0:T(8,128)(2,1)S(1)}, u32[]{:S(2)}, u32[]{:S(2)}) collective-permute-start(bf16[32,2048]{1,0:T(8,128)(2,1)S(1)} %fusion.39), channel_id=1, source_target_pairs={{0,3},{1,2},{2,1},{3,0},{16,17},{17,16},{18,19},{19,18},{32,35},{3... | collective-permute-start | bytes 393224 | tf_op jit(solution)/shard_map/ppermute | solution.py:30
  31.3 2.7 %collective-permute-start.9 = (bf16[32,2048]{1,0:T(8,128)(2,1)S(1)}, bf16[32,2048]{1,0:T(8,128)(2,1)S(1)}, u32[]{:S(2)}, u32[]{:S(2)}) collective-permute-start(bf16[32,2048]{1,0:T(8,128)(2,1)S(1)} %fusion.38), channel_id=1, source_target_pairs={{0,3},{1,2},{2,1},{3,0},{16,17},{17,16},{18,19},{19,18},{32,35},{3... | collective-permute-start | bytes 393224 | tf_op jit(solution)/shard_map/ppermute | solution.py:30
  34.0 0.4 collective-permute-done.15
  34.4 3.3 %collective-permute-start.16 = (bf16[32,2048]{1,0:T(8,128)(2,1)S(1)}, bf16[32,2048]{1,0:T(8,128)(2,1)S(1)}, u32[]{:S(2)}, u32[]{:S(2)}) collective-permute-start(bf16[32,2048]{1,0:T(8,128)(2,1)S(1)} %fusion.42), channel_id=1, source_target_pairs={{0,4},{4,0},{8,12},{12,8},{16,28},{20,24},{24,20},{28,16},{32,36},... | collective-permute-start | bytes 393224 | tf_op jit(solution)/shard_map/ppermute | solution.py:30
  37.8 3.1 %collective-permute-start.10 = (bf16[32,2048]{1,0:T(8,128)(2,1)S(1)}, bf16[32,2048]{1,0:T(8,128)(2,1)S(1)}, u32[]{:S(2)}, u32[]{:S(2)}) collective-permute-start(bf16[32,2048]{1,0:T(8,128)(2,1)S(1)} %fusion.41), channel_id=1, source_target_pairs={{0,4},{4,0},{8,12},{12,8},{16,28},{20,24},{24,20},{28,16},{32,36},... | collective-permute-start | bytes 393224 | tf_op jit(solution)/shard_map/ppermute | solution.py:30
  41.0 0.1 collective-permute-done.16
  41.1 5.6 %collective-permute-start.17 = (bf16[32,2048]{1,0:T(8,128)(2,1)S(1)}, bf16[32,2048]{1,0:T(8,128)(2,1)S(1)}, u32[]{:S(2)}, u32[]{:S(2)}) collective-permute-start(bf16[32,2048]{1,0:T(8,128)(2,1)S(1)} %fusion.37), channel_id=1, source_target_pairs={{0,12},{4,8},{8,4},{12,0},{16,20},{20,16},{24,28},{28,24},{32,44},... | collective-permute-start | bytes 393224 | tf_op jit(solution)/shard_map/ppermute | solution.py:30
  46.7 0.2 collective-permute-done.10
  46.9 7.4 %collective-permute-start.11 = (bf16[32,2048]{1,0:T(8,128)(2,1)S(1)}, bf16[32,2048]{1,0:T(8,128)(2,1)S(1)}, u32[]{:S(2)}, u32[]{:S(2)}) collective-permute-start(bf16[32,2048]{1,0:T(8,128)(2,1)S(1)} %fusion.36), channel_id=1, source_target_pairs={{0,12},{4,8},{8,4},{12,0},{16,20},{20,16},{24,28},{28,24},{32,44},... | collective-permute-start | bytes 393224 | tf_op jit(solution)/shard_map/ppermute | solution.py:30
  54.3 0.1 add_convert_fusion
  54.4 3.9 %collective-permute-start.18 = (bf16[32,2048]{1,0:T(8,128)(2,1)S(1)}, bf16[32,2048]{1,0:T(8,128)(2,1)S(1)}, u32[]{:S(2)}, u32[]{:S(2)}) collective-permute-start(bf16[32,2048]{1,0:T(8,128)(2,1)S(1)} %add_convert_fusion), channel_id=1, source_target_pairs={{0,3},{1,2},{2,1},{3,0},{16,19},{17,18},{18,17},{19,16},{32,35},{3... | collective-permute-start | bytes 393224 | tf_op jit(solution)/shard_map/ppermute | solution.py:30
  58.3 0.1 add_convert_fusion.1
  58.4 3.4 %collective-permute-start.12 = (bf16[32,2048]{1,0:T(8,128)(2,1)S(1)}, bf16[32,2048]{1,0:T(8,128)(2,1)S(1)}, u32[]{:S(2)}, u32[]{:S(2)}) collective-permute-start(bf16[32,2048]{1,0:T(8,128)(2,1)S(1)} %add_convert_fusion.1), channel_id=1, source_target_pairs={{0,3},{1,2},{2,1},{3,0},{16,19},{17,18},{18,17},{19,16},{32,35},{3... | collective-permute-start | bytes 393224 | tf_op jit(solution)/shard_map/ppermute | solution.py:30
  61.8 0.1 collective-permute-start.19
  61.9 0.5 fusion.22
  62.5 0.1 collective-permute-start.20
  62.6 2.2 %collective-permute-done.12 = bf16[32,2048]{1,0:T(8,128)(2,1)S(1)} collective-permute-done((bf16[32,2048]{1,0:T(8,128)(2,1)S(1)}, bf16[32,2048]{1,0:T(8,128)(2,1)S(1)}, u32[]{:S(2)}, u32[]{:S(2)}) %collective-permute-start.12) | collective-permute-done | bytes 131104 | tf_op jit(solution)/shard_map/ppermute | solution.py:30
  64.8 0.1 collective-permute-start.13
  64.9 3.4 %collective-permute-done.19 = bf16[64,2048]{1,0:T(8,128)(2,1)S(1)} collective-permute-done((bf16[64,2048]{1,0:T(8,128)(2,1)S(1)}, bf16[64,2048]{1,0:T(8,128)(2,1)S(1)}, u32[]{:S(2)}, u32[]{:S(2)}) %collective-permute-start.19) | collective-permute-done | bytes 262176 | tf_op jit(solution)/shard_map/ppermute | solution.py:30
  68.3 0.5 fusion.25
  68.8 0.1 collective-permute-start.21
  68.9 2.3 %collective-permute-done.13 = bf16[64,2048]{1,0:T(8,128)(2,1)S(1)} collective-permute-done((bf16[64,2048]{1,0:T(8,128)(2,1)S(1)}, bf16[64,2048]{1,0:T(8,128)(2,1)S(1)}, u32[]{:S(2)}, u32[]{:S(2)}) %collective-permute-start.13) | collective-permute-done | bytes 262176 | tf_op jit(solution)/shard_map/ppermute | solution.py:30
  71.3 0.5 fusion.4
  71.8 1.3 %collective-permute-done.21 = bf16[64,512]{1,0:T(8,128)(2,1)S(1)} collective-permute-done((bf16[64,512]{1,0:T(8,128)(2,1)S(1)}, bf16[64,512]{1,0:T(8,128)(2,1)S(1)}, u32[]{:S(2)}, u32[]{:S(2)}) %collective-permute-start.21) | collective-permute-done | bytes 65568 | tf_op jit(solution)/shard_map/ppermute | solution.py:16
  73.3 0.8 %select_convert_fusion = (bf16[128,512]{1,0:T(8,128)(2,1)}, bf16[128,512]{1,0:T(8,128)(2,1)}) fusion(pred[]{:T(512)S(6)} %eq.29, bf16[128,512]{1,0:T(8,128)(2,1)S(1)} %get-tuple-element.24, bf16[128,512]{1,0:T(8,128)(2,1)S(1)} %get-tuple-element.11, f32[2,2,32,512]{3,2,1,0:T(8,128)S(1)} %reverse_select_fusion, f32[512]{0:T(512)S(1)} %fusion.43, ...), kind=kLoop, calls=%fused_computation.48 | loop fusion | flops 1179648 | bytes 1054721 | tf_op jit(solution)/shard_map/convert_element_type | solution.py:138
  (49 shorter events, 1.1 us)
Async XLA Ops:
  1.7 5.4 %collective-permute-start = (bf16[128,512]{1,0:T(8,128)(2,1)S(1)}, bf16[128,512]{1,0:T(8,128)(2,1)S(1)}, u32[]{:S(2)}, u32[]{:S(2)}) collective-permute-start(bf16[128,512]{1,0:T(8,128)(2,1)S(1)} %get-tuple-element.24), channel_id=1, source_target_pairs={{0,32},{16,48},{32,0},{48,16},{64,96},{80,112},{96,64},{112,80},{1... | collective-permute-start | bytes 393224 | tf_op jit(solution)/shard_map/ppermute | solution.py:38
  1.9 6.4 %collective-permute-start.3 = (bf16[128,512]{1,0:T(8,128)(2,1)S(1)}, bf16[128,512]{1,0:T(8,128)(2,1)S(1)}, u32[]{:S(2)}, u32[]{:S(2)}) collective-permute-start(bf16[128,512]{1,0:T(8,128)(2,1)S(1)} %get-tuple-element.11), channel_id=1, source_target_pairs={{0,192},{16,208},{32,224},{48,240},{64,0},{80,16},{96,32},{112,48}... | collective-permute-start | bytes 393224 | tf_op jit(solution)/shard_map/ppermute | solution.py:38
  2.7 8.9 %collective-permute-start.1 = (bf16[128,512]{1,0:T(8,128)(2,1)S(1)}, bf16[128,512]{1,0:T(8,128)(2,1)S(1)}, u32[]{:S(2)}, u32[]{:S(2)}) collective-permute-start(bf16[128,512]{1,0:T(8,128)(2,1)S(1)} %get-tuple-element.11), channel_id=1, source_target_pairs={{0,64},{16,80},{32,96},{48,112},{64,128},{80,144},{96,160},{112,17... | collective-permute-start | bytes 393224 | tf_op jit(solution)/shard_map/ppermute | solution.py:38
  5.1 9.2 %collective-permute-start.5 = (bf16[128,512]{1,0:T(8,128)(2,1)S(1)}, bf16[128,512]{1,0:T(8,128)(2,1)S(1)}, u32[]{:S(2)}, u32[]{:S(2)}) collective-permute-start(bf16[128,512]{1,0:T(8,128)(2,1)S(1)} %get-tuple-element.24), channel_id=1, source_target_pairs={{0,160},{16,176},{32,128},{48,144},{64,224},{80,240},{96,192},{112... | collective-permute-start | bytes 393224 | tf_op jit(solution)/shard_map/ppermute | solution.py:38
  8.3 9.8 %collective-permute-start.4 = (bf16[256,512]{1,0:T(8,128)(2,1)S(1)}, bf16[256,512]{1,0:T(8,128)(2,1)S(1)}, u32[]{:S(2)}, u32[]{:S(2)}) collective-permute-start(bf16[256,512]{1,0:T(8,128)(2,1)S(1)} %pad_maximum_fusion.3), channel_id=1, source_target_pairs={{0,192},{16,208},{32,224},{48,240},{64,0},{80,16},{96,32},{112,48}... | collective-permute-start | bytes 786440 | tf_op jit(solution)/shard_map/ppermute | solution.py:38
  8.4 5.7 %collective-permute-start.2 = (bf16[128,512]{1,0:T(8,128)(2,1)S(1)}, bf16[128,512]{1,0:T(8,128)(2,1)S(1)}, u32[]{:S(2)}, u32[]{:S(2)}) collective-permute-start(bf16[128,512]{1,0:T(8,128)(2,1)S(1)} %collective-permute-done), channel_id=1, source_target_pairs={{0,64},{16,80},{32,96},{48,112},{64,128},{80,144},{96,160},{112,17... | collective-permute-start | bytes 393224 | tf_op jit(solution)/shard_map/ppermute | solution.py:38
  14.2 4.1 %collective-permute-start.6 = (bf16[512,512]{1,0:T(8,128)(2,1)S(1)}, bf16[512,512]{1,0:T(8,128)(2,1)S(1)}, u32[]{:S(2)}, u32[]{:S(2)}) collective-permute-start(bf16[512,512]{1,0:T(8,128)(2,1)S(1)} %pad_maximum_fusion), channel_id=1, source_target_pairs={{0,16},{16,0},{32,48},{48,32},{64,80},{80,64},{96,112},{112,96},{1... | collective-permute-start | bytes 1572872 | tf_op jit(solution)/shard_map/ppermute | solution.py:16
  18.2 2.0 %collective-permute-start.7 = (bf16[512,512]{1,0:T(8,128)(2,1)S(1)}, bf16[512,512]{1,0:T(8,128)(2,1)S(1)}, u32[]{:S(2)}, u32[]{:S(2)}) collective-permute-start(bf16[512,512]{1,0:T(8,128)(2,1)S(1)} %pad_maximum_fusion.1), channel_id=1, source_target_pairs={{0,16},{16,0},{32,48},{48,32},{64,80},{80,64},{96,112},{112,96},{1... | collective-permute-start | bytes 1572872 | tf_op jit(solution)/shard_map/ppermute | solution.py:16
  21.6 6.5 %collective-permute-start.14 = (bf16[2,32,2048]{2,1,0:T(8,128)(2,1)S(1)}, bf16[2,32,2048]{2,1,0:T(8,128)(2,1)S(1)}, u32[]{:S(2)}, u32[]{:S(2)}) collective-permute-start(bf16[2,32,2048]{2,1,0:T(8,128)(2,1)S(1)} %bitcast.82), channel_id=1, source_target_pairs={{0,1},{1,0},{2,3},{3,2},{16,19},{17,18},{18,17},{19,16},{32,33},{3... | collective-permute-start | bytes 786440 | tf_op jit(solution)/shard_map/ppermute | solution.py:30
  24.0 7.2 %collective-permute-start.8 = (bf16[2,32,2048]{2,1,0:T(8,128)(2,1)S(1)}, bf16[2,32,2048]{2,1,0:T(8,128)(2,1)S(1)}, u32[]{:S(2)}, u32[]{:S(2)}) collective-permute-start(bf16[2,32,2048]{2,1,0:T(8,128)(2,1)S(1)} %bitcast.81), channel_id=1, source_target_pairs={{0,1},{1,0},{2,3},{3,2},{16,19},{17,18},{18,17},{19,16},{32,33},{3... | collective-permute-start | bytes 786440 | tf_op jit(solution)/shard_map/ppermute | solution.py:30
  28.1 6.3 %collective-permute-start.15 = (bf16[32,2048]{1,0:T(8,128)(2,1)S(1)}, bf16[32,2048]{1,0:T(8,128)(2,1)S(1)}, u32[]{:S(2)}, u32[]{:S(2)}) collective-permute-start(bf16[32,2048]{1,0:T(8,128)(2,1)S(1)} %fusion.39), channel_id=1, source_target_pairs={{0,3},{1,2},{2,1},{3,0},{16,17},{17,16},{18,19},{19,18},{32,35},{3... | collective-permute-start | bytes 393224 | tf_op jit(solution)/shard_map/ppermute | solution.py:30
  31.3 6.5 %collective-permute-start.9 = (bf16[32,2048]{1,0:T(8,128)(2,1)S(1)}, bf16[32,2048]{1,0:T(8,128)(2,1)S(1)}, u32[]{:S(2)}, u32[]{:S(2)}) collective-permute-start(bf16[32,2048]{1,0:T(8,128)(2,1)S(1)} %fusion.38), channel_id=1, source_target_pairs={{0,3},{1,2},{2,1},{3,0},{16,17},{17,16},{18,19},{19,18},{32,35},{3... | collective-permute-start | bytes 393224 | tf_op jit(solution)/shard_map/ppermute | solution.py:30
  34.4 6.6 %collective-permute-start.16 = (bf16[32,2048]{1,0:T(8,128)(2,1)S(1)}, bf16[32,2048]{1,0:T(8,128)(2,1)S(1)}, u32[]{:S(2)}, u32[]{:S(2)}) collective-permute-start(bf16[32,2048]{1,0:T(8,128)(2,1)S(1)} %fusion.42), channel_id=1, source_target_pairs={{0,4},{4,0},{8,12},{12,8},{16,28},{20,24},{24,20},{28,16},{32,36},... | collective-permute-start | bytes 393224 | tf_op jit(solution)/shard_map/ppermute | solution.py:30
  37.8 9.1 %collective-permute-start.10 = (bf16[32,2048]{1,0:T(8,128)(2,1)S(1)}, bf16[32,2048]{1,0:T(8,128)(2,1)S(1)}, u32[]{:S(2)}, u32[]{:S(2)}) collective-permute-start(bf16[32,2048]{1,0:T(8,128)(2,1)S(1)} %fusion.41), channel_id=1, source_target_pairs={{0,4},{4,0},{8,12},{12,8},{16,28},{20,24},{24,20},{28,16},{32,36},... | collective-permute-start | bytes 393224 | tf_op jit(solution)/shard_map/ppermute | solution.py:30
  41.1 13.3 %collective-permute-start.17 = (bf16[32,2048]{1,0:T(8,128)(2,1)S(1)}, bf16[32,2048]{1,0:T(8,128)(2,1)S(1)}, u32[]{:S(2)}, u32[]{:S(2)}) collective-permute-start(bf16[32,2048]{1,0:T(8,128)(2,1)S(1)} %fusion.37), channel_id=1, source_target_pairs={{0,12},{4,8},{8,4},{12,0},{16,20},{20,16},{24,28},{28,24},{32,44},... | collective-permute-start | bytes 393224 | tf_op jit(solution)/shard_map/ppermute | solution.py:30
  46.9 11.4 %collective-permute-start.11 = (bf16[32,2048]{1,0:T(8,128)(2,1)S(1)}, bf16[32,2048]{1,0:T(8,128)(2,1)S(1)}, u32[]{:S(2)}, u32[]{:S(2)}) collective-permute-start(bf16[32,2048]{1,0:T(8,128)(2,1)S(1)} %fusion.36), channel_id=1, source_target_pairs={{0,12},{4,8},{8,4},{12,0},{16,20},{20,16},{24,28},{28,24},{32,44},... | collective-permute-start | bytes 393224 | tf_op jit(solution)/shard_map/ppermute | solution.py:30
  54.4 7.4 %collective-permute-start.18 = (bf16[32,2048]{1,0:T(8,128)(2,1)S(1)}, bf16[32,2048]{1,0:T(8,128)(2,1)S(1)}, u32[]{:S(2)}, u32[]{:S(2)}) collective-permute-start(bf16[32,2048]{1,0:T(8,128)(2,1)S(1)} %add_convert_fusion), channel_id=1, source_target_pairs={{0,3},{1,2},{2,1},{3,0},{16,19},{17,18},{18,17},{19,16},{32,35},{3... | collective-permute-start | bytes 393224 | tf_op jit(solution)/shard_map/ppermute | solution.py:30
  58.4 6.3 %collective-permute-start.12 = (bf16[32,2048]{1,0:T(8,128)(2,1)S(1)}, bf16[32,2048]{1,0:T(8,128)(2,1)S(1)}, u32[]{:S(2)}, u32[]{:S(2)}) collective-permute-start(bf16[32,2048]{1,0:T(8,128)(2,1)S(1)} %add_convert_fusion.1), channel_id=1, source_target_pairs={{0,3},{1,2},{2,1},{3,0},{16,19},{17,18},{18,17},{19,16},{32,35},{3... | collective-permute-start | bytes 393224 | tf_op jit(solution)/shard_map/ppermute | solution.py:30
  61.8 6.5 %collective-permute-start.19 = (bf16[64,2048]{1,0:T(8,128)(2,1)S(1)}, bf16[64,2048]{1,0:T(8,128)(2,1)S(1)}, u32[]{:S(2)}, u32[]{:S(2)}) collective-permute-start(bf16[64,2048]{1,0:T(8,128)(2,1)S(1)} %pad_maximum_fusion.6), channel_id=1, source_target_pairs={{0,1},{1,0},{2,3},{3,2},{16,17},{17,16},{18,19},{19,18},{32,33},{3... | collective-permute-start | bytes 786440 | tf_op jit(solution)/shard_map/ppermute | solution.py:30
  62.5 9.4 %collective-permute-start.20 = (bf16[64,512]{1,0:T(8,128)(2,1)S(1)}, bf16[64,512]{1,0:T(8,128)(2,1)S(1)}, u32[]{:S(2)}, u32[]{:S(2)}) collective-permute-start(bf16[64,512]{1,0:T(8,128)(2,1)S(1)} %fusion.22), channel_id=1, source_target_pairs={{0,32},{16,48},{32,0},{48,16},{64,96},{80,112},{96,64},{112,80},{1... | collective-permute-start | bytes 196616 | tf_op jit(solution)/shard_map/ppermute | solution.py:16
  64.8 6.5 %collective-permute-start.13 = (bf16[64,2048]{1,0:T(8,128)(2,1)S(1)}, bf16[64,2048]{1,0:T(8,128)(2,1)S(1)}, u32[]{:S(2)}, u32[]{:S(2)}) collective-permute-start(bf16[64,2048]{1,0:T(8,128)(2,1)S(1)} %pad_maximum_fusion.5), channel_id=1, source_target_pairs={{0,1},{1,0},{2,3},{3,2},{16,17},{17,16},{18,19},{19,18},{32,33},{3... | collective-permute-start | bytes 786440 | tf_op jit(solution)/shard_map/ppermute | solution.py:30
  68.8 4.4 %collective-permute-start.21 = (bf16[64,512]{1,0:T(8,128)(2,1)S(1)}, bf16[64,512]{1,0:T(8,128)(2,1)S(1)}, u32[]{:S(2)}, u32[]{:S(2)}) collective-permute-start(bf16[64,512]{1,0:T(8,128)(2,1)S(1)} %fusion.25), channel_id=1, source_target_pairs={{0,32},{16,48},{32,0},{48,16},{64,96},{80,112},{96,64},{112,80},{1... | collective-permute-start | bytes 196616 | tf_op jit(solution)/shard_map/ppermute | solution.py:16
